TPU v7x, 32 devices: a whole 2x2x4 slice. The times are simulated.
32 devices in a mesh: doc: 4 (over z), seq: 8 (over y, x, core).
Axes of the slice: x: 2, y: 2, z: 4, core: 2. Of those that a mesh axis runs over, the one named last changes fastest.
Arguments:
- dec_input: bfloat16 [4, 4, 1024, 768], P('doc', None, 'seq'), may hold values from -6 to 6
- memory: bfloat16 [4, 8192, 768], P('doc', 'seq'), may hold values from -6 to 6
- doc_lengths: int32 [4, 4], P('doc'), may hold values from 1 to 8192, as said below
- doc_count: int32 [4], P('doc'), may hold values from 1 to 4
- self_qkv: float32 [768, 2304], P('doc'), may hold values from -0.3125 to 0.3125
- self_out: float32 [768, 768], P('doc'), may hold values from -0.625 to 0.625
- cross_q: float32 [768, 768], P('doc'), may hold values from -0.4375 to 0.4375
- cross_kv: float32 [768, 1536], P('doc'), may hold values from -0.21875 to 0.21875
- cross_out: float32 [768, 768], P('doc'), may hold values from -2 to 2
- ffn_in: float32 [768, 3072], P('doc'), may hold values from -0.21875 to 0.21875
- ffn_in_bias: float32 [3072], P('doc'), may hold values from -3 to 3
- ffn_out: float32 [3072, 768], P('doc'), may hold values from -0.109375 to 0.109375
- norm_gains: float32 [3, 768], P(None, 'doc'), may hold values from 0.25 to 1.75
- biases: float32 [10, 768], P(None, 'doc'), may hold values from -1.75 to 1.75
- out_grad: bfloat16 [4, 4, 1024, 768], P('doc', None, 'seq'), may hold values from -6 to 6
Outputs:
- layer_out: bfloat16 [4, 4, 1024, 768], P('doc', None, 'seq')
- input_grad: float32 [4, 4, 1024, 768], P('doc', None, 'seq')
- memory_grad: float32 [4, 8192, 768], P('doc', 'seq')
- grad_self_qkv: float32 [768, 2304], P('doc')
- grad_self_out: float32 [768, 768], P('doc')
- grad_cross_q: float32 [768, 768], P('doc')
- grad_cross_kv: float32 [768, 1536], P('doc')
- grad_cross_out: float32 [768, 768], P('doc')
- grad_ffn_in: float32 [768, 3072], P('doc')
- grad_ffn_in_bias: float32 [3072], P('doc')
- grad_ffn_out: float32 [3072, 768], P('doc')
- grad_norm_gains: float32 [3, 768], P(None, 'doc')
- grad_biases: float32 [10, 768], P(None, 'doc')
Inputs may be any that keep to these rules, and one draw needn't show every extreme that they name: `doc_lengths`: slots below doc_count hold the lengths of a group's documents, laid end to end from the start of its memory, together at most 8192 and more than 7680; memory after them is padding. Entries of later slots are no document's length. One group holds a single document of 8192 tokens; the others hold 4 documents of about 8192 // 4 tokens each.
All inputs are finite; a program needn't handle non-finite values.
Results may differ from a plain program's by a relative error of at most 0.03.
The roundings to bfloat16 on the way count: a program that leaves them out, or rounds other values in their place, can miss the bound.
Values may be sent and summed in bfloat16 or wider, within the bound.
No kernel may reach another device: no remote copies, remote signals or barrier semaphores. Data moves between devices by JAX's collectives and lax.ppermute only.
A program may use at most 512 MiB of HBM per device.

v0:
```python
from functools import partial

import jax
import jax.numpy as jnp
from jax import lax
from jax.sharding import PartitionSpec as P

D = 768
HEADS = 12
HEAD_DIM = 64
MEM_DEV = 1024


norm_eps = 1e-05
neg_fill = -1e30


def layer_norm(resid_in, gain_row, shift_row):
    center = resid_in - jnp.mean(resid_in, axis=-1, keepdims=True)
    variance = jnp.mean(center * center, axis=-1, keepdims=True)
    return center * lax.rsqrt(variance + norm_eps) * gain_row + shift_row


def matmul(left_op, right_op):
    return jnp.dot(left_op, right_op, preferred_element_type=jnp.float32)


def product_tn(left_op, right_op):
    return lax.dot_general(
        left_op, right_op, (((0,), (0,)), ((), ())), preferred_element_type=jnp.float32
    )


def matmul_nt(left_op, right_op):
    return lax.dot_general(
        left_op, right_op, (((1,), (1,)), ((), ())), preferred_element_type=jnp.float32
    )


def col_sums(grad_low):
    return jnp.sum(grad_low.astype(jnp.float32), axis=0)


def memory_owner(lengths, live_count, first_row, num_rows):
    slot_ids = jnp.arange(lengths.shape[0])
    live_len = jnp.where(slot_ids < live_count, lengths, 0)
    ends = jnp.cumsum(live_len)
    positions = first_row + jnp.arange(num_rows)
    return jnp.sum((positions[:, None] >= ends[None, :]).astype(jnp.int32), axis=1)


def block_valid(owner, live_count, slots_n):
    slot_ids = jnp.arange(slots_n)
    return (owner[None, :] == slot_ids[:, None]) & (slot_ids[:, None] < live_count)


def block_partial(query_blk, key_blk, value_blk, key_valid, score_scale):
    scores = (
        jnp.einsum("sqhd,thd->sqht", query_blk, key_blk, preferred_element_type=jnp.float32)
        * score_scale
    )
    mask_full = key_valid[:, None, None, :]
    scores = jnp.where(mask_full, scores, neg_fill)
    part_max = jnp.max(scores, axis=-1)
    part_weight = jnp.where(mask_full, jnp.exp(scores - part_max[..., None]), 0.0)
    part_sum = jnp.sum(part_weight, axis=-1)
    part_out = jnp.einsum(
        "sqht,thd->sqhd",
        part_weight.astype(jnp.bfloat16),
        value_blk,
        preferred_element_type=jnp.float32,
    )
    return (part_max, part_sum, part_out)


def merge_partial(run_state, part_state):
    run_max, run_sum, run_out = run_state
    part_max, part_sum, part_out = part_state
    new_max = jnp.maximum(run_max, part_max)
    old_scale = jnp.exp(run_max - new_max)
    new_scale = jnp.exp(part_max - new_max)
    return (
        new_max,
        run_sum * old_scale + part_sum * new_scale,
        run_out * old_scale[..., None] + part_out * new_scale[..., None],
    )


def body(
    dec_input,
    memory,
    doc_lengths,
    doc_count,
    self_qkv,
    self_out,
    cross_q,
    cross_kv,
    cross_out,
    ffn_in,
    ffn_in_bias,
    ffn_out,
    norm_gains,
    biases,
    out_grad,
):
    f32 = jnp.float32
    half = jnp.bfloat16
    seq_index = lax.axis_index("seq")
    slots_n = dec_input.shape[1]
    rows_dev = dec_input.shape[2]
    rows_total = slots_n * rows_dev
    mem_rows = memory.shape[1]
    score_scale = HEAD_DIM ** (-0.5)
    lengths = doc_lengths[0]
    live_count = doc_count[0]
    has_keys = (jnp.arange(slots_n) < live_count)[:, None, None]
    (
        w_qkv,
        w_self_out,
        w_cross_q,
        w_cross_kv,
        w_cross_out,
        w_ffn_in,
        b_ffn_in,
        w_ffn_out,
        gains_low,
        biases_low,
    ) = (
        lax.all_gather(self_qkv.astype(half), "doc", axis=0, tiled=True),
        lax.all_gather(self_out.astype(half), "doc", axis=0, tiled=True),
        lax.all_gather(cross_q.astype(half), "doc", axis=0, tiled=True),
        lax.all_gather(cross_kv.astype(half), "doc", axis=0, tiled=True),
        lax.all_gather(cross_out.astype(half), "doc", axis=0, tiled=True),
        lax.all_gather(ffn_in.astype(half), "doc", axis=0, tiled=True),
        lax.all_gather(ffn_in_bias.astype(half), "doc", axis=0, tiled=True),
        lax.all_gather(ffn_out.astype(half), "doc", axis=0, tiled=True),
        lax.all_gather(norm_gains.astype(half), "doc", axis=1, tiled=True),
        lax.all_gather(biases.astype(half), "doc", axis=1, tiled=True),
    )
    gains_f = gains_low.astype(f32)
    biases_f = biases_low.astype(f32)
    zero_row = jnp.zeros((D,), f32)
    x_low = dec_input[0].reshape(rows_total, D)
    self_proj = (
        matmul(x_low, w_qkv) + jnp.concatenate([biases_f[0], zero_row, biases_f[1]])
    ).astype(half)
    self_proj = self_proj.reshape(slots_n, rows_dev, 3 * D)
    q_self = self_proj[..., :D].reshape(slots_n, rows_dev, HEADS, HEAD_DIM)
    kv_all = lax.all_gather(self_proj[..., D:], "seq", axis=1, tiled=True)
    dec_len = kv_all.shape[1]
    k_all = kv_all[..., :D].reshape(slots_n, dec_len, HEADS, HEAD_DIM)
    v_all = kv_all[..., D:].reshape(slots_n, dec_len, HEADS, HEAD_DIM)
    positions = seq_index * rows_dev + jnp.arange(rows_dev)
    causal = (jnp.arange(dec_len)[None, :] <= positions[:, None])[None, :, None, :]
    scores = jnp.einsum("srhd,sthd->srht", q_self, k_all, preferred_element_type=f32) * score_scale
    scores = jnp.where(causal, scores, neg_fill)
    self_max = jnp.max(scores, axis=-1)
    prob_all = jnp.exp(scores - self_max[..., None])
    self_total = jnp.sum(prob_all, axis=-1)
    self_mix = (
        jnp.einsum("srht,sthd->srhd", prob_all.astype(half), v_all, preferred_element_type=f32)
        / self_total[..., None]
    )
    self_lse = self_max + jnp.log(self_total)
    self_att = self_mix.reshape(rows_total, D).astype(half)
    branch_self = matmul(self_att, w_self_out) + biases_f[2]
    norm_one, pull_one = jax.vjp(
        layer_norm, x_low.astype(f32) + branch_self, gains_f[0], biases_f[7]
    )
    norm_one_low = norm_one.astype(half)
    cross_query = (matmul(norm_one_low, w_cross_q) + biases_f[3]).astype(half)
    mem_low = memory[0]
    mem_kv = (matmul(mem_low, w_cross_kv) + jnp.concatenate([zero_row, biases_f[4]])).astype(half)
    k_own = mem_kv[:, :D].reshape(mem_rows, HEADS, HEAD_DIM)
    v_own = mem_kv[:, D:].reshape(mem_rows, HEADS, HEAD_DIM)
    query_groups = lax.all_gather(
        cross_query.reshape(slots_n, rows_dev, D), "seq", axis=1, tiled=True
    )
    own_valid = block_valid(
        memory_owner(lengths, live_count, seq_index * mem_rows, mem_rows), live_count, slots_n
    )
    block_rows = min(dec_len, 512)
    per_slot = dec_len // block_rows
    q_blocks = query_groups.reshape(slots_n * per_slot, block_rows, HEADS, HEAD_DIM)
    valid_blocks = jnp.repeat(own_valid, per_slot, axis=0)
    q_local = cross_query.reshape(slots_n, rows_dev, HEADS, HEAD_DIM)
    fold_init = (
        jnp.full((slots_n, rows_dev, HEADS), neg_fill, f32),
        jnp.zeros((slots_n, rows_dev, HEADS), f32),
        jnp.zeros((slots_n, rows_dev, HEADS, HEAD_DIM), f32),
    )
    run_carry = fold_init
    kv_piece = lax.all_gather(mem_kv, "seq", axis=0, tiled=True)
    kv_blocks = kv_piece.reshape(kv_piece.shape[0] // MEM_DEV, MEM_DEV, kv_piece.shape[1])

    def one_block(run_state, block_item):
        kv_block, block_num = block_item
        owner = memory_owner(lengths, live_count, block_num * MEM_DEV, MEM_DEV)
        key_valid = block_valid(owner, live_count, slots_n)
        part_state = block_partial(
            q_local,
            kv_block[:, :D].reshape(MEM_DEV, HEADS, HEAD_DIM),
            kv_block[:, D:].reshape(MEM_DEV, HEADS, HEAD_DIM),
            key_valid,
            score_scale,
        )
        return (merge_partial(run_state, part_state), None)

    run_carry, unused = lax.scan(one_block, run_carry, (kv_blocks, jnp.arange(kv_blocks.shape[0])))
    top_local, denom_sum, numer_sum = run_carry
    denom_safe = jnp.where(has_keys, denom_sum, 1.0)
    cross_mix = numer_sum / denom_safe[..., None]
    cross_lse = jnp.where(has_keys, top_local + jnp.log(denom_safe), 0.0)
    cross_att = cross_mix.reshape(rows_total, D).astype(half)
    branch_cross = matmul(cross_att, w_cross_out) + biases_f[5]
    norm_two, pull_two = jax.vjp(layer_norm, norm_one + branch_cross, gains_f[1], biases_f[8])
    norm_two_low = norm_two.astype(half)
    hidden = matmul(norm_two_low, w_ffn_in) + b_ffn_in.astype(f32)
    active, pull_gelu = jax.vjp(partial(jax.nn.gelu, approximate=False), hidden)
    active_low = active.astype(half)
    branch_ffn = matmul(active_low, w_ffn_out) + biases_f[6]
    result, pull_three = jax.vjp(layer_norm, norm_two + branch_ffn, gains_f[2], biases_f[9])
    layer_out = result.astype(half).reshape(dec_input.shape)
    grad_r3, grad_g2, grad_c9 = pull_three(out_grad[0].reshape(rows_total, D).astype(f32))
    grad_ffn_low = grad_r3.astype(half)
    grad_w_down = product_tn(active_low, grad_ffn_low)
    grad_b6 = col_sums(grad_ffn_low)
    grad_hidden = pull_gelu(matmul_nt(grad_ffn_low, w_ffn_out))[0].astype(half)
    grad_w_in = product_tn(norm_two_low, grad_hidden)
    grad_b_in = col_sums(grad_hidden)
    grad_r2, grad_g1, grad_c8 = pull_two(grad_r3 + matmul_nt(grad_hidden, w_ffn_in))
    grad_cross_low = grad_r2.astype(half)
    grad_w_cross_out = product_tn(cross_att, grad_cross_low)
    grad_b5 = col_sums(grad_cross_low)
    grad_mix = matmul_nt(grad_cross_low, w_cross_out).astype(half).reshape(slots_n, rows_dev, D)
    cross_delta = jnp.sum(
        grad_mix.astype(f32).reshape(slots_n, rows_dev, HEADS, HEAD_DIM) * cross_mix, axis=-1
    )
    grad_groups = lax.all_gather(grad_mix, "seq", axis=1, tiled=True)
    lse_groups, delta_groups = (
        lax.all_gather(cross_lse, "seq", axis=1, tiled=True),
        lax.all_gather(cross_delta, "seq", axis=1, tiled=True),
    )
    g_blocks = grad_groups.reshape(slots_n * per_slot, block_rows, HEADS, HEAD_DIM)
    lse_blocks = lse_groups.reshape(slots_n * per_slot, block_rows, HEADS)
    delta_blocks = delta_groups.reshape(slots_n * per_slot, block_rows, HEADS)

    def back_block(run_carry, block_item):
        grad_keys, grad_values = run_carry
        q_blk, g_blk, lse_blk, delta_blk, key_valid = block_item
        block_scores = (
            jnp.einsum("qhd,thd->qht", q_blk, k_own, preferred_element_type=f32) * score_scale
        )
        block_prob = jnp.where(
            key_valid[None, None, :], jnp.exp(block_scores - lse_blk[..., None]), 0.0
        )
        grad_values = grad_values + jnp.einsum(
            "qht,qhd->thd", block_prob.astype(half), g_blk, preferred_element_type=f32
        )
        grad_prob = jnp.einsum("qhd,thd->qht", g_blk, v_own, preferred_element_type=f32)
        grad_score = (block_prob * (grad_prob - delta_blk[..., None])).astype(half)
        grad_query_blk = (
            jnp.einsum("qht,thd->qhd", grad_score, k_own, preferred_element_type=f32) * score_scale
        )
        grad_keys = (
            grad_keys
            + jnp.einsum("qht,qhd->thd", grad_score, q_blk, preferred_element_type=f32)
            * score_scale
        )
        return ((grad_keys, grad_values), grad_query_blk)

    zero_keys = jnp.zeros((mem_rows, HEADS, HEAD_DIM), f32)
    (grad_k_own, grad_v_own), grad_query_blocks = lax.scan(
        back_block,
        (zero_keys, zero_keys),
        (q_blocks, g_blocks, lse_blocks, delta_blocks, valid_blocks),
    )
    grad_query = lax.psum_scatter(
        grad_query_blocks.reshape(slots_n, dec_len, D).astype(jnp.bfloat16),
        "seq",
        scatter_dimension=1,
        tiled=True,
    ).astype(jnp.float32)
    grad_query_low = grad_query.reshape(rows_total, D).astype(half)
    grad_w_cross_q = product_tn(norm_one_low, grad_query_low)
    grad_b3 = col_sums(grad_query_low)
    grad_mem_kv = jnp.concatenate(
        [grad_k_own.reshape(mem_rows, D), grad_v_own.reshape(mem_rows, D)], axis=-1
    ).astype(half)
    grad_w_cross_kv = product_tn(mem_low, grad_mem_kv)
    grad_b4 = col_sums(grad_mem_kv[:, D:])
    memory_grad = matmul_nt(grad_mem_kv, w_cross_kv)[None]
    grad_r1, grad_g0, grad_c7 = pull_one(grad_r2 + matmul_nt(grad_query_low, w_cross_q))
    grad_self_low = grad_r1.astype(half)
    grad_w_self_out = product_tn(self_att, grad_self_low)
    grad_b2 = col_sums(grad_self_low)
    grad_self_mix = (
        matmul_nt(grad_self_low, w_self_out)
        .astype(half)
        .reshape(slots_n, rows_dev, HEADS, HEAD_DIM)
    )
    self_delta = jnp.sum(grad_self_mix.astype(f32) * self_mix, axis=-1)
    scores = jnp.einsum("srhd,sthd->srht", q_self, k_all, preferred_element_type=f32) * score_scale
    self_prob = jnp.where(causal, jnp.exp(scores - self_lse[..., None]), 0.0)
    grad_prob = jnp.einsum("srhd,sthd->srht", grad_self_mix, v_all, preferred_element_type=f32)
    grad_score = (self_prob * (grad_prob - self_delta[..., None])).astype(half)
    grad_q_self = (
        jnp.einsum("srht,sthd->srhd", grad_score, k_all, preferred_element_type=f32) * score_scale
    )
    grad_v_all = jnp.einsum(
        "srht,srhd->sthd", self_prob.astype(half), grad_self_mix, preferred_element_type=f32
    )
    grad_k_all = (
        jnp.einsum("srht,srhd->sthd", grad_score, q_self, preferred_element_type=f32) * score_scale
    )
    key_grads = lax.psum_scatter(
        jnp.concatenate(
            [grad_k_all.reshape(slots_n, dec_len, D), grad_v_all.reshape(slots_n, dec_len, D)],
            axis=-1,
        ).astype(jnp.bfloat16),
        "seq",
        scatter_dimension=1,
        tiled=True,
    ).astype(jnp.float32)
    grad_proj = (
        jnp.concatenate([grad_q_self.reshape(slots_n, rows_dev, D), key_grads], axis=-1)
        .reshape(rows_total, 3 * D)
        .astype(half)
    )
    grad_w_qkv = product_tn(x_low, grad_proj)
    grad_b0 = col_sums(grad_proj[:, :D])
    grad_b1 = col_sums(grad_proj[:, 2 * D :])
    input_grad = (grad_r1 + matmul_nt(grad_proj, w_qkv)).reshape(dec_input.shape)
    grad_gains = jnp.stack([grad_g0, grad_g1, grad_g2])
    grad_bias_rows = jnp.stack(
        [grad_b0, grad_b1, grad_b2, grad_b3, grad_b4, grad_b5, grad_b6, grad_c7, grad_c8, grad_c9]
    )
    split_sums = (
        lax.psum_scatter(
            grad_w_qkv.astype(jnp.bfloat16), "doc", scatter_dimension=0, tiled=True
        ).astype(jnp.float32),
        lax.psum_scatter(
            grad_w_self_out.astype(jnp.bfloat16), "doc", scatter_dimension=0, tiled=True
        ).astype(jnp.float32),
        lax.psum_scatter(
            grad_w_cross_q.astype(jnp.bfloat16), "doc", scatter_dimension=0, tiled=True
        ).astype(jnp.float32),
        lax.psum_scatter(
            grad_w_cross_kv.astype(jnp.bfloat16), "doc", scatter_dimension=0, tiled=True
        ).astype(jnp.float32),
        lax.psum_scatter(
            grad_w_cross_out.astype(jnp.bfloat16), "doc", scatter_dimension=0, tiled=True
        ).astype(jnp.float32),
        lax.psum_scatter(
            grad_w_in.astype(jnp.bfloat16), "doc", scatter_dimension=0, tiled=True
        ).astype(jnp.float32),
        lax.psum_scatter(
            grad_b_in.astype(jnp.bfloat16), "doc", scatter_dimension=0, tiled=True
        ).astype(jnp.float32),
        lax.psum_scatter(
            grad_w_down.astype(jnp.bfloat16), "doc", scatter_dimension=0, tiled=True
        ).astype(jnp.float32),
        lax.psum_scatter(
            grad_gains.astype(jnp.bfloat16), "doc", scatter_dimension=1, tiled=True
        ).astype(jnp.float32),
        lax.psum_scatter(
            grad_bias_rows.astype(jnp.bfloat16), "doc", scatter_dimension=1, tiled=True
        ).astype(jnp.float32),
    )
    shards = (
        lax.psum(split_sums[0].astype(jnp.bfloat16), "seq").astype(jnp.float32),
        lax.psum(split_sums[1].astype(jnp.bfloat16), "seq").astype(jnp.float32),
        lax.psum(split_sums[2].astype(jnp.bfloat16), "seq").astype(jnp.float32),
        lax.psum(split_sums[3].astype(jnp.bfloat16), "seq").astype(jnp.float32),
        lax.psum(split_sums[4].astype(jnp.bfloat16), "seq").astype(jnp.float32),
        lax.psum(split_sums[5].astype(jnp.bfloat16), "seq").astype(jnp.float32),
        lax.psum(split_sums[6].astype(jnp.bfloat16), "seq").astype(jnp.float32),
        lax.psum(split_sums[7].astype(jnp.bfloat16), "seq").astype(jnp.float32),
        lax.psum(split_sums[8].astype(jnp.bfloat16), "seq").astype(jnp.float32),
        lax.psum(split_sums[9].astype(jnp.bfloat16), "seq").astype(jnp.float32),
    )
    return (
        layer_out,
        input_grad,
        memory_grad,
        shards[0],
        shards[1],
        shards[2],
        shards[3],
        shards[4],
        shards[5],
        shards[6],
        shards[7],
        shards[8],
        shards[9],
    )


def solution(mesh):
    placed = (
        P("doc", None, "seq", None),
        P("doc", "seq", None),
        P("doc", None),
        P("doc"),
        P("doc", None),
        P("doc", None),
        P("doc", None),
        P("doc", None),
        P("doc", None),
        P("doc", None),
        P("doc"),
        P("doc", None),
        P(None, "doc"),
        P(None, "doc"),
        P("doc", None, "seq", None),
    )
    return jax.shard_map(
        body,
        mesh=mesh,
        in_specs=placed,
        out_specs=(
            P("doc", None, "seq", None),
            P("doc", None, "seq", None),
            P("doc", "seq", None),
            P("doc", None),
            P("doc", None),
            P("doc", None),
            P("doc", None),
            P("doc", None),
            P("doc", None),
            P("doc"),
            P("doc", None),
            P(None, "doc"),
            P(None, "doc"),
        ),
        check_vma=False,
    )
```

profile of v0, /device:TPU:0, one launch (start us, length us, event | category | flops | bytes accessed | tf_op | source)
XLA Modules:
  0.0 2855.9 jit_solution(4454121842253261244)
XLA Ops:
  38.7 44.6 %all-gather.15.cloned.1.call-done = bf16[768,2304]{1,0:T(8,128)(2,1)} async-done(((bf16[192,2304]{1,0:T(8,128)(2,1)}), bf16[768,2304]{1,0:T(8,128)(2,1)}) %all-gather.15.cloned.1.call-update) | async-done | bytes 3538960 | tf_op jit(solution)/shard_map/all_gather | solution.py:129
  92.0 42.7 %all-gather.21.cloned.1.call-done = bf16[768,1536]{1,0:T(8,128)(2,1)} async-done(((bf16[192,1536]{1,0:T(8,128)(2,1)}), bf16[768,1536]{1,0:T(8,128)(2,1)}) %all-gather.21.cloned.1.call-update) | async-done | bytes 2359312 | tf_op jit(solution)/shard_map/all_gather | solution.py:132
  165.3 42.8 %all-gather.17.cloned.1.call-done = bf16[4,1024,1536]{2,1,0:T(8,128)(2,1)} async-done(((bf16[4,128,1536]{2,1,0:T(8,128)(2,1)}), bf16[4,1024,1536]{2,1,0:T(8,128)(2,1)}) %all-gather.17.cloned.1.call-update) | async-done | bytes 12582928 | tf_op jit(solution)/shard_map/all_gather | solution.py:149
  260.1 17.2 fusion.127
  292.6 106.3 %all-gather.23.cloned.1.call-done = bf16[8192,1536]{1,0:T(8,128)(2,1)} async-done(((bf16[1024,1536]{1,0:T(8,128)(2,1)}), bf16[8192,1536]{1,0:T(8,128)(2,1)}) %all-gather.23.cloned.1.call-update) | async-done | bytes 25165840 | tf_op jit(solution)/shard_map/all_gather | solution.py:193
  399.0 401.3 %while.30 = (s32[]{:T(128)}, f32[4,128,12]{1,0,2:T(4,128)S(1)}, f32[4,128,12]{1,0,2:T(4,128)S(1)}, f32[4,128,12,64]{1,3,0,2:T(8,128)}, s32[8]{0:T(128)S(1)}, /*i...) while((s32[]{:T(128)}, f32[4,128,12]{1,0,2:T(4,128)S(1)}, ...), condition=%wide.region_9.10_spmd.clone, body=%wide.region_4.9_spmd.clone.sunk | while | flops 1694031872 | bytes 114409792 | solution.py:209
  807.9 19.8 multiply_convert_fusion.1
  909.4 19.5 all-gather.35.cloned.1.call-done
  946.2 486.6 %while.31 = (s32[]{:T(128)}, f32[1024,12,64]{0,2,1:T(8,128)}, f32[1024,12,64]{0,2,1:T(8,128)}, bf16[8,512,12,64]{1,3,2,0:T(8,128)(2,1)}, bf16[8,512,12,64]{1,3,2...) while((s32[]{:T(128)}, f32[1024,12,64]{0,2,1:T(8,128)}, ...), condition=%wide.region_22.23_spmd.clone, body=%wide.region_21.22_spmd.clone.sunk | while | flops 4093771776 | bytes 135540912 | solution.py:273
  971.5 15.9 fusion.217
  1031.7 15.9 fusion.217
  1092.6 15.9 fusion.217
  1153.7 15.9 fusion.217
  1214.7 15.9 fusion.217
  1275.7 15.9 fusion.217
  1336.7 15.9 fusion.217
  1397.7 15.9 fusion.217
  1453.2 140.8 %copy.190 = bf16[4,1024,768]{0,2,1:T(8,128)(2,1)} copy(bf16[4,1024,768]{1,0,2:T(4,128)(2,1)} %convert_element_type.291) | data formatting | bytes 12582912
  1594.0 399.7 %reshape.442 = bf16[1024,3072]{1,0:T(8,128)(2,1)} reshape(bf16[1024,768,4]{2,1,0:T(8,128)(2,1)} %bitcast.63) | data formatting | bytes 12582912
  1994.5 61.1 %reduce-scatter.34.cloned.1.call-done = bf16[128,3072]{1,0:T(8,128)(2,1)} async-done(((bf16[1024,3072]{1,0:T(8,128)(2,1)}), bf16[128,3072]{1,0:T(8,128)(2,1)}) %reduce-scatter.34.cloned.1.call-update) | async-done | bytes 786448
  2055.6 56.4 %reshape.443 = bf16[128,768,4]{2,1,0:T(8,128)(2,1)} reshape(bf16[128,3072]{1,0:T(8,128)(2,1)} %reduce-scatter.34.cloned.1.call-done) | data formatting | bytes 1572864
  2112.0 23.6 copy.191
  2157.6 19.5 fusion.40
  2243.3 65.5 %reduce-scatter.22.cloned.1.call-done = bf16[4,128,1536]{2,1,0:T(8,128)(2,1)} async-done(((bf16[4,1024,1536]{2,1,0:T(8,128)(2,1)}), bf16[4,128,1536]{2,1,0:T(8,128)(2,1)}) %reduce-scatter.22.cloned.1.call-update) | async-done | bytes 1572880 | tf_op jit(solution)/shard_map/reduce_scatter | solution.py:316
  2361.9 65.9 %reduce-scatter.36.cloned.1.call-done = bf16[192,2304]{1,0:T(8,128)(2,1)} async-done(((bf16[768,2304]{1,0:T(8,128)(2,1)}), bf16[192,2304]{1,0:T(8,128)(2,1)}) %reduce-scatter.36.cloned.1.call-update) | async-done | bytes 884752
  2430.2 29.5 %reduce-scatter.28.cloned.1.call-done = bf16[192,768]{1,0:T(8,128)(2,1)} async-done(((bf16[768,768]{1,0:T(8,128)(2,1)}), bf16[192,768]{1,0:T(8,128)(2,1)}) %reduce-scatter.28.cloned.1.call-update) | async-done | bytes 294928 | tf_op jit(solution)/shard_map/reduce_scatter | solution.py:351
  2459.6 86.3 %reduce-scatter.30.cloned.1.call-done = bf16[192,3072]{1,0:T(8,128)(2,1)} async-done(((bf16[768,3072]{1,0:T(8,128)(2,1)}), bf16[192,3072]{1,0:T(8,128)(2,1)}) %reduce-scatter.30.cloned.1.call-update) | async-done | bytes 1179664 | tf_op jit(solution)/shard_map/reduce_scatter | solution.py:354
  2545.9 88.1 %reduce-scatter.32.cloned.1.call-done = bf16[768,768]{1,0:T(8,128)(2,1)} async-done(((bf16[3072,768]{1,0:T(8,128)(2,1)}), bf16[768,768]{1,0:T(8,128)(2,1)}) %reduce-scatter.32.cloned.1.call-update) | async-done | bytes 1179664 | tf_op jit(solution)/shard_map/reduce_scatter | solution.py:360
  2634.0 32.7 %reduce-scatter.26.cloned.1.call-done = bf16[192,768]{1,0:T(8,128)(2,1)} async-done(((bf16[768,768]{1,0:T(8,128)(2,1)}), bf16[192,768]{1,0:T(8,128)(2,1)}) %reduce-scatter.26.cloned.1.call-update) | async-done | bytes 294928 | tf_op jit(solution)/shard_map/reduce_scatter | solution.py:345
  2666.7 30.8 %reduce-scatter.24.cloned.1.call-done = bf16[192,768]{1,0:T(8,128)(2,1)} async-done(((bf16[768,768]{1,0:T(8,128)(2,1)}), bf16[192,768]{1,0:T(8,128)(2,1)}) %reduce-scatter.24.cloned.1.call-update) | async-done | bytes 294928 | tf_op jit(solution)/shard_map/reduce_scatter | solution.py:342
  2739.8 23.2 all-reduce.2
  2764.8 72.3 %all-reduce.6.cloned.1.call-done = (bf16[192,2304]{0,1:T(8,128)(2,1)}, bf16[192,1536]{0,1:T(8,128)(2,1)}, bf16[192,768]{1,0:T(8,128)(2,1)}, bf16[192,768]{1,0:T(...) async-done(((bf16[192,2304]{0,1:T(8,128)(2,1)}, bf16[192,1536]{0,1:T(8,128)(2,1)}, bf16[192,768]{1,0:T(8,128)(2,1)}, ...) | async-done | bytes 4718608 | tf_op jit(solution)/shard_map/psum | solution.py:371
  (604 shorter events, 1217.0 us)
Async XLA Ops:
  7.2 76.1 %all-gather.15.cloned.1.call-start = ((), (), s32[]{:S(2)}) async-start(), calls=%async_computation.11 | async-start | bytes 4423680 | tf_op jit(solution)/shard_map/all_gather | solution.py:129
  9.9 124.7 %all-gather.21.cloned.1.call-start = ((), (), s32[]{:S(2)}) async-start(), calls=%async_computation.14 | async-start | bytes 2949120 | tf_op jit(solution)/shard_map/all_gather | solution.py:132
  10.9 197.2 %all-gather.17.cloned.1.call-start = ((), (), s32[]{:S(2)}) async-start(), calls=%async_computation.12 | async-start | bytes 14155776 | tf_op jit(solution)/shard_map/all_gather | solution.py:149
  38.7 243.7 %copy-start.68 = (f32[768]{0:T(1024)}, f32[768]{0:T(1024)S(1)}, u32[]{:S(2)}) copy-start(f32[768]{0:T(1024)S(1)} %get-tuple-element.372) | copy-start | bytes 9220
  90.3 188.6 %all-gather.19.cloned.1.call-start = ((), (), s32[]{:S(2)}) async-start(), calls=%async_computation.13 | async-start | bytes 1474560 | tf_op jit(solution)/shard_map/all_gather | solution.py:130
  91.1 191.2 %all-gather.25.cloned.1.call-start = ((), (), s32[]{:S(2)}) async-start(), calls=%async_computation.16 | async-start | bytes 1474560 | tf_op jit(solution)/shard_map/all_gather | solution.py:131
  91.9 307.0 %all-gather.23.cloned.1.call-start = ((), (), s32[]{:S(2)}) async-start(), calls=%async_computation.15 | async-start | bytes 28311552 | tf_op jit(solution)/shard_map/all_gather | solution.py:193
  140.3 664.1 %all-gather.27.cloned.1.call-start = ((), (), s32[]{:S(2)}) async-start(), calls=%async_computation.17 | async-start | bytes 1474560 | tf_op jit(solution)/shard_map/all_gather | solution.py:133
  142.1 665.8 %all-gather.29.cloned.1.call-start = ((), (), s32[]{:S(2)}) async-start(), calls=%async_computation.18 | async-start | bytes 5898240 | tf_op jit(solution)/shard_map/all_gather | solution.py:134
  145.4 682.3 %all-gather.31.cloned.1.call-start = ((), (), s32[]{:S(2)}) async-start(), calls=%async_computation.19 | async-start | bytes 5898240 | tf_op jit(solution)/shard_map/all_gather | solution.py:136
  148.6 715.2 %all-gather.33.cloned.1.call-start = ((), (), s32[]{:S(2)}) async-start(), calls=%async_computation.20 | async-start | bytes 7077888 | tf_op jit(solution)/shard_map/all_gather | solution.py:176
  292.6 636.3 %all-gather.35.cloned.1.call-start = ((), (), s32[]{:S(2)}) async-start(), calls=%async_computation.21 | async-start | bytes 7077888 | tf_op jit(solution)/shard_map/all_gather | solution.py:239
  399.0 401.3 %copy-start.77 = (pred[4]{0:T(512)(128)(4,1)S(1)}, pred[4]{0:T(512)(128)(4,1)}, u32[]{:S(2)}) copy-start(pred[4]{0:T(512)(128)(4,1)} %iota_compare_fusion.4) | copy-start | bytes 16
  399.0 405.4 %copy-start.43 = (f32[512]{0:T(512)S(1)}, f32[512]{0:T(512)}, u32[]{:S(2)}) copy-start(f32[512]{0:T(512)} %copy-done.42) | copy-start | bytes 6148
  399.0 405.4 %copy-start.52 = (f32[768]{0:T(1024)S(1)}, f32[768]{0:T(1024)}, u32[]{:S(2)}) copy-start(f32[768]{0:T(1024)} %copy-done.51) | copy-start | bytes 9220
  399.0 405.4 %copy-start.58 = (f32[512]{0:T(512)S(1)}, f32[512]{0:T(512)}, u32[]{:S(2)}) copy-start(f32[512]{0:T(512)} %copy-done.57) | copy-start | bytes 6148
  399.0 405.4 %copy-start.69 = (f32[768]{0:T(1024)S(1)}, f32[768]{0:T(1024)}, u32[]{:S(2)}) copy-start(f32[768]{0:T(1024)} %copy-done.68) | copy-start | bytes 9220
  399.0 405.4 %copy-start.74 = (f32[768]{0:T(1024)S(1)}, f32[768]{0:T(1024)}, u32[]{:S(2)}) copy-start(f32[768]{0:T(1024)} %get-tuple-element.369) | copy-start | bytes 9220
  856.7 1198.9 %reduce-scatter.34.cloned.1.call-start = ((), (), s32[]{:S(2)}) async-start(), calls=%async_computation.28 | async-start | bytes 7077888
  1993.8 315.0 %reduce-scatter.22.cloned.1.call-start = ((), (), s32[]{:S(2)}) async-start(), calls=%async_computation.22 | async-start | bytes 14155776 | tf_op jit(solution)/shard_map/reduce_scatter | solution.py:316
  2216.2 143.5 %reduce-scatter.38.cloned.1.call-start = ((), (), s32[]{:S(2)}) async-start(), calls=%async_computation.30 | async-start | bytes 2949120
  2232.0 195.8 %reduce-scatter.36.cloned.1.call-start = ((), (), s32[]{:S(2)}) async-start(), calls=%async_computation.29 | async-start | bytes 4423680
  2320.2 139.4 %reduce-scatter.28.cloned.1.call-start = ((), (), s32[]{:S(2)}) async-start(), calls=%async_computation.25 | async-start | bytes 1474560 | tf_op jit(solution)/shard_map/reduce_scatter | solution.py:351
  2323.8 222.1 %reduce-scatter.30.cloned.1.call-start = ((), (), s32[]{:S(2)}) async-start(), calls=%async_computation.26 | async-start | bytes 5898240 | tf_op jit(solution)/shard_map/reduce_scatter | solution.py:354
  2330.5 303.5 %reduce-scatter.32.cloned.1.call-start = ((), (), s32[]{:S(2)}) async-start(), calls=%async_computation.27 | async-start | bytes 5898240 | tf_op jit(solution)/shard_map/reduce_scatter | solution.py:360
  2338.3 328.4 %reduce-scatter.26.cloned.1.call-start = ((), (), s32[]{:S(2)}) async-start(), calls=%async_computation.24 | async-start | bytes 1474560 | tf_op jit(solution)/shard_map/reduce_scatter | solution.py:345
  2343.0 354.5 %reduce-scatter.24.cloned.1.call-start = ((), (), s32[]{:S(2)}) async-start(), calls=%async_computation.23 | async-start | bytes 1474560 | tf_op jit(solution)/shard_map/reduce_scatter | solution.py:342
  2346.3 372.2 %reduce-scatter.40.cloned.1.call-start = ((), (), s32[]{:S(2)}) async-start(), calls=%async_computation.31 | async-start | bytes 245760
  2358.3 380.6 %reduce-scatter.42.cloned.1.call-start = ((), (), s32[]{:S(2)}) async-start(), calls=%async_computation.32 | async-start | bytes 245760
  2359.5 477.6 %all-reduce.6.cloned.1.call-start = ((), (), s32[]{:S(2)}) async-start(), calls=%async_computation.33 | async-start | bytes 10420224 | tf_op jit(solution)/shard_map/psum | solution.py:371
  2361.9 335.6 %copy-start.84 = (u32[32]{0:T(128)S(1)}, u32[32]{0:T(128)}, u32[]{:S(2)}) copy-start(u32[32]{0:T(128)} %constant.169) | copy-start | bytes 388
  2361.9 336.8 %copy-start.67 = (bf16[3072]{0:T(1024)(128)(2,1)S(1)}, bf16[3072]{0:T(1024)(128)(2,1)}, u32[]{:S(2)}) copy-start(bf16[3072]{0:T(1024)(128)(2,1)} %get-tuple-element.441) | copy-start | bytes 18436
  (93 other events, 1375.2 us)
Sparse Core Ops, SparseCore 0:
  10.2 73.0 all-gather.14
  85.5 49.1 all-gather.20
  137.1 70.9 all-gather.16
  210.1 30.4 all-gather.18
  242.6 29.5 all-gather.24
  274.5 124.4 all-gather.22
  401.1 30.4 all-gather.26
  433.7 88.5 all-gather.28
  524.4 87.8 all-gather.30
  614.0 69.8 all-gather.32
  856.8 72.0 all-gather.34
  1993.9 61.6 reduce-scatter.33
  2216.3 92.4 reduce-scatter.21
  2311.6 48.0 reduce-scatter.37
  2362.0 65.8 reduce-scatter.35
  2430.1 29.4 reduce-scatter.27
  2461.9 83.9 reduce-scatter.29
  2548.2 85.7 reduce-scatter.31
  2637.0 29.6 reduce-scatter.25
  2669.5 27.8 reduce-scatter.23
  2700.4 18.0 reduce-scatter.39
  2721.3 17.5 reduce-scatter.41
  2744.8 92.2 all-reduce.5
where the time goes:
time: 2880 us; the launch traced here: 2860 us
  local copies, waits for them, and re-layouts  890 us (31%)
  matrix products  857 us (30%)
  waiting for transfers between devices  805 us (28%)
  other arithmetic  188 us (7%)
  blocking collectives  91.2 us (3%)
    unnamed x193, local copies, waits for them, and re-layouts  671 us
    unnamed x28, waiting for transfers between devices  144 us
    dot_general x8, matrix products, back_block(): jnp.einsum('qhd,thd->qht', g_blk, v_own, preferred_element_type=f32)  127 us
    dot_general x8, matrix products, back_block(): jnp.einsum('qht,qhd->thd', block_prob.astype(half), g_blk, preferred_elem...  109 us
    all_gather x1, waiting for transfers between devices, body(): kv_piece = lax.all_gather(mem_kv, 'seq', axis=0, tiled=True)  106 us
    reduce_sum x8, other arithmetic, block_partial(): part_sum = jnp.sum(part_weight, axis=-1)  97.1 us
    dot_general x8, matrix products, block_partial(): jnp.einsum('sqht,thd->sqhd', part_weight.astype(jnp.bfloat16), value_blk,...  95 us
    dot_general x8, matrix products, block_partial(): jnp.einsum('sqhd,thd->sqht', query_blk, key_blk, preferred_element_type=j...  90.6 us
  transfers between devices with their start and end apart: 23, of which 17 were waited for; matrix products, arithmetic and copies ran while one was open for 24% of the time, Pallas kernels for 0%

commit v1 on v0

v1 whole, which is shorter than its diff:
```python
from functools import partial

import jax
import jax.numpy as jnp
from jax import lax
from jax.experimental import pallas as pl
from jax.experimental.pallas import tpu as pltpu
from jax.sharding import PartitionSpec as P

D = 768
HEADS = 12
HEAD_DIM = 64
HEAD_GROUPS = 4
GROUP_HEADS = HEADS // HEAD_GROUPS
GROUP_FEATS = GROUP_HEADS * HEAD_DIM

norm_eps = 1e-05
masked_score = -2e30
start_max = -1e30
score_scale = HEAD_DIM ** (-0.5)
key_tile = 256
row_tile = 256
vmem_bytes = 56 * 2**20

f32 = jnp.float32
half = jnp.bfloat16


def layer_norm(resid_in, gain_row, shift_row):
    center = resid_in - jnp.mean(resid_in, axis=-1, keepdims=True)
    variance = jnp.mean(center * center, axis=-1, keepdims=True)
    return center * lax.rsqrt(variance + norm_eps) * gain_row + shift_row


def contract(left_op, right_op, left_dim, right_dim):
    return lax.dot_general(
        left_op,
        right_op,
        (((left_dim,), (right_dim,)), ((), ())),
        preferred_element_type=f32,
    )


def dot_nn(left_op, right_op):
    return contract(left_op, right_op, 1, 0)


def dot_nt(left_op, right_op):
    return contract(left_op, right_op, 1, 1)


def dot_tn(left_op, right_op):
    return contract(left_op, right_op, 0, 0)


def dot_tt(left_op, right_op):
    return contract(left_op, right_op, 0, 1)


def col_sums(grad_low):
    return jnp.sum(grad_low.astype(f32), axis=0)


def head_rows(head):
    return slice(head * HEAD_DIM, (head + 1) * HEAD_DIM)


def self_forward_kernel(proj_ref, mix_ref, att_ref, lse_ref):
    length = proj_ref.shape[2]
    rows = min(row_tile, length)
    for head in range(GROUP_HEADS):
        feats = head_rows(head)
        for first in range(0, length, rows):
            upto = first + rows
            cols = slice(first, upto)
            q_low = proj_ref[0, feats, cols] * jnp.asarray(score_scale, half)
            k_low = proj_ref[0, GROUP_FEATS + head * HEAD_DIM : GROUP_FEATS + (head + 1) * HEAD_DIM, :upto]
            v_low = proj_ref[0, 2 * GROUP_FEATS + head * HEAD_DIM : 2 * GROUP_FEATS + (head + 1) * HEAD_DIM, :upto]
            scores = dot_tn(k_low, q_low)
            key_pos = lax.broadcasted_iota(jnp.int32, scores.shape, 0)
            row_pos = first + lax.broadcasted_iota(jnp.int32, scores.shape, 1)
            scores = jnp.where(key_pos <= row_pos, scores, masked_score)
            top = jnp.max(scores, axis=0, keepdims=True)
            weight = jnp.exp(scores - top)
            total = jnp.sum(weight, axis=0, keepdims=True)
            mix = dot_nn(v_low, weight.astype(half)) / total
            mix_ref[0, feats, cols] = mix
            att_ref[0, feats, cols] = mix.astype(half)
            lse_ref[0, head : head + 1, cols] = top + jnp.log(total)


def self_forward(proj):
    slots, feats, length = proj.shape
    return pl.pallas_call(
        self_forward_kernel,
        grid=(slots,),
        in_specs=[pl.BlockSpec((1, feats, length), lambda s: (s, 0, 0))],
        out_specs=[
            pl.BlockSpec((1, GROUP_FEATS, length), lambda s: (s, 0, 0)),
            pl.BlockSpec((1, GROUP_FEATS, length), lambda s: (s, 0, 0)),
            pl.BlockSpec((1, GROUP_HEADS, length), lambda s: (s, 0, 0)),
        ],
        out_shape=[
            jax.ShapeDtypeStruct((slots, GROUP_FEATS, length), f32),
            jax.ShapeDtypeStruct((slots, GROUP_FEATS, length), half),
            jax.ShapeDtypeStruct((slots, GROUP_HEADS, length), f32),
        ],
        compiler_params=pltpu.CompilerParams(vmem_limit_bytes=vmem_bytes),
        name="self_forward",
    )(proj)


def self_backward_kernel(proj_ref, grad_ref, mix_ref, lse_ref, dproj_ref, dk_ref, dv_ref):
    length = proj_ref.shape[2]
    rows = min(row_tile, length)
    dk_ref[...] = jnp.zeros_like(dk_ref)
    dv_ref[...] = jnp.zeros_like(dv_ref)
    for head in range(GROUP_HEADS):
        feats = head_rows(head)
        for first in range(0, length, rows):
            upto = first + rows
            cols = slice(first, upto)
            q_low = proj_ref[0, feats, cols] * jnp.asarray(score_scale, half)
            k_low = proj_ref[0, GROUP_FEATS + head * HEAD_DIM : GROUP_FEATS + (head + 1) * HEAD_DIM, :upto]
            v_low = proj_ref[0, 2 * GROUP_FEATS + head * HEAD_DIM : 2 * GROUP_FEATS + (head + 1) * HEAD_DIM, :upto]
            g_low = grad_ref[0, feats, cols]
            delta = jnp.sum(g_low.astype(f32) * mix_ref[0, feats, cols], axis=0, keepdims=True)
            scores = dot_tn(k_low, q_low)
            key_pos = lax.broadcasted_iota(jnp.int32, scores.shape, 0)
            row_pos = first + lax.broadcasted_iota(jnp.int32, scores.shape, 1)
            scores = jnp.where(key_pos <= row_pos, scores, masked_score)
            prob = jnp.exp(scores - lse_ref[0, head : head + 1, cols])
            grad_prob = dot_tn(v_low, g_low)
            grad_score = (prob * (grad_prob - delta)).astype(half)
            dv_ref[feats, :upto] += dot_nt(g_low, prob.astype(half))
            dk_ref[feats, :upto] += dot_nt(q_low, grad_score)
            dproj_ref[0, feats, cols] = (dot_nn(k_low, grad_score) * score_scale).astype(half)
    dproj_ref[0, GROUP_FEATS : 2 * GROUP_FEATS, :] = dk_ref[...].astype(half)
    dproj_ref[0, 2 * GROUP_FEATS :, :] = dv_ref[...].astype(half)


def self_backward(proj, grad_mix, mix, lse):
    slots, feats, length = proj.shape
    return pl.pallas_call(
        self_backward_kernel,
        grid=(slots,),
        in_specs=[
            pl.BlockSpec((1, feats, length), lambda s: (s, 0, 0)),
            pl.BlockSpec((1, GROUP_FEATS, length), lambda s: (s, 0, 0)),
            pl.BlockSpec((1, GROUP_FEATS, length), lambda s: (s, 0, 0)),
            pl.BlockSpec((1, GROUP_HEADS, length), lambda s: (s, 0, 0)),
        ],
        out_specs=pl.BlockSpec((1, feats, length), lambda s: (s, 0, 0)),
        out_shape=jax.ShapeDtypeStruct((slots, feats, length), half),
        scratch_shapes=[pltpu.VMEM((GROUP_FEATS, length), f32)] * 2,
        compiler_params=pltpu.CompilerParams(vmem_limit_bytes=vmem_bytes),
        name="self_backward",
    )(proj, grad_mix, mix, lse)


def cross_forward_kernel(low_ref, high_ref, q_ref, k_ref, v_ref, mix_ref, att_ref, lse_ref, acc_ref):
    slot = pl.program_id(0)
    low, high = low_ref[slot], high_ref[slot]
    rows = q_ref.shape[2]
    q_low = q_ref[0] * jnp.asarray(score_scale, half)
    first_tile = low // key_tile
    end_tile = jnp.where(high > low, (high + key_tile - 1) // key_tile, first_tile)
    acc_ref[...] = jnp.zeros_like(acc_ref)

    def step(tile, carry):
        tops, totals = carry
        start = pl.multiple_of(tile * key_tile, key_tile)
        key_pos = start + lax.broadcasted_iota(jnp.int32, (key_tile, rows), 0)
        counted = (key_pos >= low) & (key_pos < high)
        new_tops, new_totals = [], []
        for head in range(GROUP_HEADS):
            feats = head_rows(head)
            k_low = k_ref[feats, pl.ds(start, key_tile)]
            v_low = v_ref[feats, pl.ds(start, key_tile)]
            scores = jnp.where(counted, dot_tn(k_low, q_low[feats]), masked_score)
            top = jnp.maximum(tops[head], jnp.max(scores, axis=0, keepdims=True))
            weight = jnp.exp(scores - top)
            rescale = jnp.exp(tops[head] - top)
            new_totals.append(totals[head] * rescale + jnp.sum(weight, axis=0, keepdims=True))
            new_tops.append(top)
            acc_ref[feats, :] = acc_ref[feats, :] * rescale + dot_nn(v_low, weight.astype(half))
        return (tuple(new_tops), tuple(new_totals))

    init = (
        tuple(jnp.full((1, rows), start_max, f32) for _ in range(GROUP_HEADS)),
        tuple(jnp.zeros((1, rows), f32) for _ in range(GROUP_HEADS)),
    )
    tops, totals = lax.fori_loop(first_tile, end_tile, step, init)
    for head in range(GROUP_HEADS):
        feats = head_rows(head)
        live = totals[head] > 0
        total = jnp.where(live, totals[head], 1.0)
        mix = acc_ref[feats, :] / total
        mix_ref[0, feats, :] = mix
        att_ref[0, feats, :] = mix.astype(half)
        lse_ref[0, head : head + 1, :] = jnp.where(live, tops[head] + jnp.log(total), 0.0)


def cross_forward(low, high, queries, keys, values):
    slots, feats, rows = queries.shape
    tokens = keys.shape[1]
    row_block = pl.BlockSpec((1, feats, rows), lambda s, *_: (s, 0, 0))
    key_block = pl.BlockSpec((feats, tokens), lambda s, *_: (0, 0))
    return pl.pallas_call(
        cross_forward_kernel,
        grid_spec=pltpu.PrefetchScalarGridSpec(
            num_scalar_prefetch=2,
            grid=(slots,),
            in_specs=[row_block, key_block, key_block],
            out_specs=[
                row_block,
                row_block,
                pl.BlockSpec((1, GROUP_HEADS, rows), lambda s, *_: (s, 0, 0)),
            ],
            scratch_shapes=[pltpu.VMEM((feats, rows), f32)],
        ),
        out_shape=[
            jax.ShapeDtypeStruct((slots, feats, rows), f32),
            jax.ShapeDtypeStruct((slots, feats, rows), half),
            jax.ShapeDtypeStruct((slots, GROUP_HEADS, rows), f32),
        ],
        compiler_params=pltpu.CompilerParams(vmem_limit_bytes=vmem_bytes),
        name="cross_forward",
    )(low, high, queries, keys, values)


def cross_backward_kernel(
    low_ref, high_ref, q_ref, g_ref, mix_ref, lse_ref, k_ref, v_ref, dq_ref, dk_ref, dv_ref, acc_ref
):
    slot = pl.program_id(0)
    low, high = low_ref[slot], high_ref[slot]
    rows = q_ref.shape[2]
    q_low = q_ref[0] * jnp.asarray(score_scale, half)
    g_low = g_ref[0]

    @pl.when(slot == 0)
    def _():
        dk_ref[...] = jnp.zeros_like(dk_ref)
        dv_ref[...] = jnp.zeros_like(dv_ref)

    acc_ref[...] = jnp.zeros_like(acc_ref)
    product = g_low.astype(f32) * mix_ref[0]
    delta = [jnp.sum(product[head_rows(h)], axis=0, keepdims=True) for h in range(GROUP_HEADS)]
    lse = [lse_ref[0, h : h + 1, :] for h in range(GROUP_HEADS)]
    first_tile = low // key_tile
    end_tile = jnp.where(high > low, (high + key_tile - 1) // key_tile, first_tile)

    def step(tile, carry):
        start = pl.multiple_of(tile * key_tile, key_tile)
        key_pos = start + lax.broadcasted_iota(jnp.int32, (key_tile, rows), 0)
        counted = (key_pos >= low) & (key_pos < high)
        for head in range(GROUP_HEADS):
            feats = head_rows(head)
            where_keys = (feats, pl.ds(start, key_tile))
            k_low = k_ref[where_keys]
            v_low = v_ref[where_keys]
            scores = jnp.where(counted, dot_tn(k_low, q_low[feats]), masked_score)
            prob = jnp.exp(scores - lse[head])
            grad_prob = dot_tn(v_low, g_low[feats])
            grad_score = (prob * (grad_prob - delta[head])).astype(half)
            dv_ref[where_keys] += dot_nt(g_low[feats], prob.astype(half)).astype(half)
            dk_ref[where_keys] += dot_nt(q_low[feats], grad_score).astype(half)
            acc_ref[feats, :] += dot_nn(k_low, grad_score)
        return carry

    lax.fori_loop(first_tile, end_tile, step, 0)
    dq_ref[0] = (acc_ref[...] * score_scale).astype(half)


def cross_backward(low, high, queries, grad_mix, mix, lse, keys, values):
    slots, feats, rows = queries.shape
    tokens = keys.shape[1]
    row_block = pl.BlockSpec((1, feats, rows), lambda s, *_: (s, 0, 0))
    key_block = pl.BlockSpec((feats, tokens), lambda s, *_: (0, 0))
    return pl.pallas_call(
        cross_backward_kernel,
        grid_spec=pltpu.PrefetchScalarGridSpec(
            num_scalar_prefetch=2,
            grid=(slots,),
            in_specs=[
                row_block,
                row_block,
                row_block,
                pl.BlockSpec((1, GROUP_HEADS, rows), lambda s, *_: (s, 0, 0)),
                key_block,
                key_block,
            ],
            out_specs=[row_block, key_block, key_block],
            scratch_shapes=[pltpu.VMEM((feats, rows), f32)],
        ),
        out_shape=[
            jax.ShapeDtypeStruct((slots, feats, rows), half),
            jax.ShapeDtypeStruct((feats, tokens), half),
            jax.ShapeDtypeStruct((feats, tokens), half),
        ],
        compiler_params=pltpu.CompilerParams(vmem_limit_bytes=vmem_bytes),
        name="cross_backward",
    )(low, high, queries, grad_mix, mix, lse, keys, values)


def body(
    n_doc,
    n_seq,
    dec_input,
    memory,
    doc_lengths,
    doc_count,
    self_qkv,
    self_out,
    cross_q,
    cross_kv,
    cross_out,
    ffn_in,
    ffn_in_bias,
    ffn_out,
    norm_gains,
    biases,
    out_grad,
):
    seq_index = lax.axis_index("seq")
    slots_n, rows_dev = dec_input.shape[1:3]
    rows_total = slots_n * rows_dev
    mem_rows = memory.shape[1]
    spread = n_seq // HEAD_GROUPS
    head_group = seq_index // spread
    member = seq_index % spread
    member_slots = slots_n // spread
    dec_len = rows_dev * n_seq
    same_member = [[h * spread + m for h in range(HEAD_GROUPS)] for m in range(spread)]

    def gather_weight(weight):
        share = weight.shape[0] // n_seq
        piece = lax.dynamic_slice_in_dim(weight, seq_index * share, share, 0).astype(half)
        return lax.all_gather(piece, ("doc", "seq"), axis=0, tiled=True)

    def swap_heads(blocks):
        return lax.all_to_all(blocks, "seq", 0, 0, axis_index_groups=same_member, tiled=True)

    def rotate_heads(block, turn):
        return lax.ppermute(
            block,
            "seq",
            [
                (h * spread + m, (h + turn) % HEAD_GROUPS * spread + m)
                for h in range(HEAD_GROUPS)
                for m in range(spread)
            ],
        )

    def rotate_members(block, turn):
        return lax.ppermute(
            block,
            "seq",
            [
                (h * spread + m, h * spread + (m + turn) % spread)
                for h in range(HEAD_GROUPS)
                for m in range(spread)
            ],
        )

    def exchange(blocks, count, own, rotate):
        got = [lax.dynamic_index_in_dim(blocks, own, 0, keepdims=False)]
        for turn in range(1, count):
            block = lax.dynamic_index_in_dim(blocks, (own + turn) % count, 0, keepdims=False)
            got.append(rotate(block, turn))
        return jnp.stack(got)[(own - jnp.arange(count)) % count]

    qkv_piece = self_qkv.reshape(self_qkv.shape[0], 3, HEAD_GROUPS, GROUP_FEATS)
    qkv_piece = lax.dynamic_index_in_dim(qkv_piece, head_group, 2, keepdims=False)
    qkv_piece = qkv_piece.reshape(self_qkv.shape[0], 3 * GROUP_FEATS).astype(half)
    part = norm_gains.shape[1]
    small = jnp.concatenate([norm_gains, biases, ffn_in_bias.reshape(-1, part)], axis=0).astype(half)
    small_rows = small.shape[0]
    width = 3 * GROUP_FEATS
    pad_rows = -(-small_rows * part // (8 * width)) * 8
    small = jnp.pad(small.reshape(-1), (0, pad_rows * width - small_rows * part))
    first_gather = lax.all_gather(
        jnp.concatenate([qkv_piece, small.reshape(pad_rows, width)], axis=0), "doc", axis=0
    )
    w_qkv_part = first_gather[:, : self_qkv.shape[0]].reshape(D, width)
    small = first_gather[:, self_qkv.shape[0] :].reshape(n_doc, -1)[:, : small_rows * part]
    small = small.reshape(n_doc, small_rows, part).astype(f32)
    gains_f = small[:, :3].transpose(1, 0, 2).reshape(3, D)
    biases_f = small[:, 3:13].transpose(1, 0, 2).reshape(10, D)
    b_ffn_in = small[:, 13:].reshape(-1)

    x_low = dec_input[0].reshape(rows_total, D)
    x_all = lax.all_gather(dec_input[0], "seq", axis=1, tiled=True)
    x_part = lax.dynamic_slice_in_dim(x_all, member * member_slots, member_slots, 0)
    x_part = x_part.reshape(member_slots * dec_len, D)

    w_cross_kv = gather_weight(cross_kv)
    w_self_out = gather_weight(self_out)
    w_cross_q = gather_weight(cross_q)
    w_cross_out = gather_weight(cross_out)
    w_ffn_in = gather_weight(ffn_in)
    w_ffn_out = gather_weight(ffn_out)
    w_qkv = gather_weight(self_qkv)

    zero_part = jnp.zeros((GROUP_FEATS,), f32)
    b_query = lax.dynamic_slice_in_dim(biases_f[0], head_group * GROUP_FEATS, GROUP_FEATS)
    b_value = lax.dynamic_slice_in_dim(biases_f[1], head_group * GROUP_FEATS, GROUP_FEATS)
    proj = dot_tt(w_qkv_part, x_part) + jnp.concatenate([b_query, zero_part, b_value])[:, None]
    proj = proj.astype(half).reshape(width, member_slots, dec_len).transpose(1, 0, 2)
    self_mix, self_att_part, self_lse = self_forward(proj)

    def to_rows(part_grid, feats):
        blocks = part_grid.reshape(member_slots, feats, n_seq, rows_dev).transpose(2, 0, 1, 3)
        got = lax.all_to_all(blocks, "seq", 0, 0, tiled=True)
        return got.reshape(HEAD_GROUPS, spread, member_slots, feats, rows_dev)

    got = to_rows(self_att_part, GROUP_FEATS)
    self_att = got.transpose(0, 3, 1, 2, 4).reshape(D, rows_total)
    branch_self = dot_tn(self_att, w_self_out) + biases_f[2]
    norm_one, pull_one = jax.vjp(
        layer_norm, x_low.astype(f32) + branch_self, gains_f[0], biases_f[7]
    )
    norm_one_low = norm_one.astype(half)

    mem_low = memory[0]
    kv_bias = jnp.concatenate([jnp.zeros((D,), f32), biases_f[4]])
    mem_kv = (dot_tt(w_cross_kv, mem_low) + kv_bias[:, None]).astype(half)
    kv_blocks = mem_kv.reshape(2, HEAD_GROUPS, GROUP_FEATS, mem_rows).transpose(1, 0, 2, 3)
    kv_mine = exchange(kv_blocks, HEAD_GROUPS, head_group, rotate_heads)
    kv_members = [kv_mine] + [rotate_members(kv_mine, turn) for turn in range(1, spread)]
    kv_all = jnp.stack(kv_members)[(member - jnp.arange(spread)) % spread]
    kv_all = kv_all.transpose(2, 3, 1, 0, 4).reshape(2, GROUP_FEATS, n_seq * mem_rows)
    keys_all, values_all = kv_all[0], kv_all[1]

    lengths = doc_lengths[0]
    live_len = jnp.where(jnp.arange(slots_n) < doc_count[0], lengths, 0)
    key_high = jnp.minimum(jnp.cumsum(live_len), n_seq * mem_rows).astype(jnp.int32)
    key_low = jnp.concatenate([jnp.zeros((1,), jnp.int32), key_high[:-1]])

    def rows_to_heads(rows_grid):
        got = swap_heads(rows_grid.reshape(HEAD_GROUPS, GROUP_FEATS, slots_n, rows_dev))
        return got.transpose(2, 1, 0, 3).reshape(slots_n, GROUP_FEATS, HEAD_GROUPS * rows_dev)

    def heads_to_rows(heads_grid):
        blocks = heads_grid.reshape(slots_n, GROUP_FEATS, HEAD_GROUPS, rows_dev)
        return swap_heads(blocks.transpose(2, 1, 0, 3)).reshape(D, rows_total)

    cross_query = (dot_tt(w_cross_q, norm_one_low) + biases_f[3][:, None]).astype(half)
    query_part = rows_to_heads(cross_query)
    cross_mix, cross_att_part, cross_lse = cross_forward(
        key_low, key_high, query_part, keys_all, values_all
    )
    cross_att = heads_to_rows(cross_att_part)
    branch_cross = dot_tn(cross_att, w_cross_out) + biases_f[5]
    norm_two, pull_two = jax.vjp(layer_norm, norm_one + branch_cross, gains_f[1], biases_f[8])
    norm_two_low = norm_two.astype(half)
    hidden = dot_nn(norm_two_low, w_ffn_in) + b_ffn_in
    active, pull_gelu = jax.vjp(partial(jax.nn.gelu, approximate=False), hidden)
    active_low = active.astype(half)
    branch_ffn = dot_nn(active_low, w_ffn_out) + biases_f[6]
    result, pull_three = jax.vjp(layer_norm, norm_two + branch_ffn, gains_f[2], biases_f[9])
    layer_out = result.astype(half).reshape(dec_input.shape)

    def reduce_weight(grad):
        rows, cols = grad.shape
        share = rows // (n_doc * n_seq)
        pieces = grad.astype(half).reshape(n_doc, n_seq, share, cols).transpose(1, 0, 2, 3)
        over_seq = lax.psum_scatter(
            pieces.reshape(rows, cols), "seq", scatter_dimension=0, tiled=True
        )
        over_doc = lax.psum_scatter(over_seq, "doc", scatter_dimension=0, tiled=True)
        return lax.all_gather(over_doc, "seq", axis=0, tiled=True).astype(f32)

    grad_r3, grad_g2, grad_c9 = pull_three(out_grad[0].reshape(rows_total, D).astype(f32))
    grad_ffn_low = grad_r3.astype(half)
    grad_w_down = reduce_weight(dot_tn(active_low, grad_ffn_low))
    grad_b6 = col_sums(grad_ffn_low)
    grad_hidden = pull_gelu(dot_nt(grad_ffn_low, w_ffn_out))[0].astype(half)
    grad_w_in = reduce_weight(dot_tn(norm_two_low, grad_hidden))
    grad_b_in = col_sums(grad_hidden)
    grad_r2, grad_g1, grad_c8 = pull_two(grad_r3 + dot_nt(grad_hidden, w_ffn_in))
    grad_cross_low = grad_r2.astype(half)
    grad_w_cross_out = reduce_weight(dot_nn(cross_att, grad_cross_low))
    grad_b5 = col_sums(grad_cross_low)
    grad_mix = dot_nt(w_cross_out, grad_cross_low).astype(half)
    grad_query_part, grad_keys, grad_values = cross_backward(
        key_low,
        key_high,
        query_part,
        rows_to_heads(grad_mix),
        cross_mix,
        cross_lse,
        keys_all,
        values_all,
    )
    grad_query = heads_to_rows(grad_query_part)
    grad_w_cross_q = reduce_weight(dot_tt(norm_one_low, grad_query))
    grad_b3 = jnp.sum(grad_query.astype(f32), axis=1)
    grad_r1, grad_g0, grad_c7 = pull_one(grad_r2 + dot_tt(grad_query, w_cross_q))
    grad_self_low = grad_r1.astype(half)
    grad_w_self_out = reduce_weight(dot_nn(self_att, grad_self_low))
    grad_b2 = col_sums(grad_self_low)
    grad_self_mix = dot_nt(w_self_out, grad_self_low).astype(half)
    blocks = grad_self_mix.reshape(HEAD_GROUPS, GROUP_FEATS, spread, member_slots, rows_dev)
    blocks = blocks.transpose(0, 2, 3, 1, 4).reshape(n_seq, member_slots, GROUP_FEATS, rows_dev)
    got = lax.all_to_all(blocks, "seq", 0, 0, tiled=True)
    grad_self_part = got.transpose(1, 2, 0, 3).reshape(member_slots, GROUP_FEATS, dec_len)
    grad_proj_part = self_backward(proj, grad_self_part, self_mix, self_lse)

    grad_kv = jnp.stack([grad_keys, grad_values]).reshape(
        2, GROUP_FEATS, HEAD_GROUPS, spread, mem_rows
    )
    grad_kv = grad_kv.transpose(3, 2, 0, 1, 4)
    grad_kv = jnp.sum(exchange(grad_kv, spread, member, rotate_members).astype(f32), axis=0)
    grad_kv = exchange(grad_kv.astype(half), HEAD_GROUPS, head_group, rotate_heads)
    grad_mem_kv = grad_kv.transpose(1, 0, 2, 3).reshape(2 * D, mem_rows)
    grad_w_cross_kv = reduce_weight(dot_tt(mem_low, grad_mem_kv))
    grad_b4 = jnp.sum(grad_mem_kv[D:].astype(f32), axis=1)
    memory_grad = dot_tt(grad_mem_kv, w_cross_kv)[None]

    grad_part = dot_tt(
        x_part, grad_proj_part.transpose(1, 0, 2).reshape(width, member_slots * dec_len)
    ).astype(half)
    share = self_qkv.shape[0] // spread
    grad_part = grad_part.reshape(n_doc, spread, share, width).transpose(1, 0, 2, 3)
    grad_part = jnp.sum(exchange(grad_part, spread, member, rotate_members).astype(f32), axis=0)
    grad_part = lax.psum_scatter(
        grad_part.astype(half).reshape(n_doc * share, width), "doc", scatter_dimension=0, tiled=True
    )
    grad_w_qkv = lax.all_gather(grad_part, "seq", axis=0)
    grad_w_qkv = grad_w_qkv.reshape(HEAD_GROUPS, spread, share, 3, GROUP_FEATS)
    grad_w_qkv = grad_w_qkv.transpose(1, 2, 3, 0, 4).reshape(self_qkv.shape).astype(f32)
    got = to_rows(grad_proj_part, width).reshape(
        HEAD_GROUPS, slots_n, 3, GROUP_FEATS, rows_dev
    )
    grad_proj = got.transpose(2, 0, 3, 1, 4).reshape(3 * D, rows_total)
    row_sums = jnp.sum(grad_proj.astype(f32), axis=1)
    grad_b0 = row_sums[:D]
    grad_b1 = row_sums[2 * D :]
    input_grad = (grad_r1 + dot_tt(grad_proj, w_qkv)).reshape(dec_input.shape)

    small_grad = jnp.concatenate(
        [
            jnp.stack(
                [grad_g0, grad_g1, grad_g2]
                + [grad_b0, grad_b1, grad_b2, grad_b3, grad_b4, grad_b5, grad_b6]
                + [grad_c7, grad_c8, grad_c9]
            ),
            grad_b_in.reshape(n_doc, -1, part).transpose(1, 0, 2).reshape(-1, D),
        ]
    ).astype(half)
    small_grad = lax.psum(small_grad, ("doc", "seq"))
    small_grad = lax.dynamic_slice_in_dim(
        small_grad, lax.axis_index("doc") * part, part, 1
    ).astype(f32)
    return (
        layer_out,
        input_grad,
        memory_grad,
        grad_w_qkv,
        grad_w_self_out,
        grad_w_cross_q,
        grad_w_cross_kv,
        grad_w_cross_out,
        grad_w_in,
        small_grad[13:].reshape(-1),
        grad_w_down,
        small_grad[:3],
        small_grad[3:13],
    )


def solution(mesh):
    placed = (
        P("doc", None, "seq", None),
        P("doc", "seq", None),
        P("doc", None),
        P("doc"),
        P("doc", None),
        P("doc", None),
        P("doc", None),
        P("doc", None),
        P("doc", None),
        P("doc", None),
        P("doc"),
        P("doc", None),
        P(None, "doc"),
        P(None, "doc"),
        P("doc", None, "seq", None),
    )
    return jax.shard_map(
        partial(body, mesh.shape["doc"], mesh.shape["seq"]),
        mesh=mesh,
        in_specs=placed,
        out_specs=(
            P("doc", None, "seq", None),
            P("doc", None, "seq", None),
            P("doc", "seq", None),
            P("doc", None),
            P("doc", None),
            P("doc", None),
            P("doc", None),
            P("doc", None),
            P("doc", None),
            P("doc"),
            P("doc", None),
            P(None, "doc"),
            P(None, "doc"),
        ),
        check_vma=False,
    )
```

time: 2880 us -> 1060 us (0.37)
  matrix products: 857 us -> 94 us
  local copies, waits for them, and re-layouts: 890 us -> 156 us
  waiting for transfers between devices: 805 us -> 455 us
  other arithmetic: 188 us -> 43.2 us
  Pallas kernels: 0 us -> 125 us
  starting transfers between devices: 1.17 us -> 37.1 us
  blocking collectives: 91.2 us -> 125 us
    dot_general x83 -> x21, matrix products: 857 us -> 94 us  [contract(): lax.dot_general(left_op, right_op, (((left_dim,), (right_dim,)), ((), ())...]
    unnamed x193 -> x68, local copies, waits for them, and re-layouts: 671 us -> 12.2 us
    reduce_scatter x6 -> x13, waiting for transfers between devices: 333 us -> 116 us  [the longest x6 54 us: reduce_weight(): lax.psum_scatter(pieces.reshape(rows, cols), 'seq', scatter_dimension=0,...]
    unnamed x28 -> x23, waiting for transfers between devices: 144 us -> 2.51 us
    pallas_call x0 -> x4, Pallas kernels: none -> 125 us  [the longest x1 52.4 us: cross_backward(): pl.pallas_call(cross_backward_kernel, grid_spec=pltpu.PrefetchScalarGridS...]
    reduce_sum x26 -> x8, other arithmetic: 130 us -> 11 us  [the longest x1 4.66 us: body(): jnp.sum(exchange(grad_kv, spread, member, rotate_members).astype(f32), ax...]
    ppermute x0 -> x9, waiting for transfers between devices: none -> 80.8 us  [the longest x6 79 us: rotate_heads(): lax.ppermute(block, 'seq', [(h * spread + m, (h + turn) % HEAD_GROUPS * s...]
    psum x1 -> x0, waiting for transfers between devices: 72.3 us -> none  [body(): lax.psum(split_sums[0].astype(jnp.bfloat16), 'seq').astype(jnp.float32)]
  transfers between devices with their start and end apart: 23 -> 39, of which waited for: 17 -> 25; matrix products, arithmetic and copies ran while one was open for 24% -> 25% of each run, Pallas kernels for 0% -> 12%
where the time goes in v1:
time: 1060 us; the launch traced here: 1050 us
  waiting for transfers between devices  455 us (43%)
  local copies, waits for them, and re-layouts  156 us (15%)
  blocking collectives  125 us (12%)
  Pallas kernels  125 us (12%)
  matrix products  94 us (9%)
  other arithmetic  43.2 us (4%)
  starting transfers between devices  37.1 us (4%)
  between operations  16.2 us (2%)
    all_gather x7, waiting for transfers between devices, gather_weight(): return lax.all_gather(piece, ('doc', 'seq'), axis=0, tiled=True)  197 us
    dot_general x21, matrix products, contract(): lax.dot_general(left_op, right_op, (((left_dim,), (right_dim,)), ((), ())...  94 us
    ppermute x6, waiting for transfers between devices, rotate_heads(): lax.ppermute(block, 'seq', [(h * spread + m, (h + turn) % HEAD_GROUPS * s...  79 us
    reduce_scatter x6, waiting for transfers between devices, reduce_weight(): lax.psum_scatter(pieces.reshape(rows, cols), 'seq', scatter_dimension=0,...  54 us
    pallas_call x1, Pallas kernels, cross_backward(): pl.pallas_call(cross_backward_kernel, grid_spec=pltpu.PrefetchScalarGridS...  52.4 us
    all_gather x4, blocking collectives, reduce_weight(): return lax.all_gather(over_doc, 'seq', axis=0, tiled=True).astype(f32)  49.2 us
    pallas_call x1, Pallas kernels, cross_forward(): pl.pallas_call(cross_forward_kernel, grid_spec=pltpu.PrefetchScalarGridSp...  45.6 us
    reduce_scatter x6, waiting for transfers between devices, reduce_weight(): lax.psum_scatter(over_seq, 'doc', scatter_dimension=0, tiled=True)  39.6 us
  transfers between devices with their start and end apart: 39, of which 25 were waited for; matrix products, arithmetic and copies ran while one was open for 25% of the time, Pallas kernels for 12%

profile of v1, /device:TPU:0, one launch (start us, length us, event | category | flops | bytes accessed | tf_op | source)
XLA Modules:
  0.0 1051.9 jit_solution(14212440523517144452)
XLA Ops:
  22.7 25.8 %all-gather = bf16[800,576]{1,0:T(8,128)(2,1)S(1)} all-gather(bf16[200,576]{1,0:T(8,128)(2,1)S(1)} %copy.182), channel_id=2, replica_groups=mesh['doc'=4,'seq'=8] {'doc'}, dimensions={0}, use_global_device_ids=true | all-gather | bytes 1152000 | tf_op jit(solution)/shard_map/all_gather | solution.py:382
  49.9 23.2 %all-gather.18.cloned.1.call-done = bf16[768,1536]{1,0:T(8,128)(2,1)} async-done(((bf16[24,1536]{1,0:T(8,128)(2,1)}), bf16[768,1536]{1,0:T(8,128)(2,1)}) %all-gather.18.cloned.1.call-update) | async-done | bytes 2359312 | tf_op jit(solution)/shard_map/all_gather | solution.py:339
  82.3 25.1 %collective-permute-done.2 = bf16[2,192,1024]{2,1,0:T(8,128)(2,1)S(1)} collective-permute-done((bf16[2,192,1024]{2,1,0:T(8,128)(2,1)S(1)}, bf16[2,192,1024]{2,1,0:T(8,128)(2,1)S(1)}, u32[]{:S(2)}, u32[]{:S(2)}) %collective-permute-start.2) | collective-permute-done | bytes 786464 | tf_op jit(solution)/shard_map/ppermute | solution.py:345
  107.4 18.1 %collective-permute-done.1 = bf16[2,192,1024]{2,1,0:T(8,128)(2,1)S(1)} collective-permute-done((bf16[2,192,1024]{2,1,0:T(8,128)(2,1)S(1)}, bf16[2,192,1024]{2,1,0:T(8,128)(2,1)S(1)}, u32[]{:S(2)}, u32[]{:S(2)}) %collective-permute-start.1) | collective-permute-done | bytes 786464 | tf_op jit(solution)/shard_map/ppermute | solution.py:345
  133.6 9.9 all-gather.32.cloned.1.call-done
  149.7 13.4 %self_forward.1 = (f32[2,192,1024]{2,1,0:T(8,128)}, bf16[2,192,1024]{2,1,0:T(8,128)(2,1)}, f32[2,3,1024]{2,1,0:T(4,128)}) custom-call(bf16[2,576,1024]{2,1,0:T(8,128)(2,1)} %bitcast.228), custom_call_target="tpu_custom_call" | custom-call | tf_op jit(solution)/shard_map/self_forward/pallas_call | solution.py:94
  189.1 11.8 %all-gather.14.cloned.1.call-done = bf16[768,768]{1,0:T(8,128)(2,1)} async-done(((bf16[24,768]{1,0:T(8,128)(2,1)}), bf16[768,768]{1,0:T(8,128)(2,1)}) %all-gather.14.cloned.1.call-update) | async-done | bytes 1179664 | tf_op jit(solution)/shard_map/all_gather | solution.py:339
  205.0 52.2 %all-gather.16.cloned.1.call-done = bf16[768,768]{1,0:T(8,128)(2,1)} async-done(((bf16[24,768]{1,0:T(8,128)(2,1)}), bf16[768,768]{1,0:T(8,128)(2,1)}) %all-gather.16.cloned.1.call-update) | async-done | bytes 1179664 | tf_op jit(solution)/shard_map/all_gather | solution.py:339
  294.3 45.6 %cross_forward.1 = (f32[4,192,512]{2,1,0:T(8,128)}, bf16[4,192,512]{2,1,0:T(8,128)(2,1)}, f32[4,3,512]{2,1,0:T(4,128)}) custom-call(s32[4]{0:T(128)} %pad_add_fusion.low_ref, s32[4]{0:T(128)} %get-tuple-element.89.high_ref, bf16[4,192,512]{2,1,0:T(8,128)(2,1)} %copy_bitcast_fusion.2.q_ref, bf16[192,8192]{1,0:T(8,128)(2,1)} %squeeze.70.k_ref, ...), custom_call_target="tpu_custom_call" | custom-call | tf_op jit(solution)/shard_map/cross_forward/pallas_call | solution.py:209
  347.9 10.4 all-to-all-done.2
  362.6 16.9 %all-gather.22.cloned.1.call-done = bf16[768,3072]{1,0:T(8,128)(2,1)} async-done(((bf16[24,3072]{1,0:T(8,128)(2,1)}), bf16[768,3072]{1,0:T(8,128)(2,1)}) %all-gather.22.cloned.1.call-update) | async-done | bytes 4718608 | tf_op jit(solution)/shard_map/all_gather | solution.py:339
  379.5 19.8 %multiply_convert_fusion = (bf16[512,3072]{1,0:T(8,128)(2,1)}, f32[512,3072]{1,0:T(8,128)}, f32[512,3072]{1,0:T(8,128)}) fusion(f32[3072]{0:T(1024)S(1)} %add.359, bf16[768,3072]{1,0:T(8,128)(2,1)} %all-gather.22.cloned.1.call-done, f32[512,768]{1,0:T(8,128)S(1)} %get-tuple-element.94, f32[768]{0:T(1024)S(1)} %add.356, f32[768]{0:T(1024)S(1)} %mul.228, ...), kind=kOutput, calls=%fused_computation.16 | convolution fusion | flops 2521694208 | bytes 22042624 | tf_op jit(solution)/shard_map/dot_general | solution.py:36
  399.3 46.1 %all-gather.24.cloned.1.call-done = bf16[3072,768]{1,0:T(8,128)(2,1)} async-done(((bf16[96,768]{1,0:T(8,128)(2,1)}), bf16[3072,768]{1,0:T(8,128)(2,1)}) %all-gather.24.cloned.1.call-update) | async-done | bytes 4718608 | tf_op jit(solution)/shard_map/all_gather | solution.py:339
  493.5 20.3 %all-to-all-done.3 = bf16[4,192,4,128]{3,1,2,0:T(8,128)(2,1)S(1)} async-done(((bf16[4,192,4,128]{3,1,2,0:T(8,128)(2,1)}), bf16[4,192,4,128]{3,1,2,0:T(8,128)(2,1)S(1)}, u32[]{:S(2)}, u32[]{:S(2)}) %all-to-all-start.3) | async-done | bytes 786464 | tf_op jit(solution)/shard_map/all_to_all | solution.py:342
  514.8 52.4 %cross_backward.1 = (bf16[4,192,512]{2,1,0:T(8,128)(2,1)}, bf16[192,8192]{1,0:T(8,128)(2,1)}, bf16[192,8192]{1,0:T(8,128)(2,1)}) custom-call(s32[4]{0:T(128)} %pad_add_fusion.low_ref, s32[4]{0:T(128)} %get-tuple-element.89.high_ref, bf16[4,192,512]{2,1,0:T(8,128)(2,1)} %copy_bitcast_fusion.2.q_ref, bf16[4,192,512]{2,1,0:T(8,128)(2,1)} %copy_bitcast_fusion.1.g_ref, ...), custom_call_target="tpu_custom_call" | custom-call | tf_op jit(solution)/shard_map/cross_backward/pallas_call | solution.py:280
  591.5 6.8 dynamic-slice_bitcast_fusion.1
  628.2 16.7 %collective-permute-done.7 = bf16[2,192,1024]{2,1,0:T(8,128)(2,1)S(1)} collective-permute-done((bf16[2,192,1024]{2,1,0:T(8,128)(2,1)S(1)}, bf16[2,192,1024]{2,1,0:T(8,128)(2,1)S(1)}, u32[]{:S(2)}, u32[]{:S(2)}) %collective-permute-start.7) | collective-permute-done | bytes 786464 | tf_op jit(solution)/shard_map/ppermute | solution.py:345
  644.9 18.6 %collective-permute-done.6 = bf16[2,192,1024]{2,1,0:T(8,128)(2,1)S(1)} collective-permute-done((bf16[2,192,1024]{2,1,0:T(8,128)(2,1)S(1)}, bf16[2,192,1024]{2,1,0:T(8,128)(2,1)S(1)}, u32[]{:S(2)}, u32[]{:S(2)}) %collective-permute-start.6) | collective-permute-done | bytes 786464 | tf_op jit(solution)/shard_map/ppermute | solution.py:345
  682.3 13.4 %all-to-all-done.5 = bf16[8,2,192,128]{3,2,1,0:T(8,128)(2,1)S(1)} async-done(((bf16[8,2,192,128]{3,2,1,0:T(8,128)(2,1)}), bf16[8,2,192,128]{3,2,1,0:T(8,128)(2,1)S(1)}, u32[]{:S(2)}, u32[]{:S(2)}) %all-to-all-start.5) | async-done | bytes 786464 | tf_op jit(solution)/shard_map/all_to_all | solution.py:506
  696.8 13.8 %self_backward.1 = bf16[2,576,1024]{2,1,0:T(8,128)(2,1)} custom-call(bf16[2,576,1024]{2,1,0:T(8,128)(2,1)} %bitcast.229, bf16[2,192,1024]{2,1,0:T(8,128)(2,1)} %copy_bitcast_fusion.grad_ref, f32[2,192,1024]{2,1,0:T(8,128)} %get-tuple-element.27.mix_ref, f32[2,3,1024]{2,1,0:T(4,128)} %get-tuple-element.28.lse_ref), custom_call_target="tpu_custom_call" | custom-call | tf_op jit(solution)/shard_map/self_backward/pallas_call | solution.py:144
  723.7 9.5 reduce-scatter.20.cloned.1.call-done
  735.0 44.5 %reduce-scatter.24.cloned.1.call-done = bf16[96,1536]{1,0:T(8,128)(2,1)} async-done(((bf16[768,1536]{1,0:T(8,128)(2,1)}), bf16[96,1536]{1,0:T(8,128)(2,1)}) %reduce-scatter.24.cloned.1.call-update) | async-done | bytes 294928 | tf_op jit(solution)/shard_map/reduce_scatter | solution.py:468
  779.5 24.1 %reduce-scatter.34.cloned.1.call-done = bf16[24,3072]{1,0:T(8,128)(2,1)} async-done(((bf16[96,3072]{1,0:T(8,128)(2,1)}), bf16[24,3072]{1,0:T(8,128)(2,1)}) %reduce-scatter.34.cloned.1.call-update) | async-done | bytes 147472 | tf_op jit(solution)/shard_map/reduce_scatter | solution.py:471
  812.6 10.7 %reduce-scatter.30.cloned.1.call-done = bf16[24,768]{1,0:T(8,128)(2,1)} async-done(((bf16[96,768]{1,0:T(8,128)(2,1)}), bf16[24,768]{1,0:T(8,128)(2,1)}) %reduce-scatter.30.cloned.1.call-update) | async-done | bytes 36880 | tf_op jit(solution)/shard_map/reduce_scatter | solution.py:471
  823.3 19.3 %all_gather.69 = bf16[192,768]{1,0:T(8,128)(2,1)S(1)} all-gather(bf16[24,768]{1,0:T(8,128)(2,1)} %reduce-scatter.30.cloned.1.call-done), channel_id=1, replica_groups=mesh['doc'=4,'seq'=8] {'seq'}, dimensions={0}, use_global_device_ids=true | all-gather | bytes 331776 | tf_op jit(solution)/shard_map/all_gather | solution.py:472
  845.8 22.5 %reduce-scatter.40.cloned.1.call-done = bf16[96,576]{1,0:T(8,128)(2,1)} async-done(((bf16[384,576]{1,0:T(8,128)(2,1)}), bf16[96,576]{1,0:T(8,128)(2,1)}) %reduce-scatter.40.cloned.1.call-update) | async-done | bytes 110608 | tf_op jit(solution)/shard_map/reduce_scatter | solution.py:527
  868.3 11.1 %all-gather.2 = bf16[768,576]{1,0:T(8,128)(2,1)S(1)} all-gather(bf16[96,576]{1,0:T(8,128)(2,1)} %reduce-scatter.40.cloned.1.call-done), channel_id=4, replica_groups=mesh['doc'=4,'seq'=8] {'seq'}, dimensions={0}, use_global_device_ids=true | all-gather | bytes 995328 | tf_op jit(solution)/shard_map/all_gather | solution.py:530
  895.2 9.3 all_gather.66
  907.9 9.6 all_gather.67
  922.2 47.2 %all-gather.26.cloned.1.call-done = bf16[768,2304]{1,0:T(8,128)(2,1)} async-done(((bf16[24,2304]{1,0:T(8,128)(2,1)}), bf16[768,2304]{1,0:T(8,128)(2,1)}) %all-gather.26.cloned.1.call-update) | async-done | bytes 3538960 | tf_op jit(solution)/shard_map/all_gather | solution.py:339
  976.6 39.1 %psum.7 = bf16[17,768]{1,0:T(8,128)(2,1)S(1)} all-reduce(bf16[17,768]{1,0:T(8,128)(2,1)S(1)} %concatenate.26), channel_id=1, replica_groups=mesh['doc'=4,'seq'=8] {'doc','seq'}, use_global_device_ids=true, to_apply=%region_39.40 | all-reduce | flops 13056 | bytes 52224 | tf_op jit(solution)/shard_map/psum | solution.py:552
  1023.6 11.1 %all_gather.68 = bf16[192,1536]{1,0:T(8,128)(2,1)S(1)} all-gather(bf16[24,1536]{1,0:T(8,128)(2,1)} %reduce-scatter.26.cloned.1.call-done), channel_id=1, replica_groups=mesh['doc'=4,'seq'=8] {'seq'}, dimensions={0}, use_global_device_ids=true | all-gather | bytes 663552 | tf_op jit(solution)/shard_map/all_gather | solution.py:472
  (341 shorter events, 317.6 us)
Async XLA Ops:
  7.2 65.9 %all-gather.18.cloned.1.call-start = ((), (), s32[]{:S(2)}) async-start(), calls=%async_computation.22 | async-start | bytes 2433024 | tf_op jit(solution)/shard_map/all_gather | solution.py:339
  9.0 134.5 %all-gather.32.cloned.1.call-start = ((), (), s32[]{:S(2)}) async-start(), calls=%async_computation.41 | async-start | bytes 7077888 | tf_op jit(solution)/shard_map/all_gather | solution.py:393
  9.7 191.2 %all-gather.14.cloned.1.call-start = ((), (), s32[]{:S(2)}) async-start(), calls=%async_computation.20 | async-start | bytes 1216512 | tf_op jit(solution)/shard_map/all_gather | solution.py:339
  11.3 245.9 %all-gather.16.cloned.1.call-start = ((), (), s32[]{:S(2)}) async-start(), calls=%async_computation.21 | async-start | bytes 1216512 | tf_op jit(solution)/shard_map/all_gather | solution.py:339
  12.9 335.0 %all-gather.20.cloned.1.call-start = ((), (), s32[]{:S(2)}) async-start(), calls=%async_computation.23 | async-start | bytes 1216512 | tf_op jit(solution)/shard_map/all_gather | solution.py:339
  14.5 365.0 %all-gather.22.cloned.1.call-start = ((), (), s32[]{:S(2)}) async-start(), calls=%async_computation.24 | async-start | bytes 4866048 | tf_op jit(solution)/shard_map/all_gather | solution.py:339
  15.3 430.2 %all-gather.24.cloned.1.call-start = ((), (), s32[]{:S(2)}) async-start(), calls=%async_computation.25 | async-start | bytes 4866048 | tf_op jit(solution)/shard_map/all_gather | solution.py:339
  78.6 28.8 %collective-permute-start.2 = (bf16[2,192,1024]{2,1,0:T(8,128)(2,1)S(1)}, bf16[2,192,1024]{2,1,0:T(8,128)(2,1)S(1)}, u32[]{:S(2)}, u32[]{:S(2)}) collective-permute-start(bf16[2,192,1024]{2,1,0:T(8,128)(2,1)S(1)} %get-tuple-element.83), channel_id=1, source_target_pairs={{0,6},{1,7},{2,0},{3,1},{4,2},{5,3},{6,4},{7,5},{8,14},{9,15},{10,... | collective-permute-start | bytes 2359304 | tf_op jit(solution)/shard_map/ppermute | solution.py:345
  80.1 45.4 %collective-permute-start.1 = (bf16[2,192,1024]{2,1,0:T(8,128)(2,1)S(1)}, bf16[2,192,1024]{2,1,0:T(8,128)(2,1)S(1)}, u32[]{:S(2)}, u32[]{:S(2)}) collective-permute-start(bf16[2,192,1024]{2,1,0:T(8,128)(2,1)S(1)} %get-tuple-element.84), channel_id=1, source_target_pairs={{0,4},{1,5},{2,6},{3,7},{4,0},{5,1},{6,2},{7,3},{8,12},{9,13},{10,... | collective-permute-start | bytes 2359304 | tf_op jit(solution)/shard_map/ppermute | solution.py:345
  81.5 44.5 %collective-permute-start = (bf16[2,192,1024]{2,1,0:T(8,128)(2,1)S(1)}, bf16[2,192,1024]{2,1,0:T(8,128)(2,1)S(1)}, u32[]{:S(2)}, u32[]{:S(2)}) collective-permute-start(bf16[2,192,1024]{2,1,0:T(8,128)(2,1)S(1)} %get-tuple-element.85), channel_id=1, source_target_pairs={{0,2},{1,3},{2,4},{3,5},{4,6},{5,7},{6,0},{7,1},{8,10},{9,11},{10,... | collective-permute-start | bytes 2359304 | tf_op jit(solution)/shard_map/ppermute | solution.py:345
  128.8 42.0 %collective-permute-start.3 = (bf16[4,2,192,1024]{3,2,1,0:T(8,128)(2,1)}, bf16[4,2,192,1024]{3,2,1,0:T(8,128)(2,1)}, u32[]{:S(2)}, u32[]{:S(2)}) collective-permute-start(bf16[4,2,192,1024]{3,2,1,0:T(8,128)(2,1)} %gather_fusion), channel_id=1, source_target_pairs={{0,1},{1,0},{2,3},{3,2},{4,5},{5,4},{6,7},{7,6},{8,9},{9,8},{10,11... | collective-permute-start | bytes 9437192 | tf_op jit(solution)/shard_map/ppermute | solution.py:356
  265.5 26.6 %all-to-all-start.1 = ((bf16[4,192,4,128]{3,1,2,0:T(8,128)(2,1)}), bf16[4,192,4,128]{3,1,2,0:T(8,128)(2,1)}, u32[]{:S(2)}, u32[]{:S(2)}) async-start(bf16[4,192,4,128]{3,1,2,0:T(8,128)(2,1)} %copy.186), calls=%async_computation.1 | async-start | bytes 1572864 | tf_op jit(solution)/shard_map/all_to_all | solution.py:342
  347.4 328.1 %reduce-scatter.32.cloned.1.call-start = ((), (), s32[]{:S(2)}) async-start(), calls=%async_computation.35 | async-start | bytes 5308416 | tf_op jit(solution)/shard_map/reduce_scatter | solution.py:468
  469.5 212.3 %reduce-scatter.28.cloned.1.call-start = ((), (), s32[]{:S(2)}) async-start(), calls=%async_computation.33 | async-start | bytes 1327104 | tf_op jit(solution)/shard_map/reduce_scatter | solution.py:468
  479.2 231.4 %reduce-scatter.36.cloned.1.call-start = ((), (), s32[]{:S(2)}) async-start(), calls=%async_computation.38 | async-start | bytes 5308416 | tf_op jit(solution)/shard_map/reduce_scatter | solution.py:468
  570.4 27.9 %all-to-all-start.4 = ((bf16[4,192,4,128]{3,2,1,0:T(4,128)(2,1)}), bf16[4,192,4,128]{3,2,1,0:T(4,128)(2,1)}, u32[]{:S(2)}, u32[]{:S(2)}) async-start(bf16[4,192,4,128]{3,2,1,0:T(4,128)(2,1)} %bitcast.225), calls=%async_computation.4 | async-start | bytes 1572864 | tf_op jit(solution)/shard_map/all_to_all | solution.py:342
  574.5 148.6 %reduce-scatter.16.cloned.1.call-start = ((), (), s32[]{:S(2)}) async-start(), calls=%async_computation.27 | async-start | bytes 1327104 | tf_op jit(solution)/shard_map/reduce_scatter | solution.py:468
  604.4 128.9 %reduce-scatter.20.cloned.1.call-start = ((), (), s32[]{:S(2)}) async-start(), calls=%async_computation.29 | async-start | bytes 1327104 | tf_op jit(solution)/shard_map/reduce_scatter | solution.py:468
  607.8 171.7 %reduce-scatter.24.cloned.1.call-start = ((), (), s32[]{:S(2)}) async-start(), calls=%async_computation.31 | async-start | bytes 2654208 | tf_op jit(solution)/shard_map/reduce_scatter | solution.py:468
  627.0 36.5 %collective-permute-start.6 = (bf16[2,192,1024]{2,1,0:T(8,128)(2,1)S(1)}, bf16[2,192,1024]{2,1,0:T(8,128)(2,1)S(1)}, u32[]{:S(2)}, u32[]{:S(2)}) collective-permute-start(bf16[2,192,1024]{2,1,0:T(8,128)(2,1)S(1)} %get-tuple-element.80), channel_id=1, source_target_pairs={{0,4},{1,5},{2,6},{3,7},{4,0},{5,1},{6,2},{7,3},{8,12},{9,13},{10,... | collective-permute-start | bytes 2359304 | tf_op jit(solution)/shard_map/ppermute | solution.py:345
  627.6 35.9 %collective-permute-start.5 = (bf16[2,192,1024]{2,1,0:T(8,128)(2,1)S(1)}, bf16[2,192,1024]{2,1,0:T(8,128)(2,1)S(1)}, u32[]{:S(2)}, u32[]{:S(2)}) collective-permute-start(bf16[2,192,1024]{2,1,0:T(8,128)(2,1)S(1)} %get-tuple-element.81), channel_id=1, source_target_pairs={{0,2},{1,3},{2,4},{3,5},{4,6},{5,7},{6,0},{7,1},{8,10},{9,11},{10,... | collective-permute-start | bytes 2359304 | tf_op jit(solution)/shard_map/ppermute | solution.py:345
  675.4 128.2 %reduce-scatter.34.cloned.1.call-start = ((), (), s32[]{:S(2)}) async-start(), calls=%async_computation.36 | async-start | bytes 737280 | tf_op jit(solution)/shard_map/reduce_scatter | solution.py:471
  681.7 141.6 %reduce-scatter.30.cloned.1.call-start = ((), (), s32[]{:S(2)}) async-start(), calls=%async_computation.34 | async-start | bytes 184320 | tf_op jit(solution)/shard_map/reduce_scatter | solution.py:471
  682.3 163.5 %reduce-scatter.38.cloned.1.call-start = ((), (), s32[]{:S(2)}) async-start(), calls=%async_computation.39 | async-start | bytes 737280 | tf_op jit(solution)/shard_map/reduce_scatter | solution.py:471
  710.6 157.7 %reduce-scatter.40.cloned.1.call-start = ((), (), s32[]{:S(2)}) async-start(), calls=%async_computation.42 | async-start | bytes 614400 | tf_op jit(solution)/shard_map/reduce_scatter | solution.py:527
  723.1 172.1 %reduce-scatter.18.cloned.1.call-start = ((), (), s32[]{:S(2)}) async-start(), calls=%async_computation.28 | async-start | bytes 184320 | tf_op jit(solution)/shard_map/reduce_scatter | solution.py:471
  723.7 184.2 %reduce-scatter.22.cloned.1.call-start = ((), (), s32[]{:S(2)}) async-start(), calls=%async_computation.30 | async-start | bytes 184320 | tf_op jit(solution)/shard_map/reduce_scatter | solution.py:471
  733.3 236.2 %all-gather.26.cloned.1.call-start = ((), (), s32[]{:S(2)}) async-start(), calls=%async_computation.26 | async-start | bytes 3649536 | tf_op jit(solution)/shard_map/all_gather | solution.py:339
  734.9 288.7 %reduce-scatter.26.cloned.1.call-start = ((), (), s32[]{:S(2)}) async-start(), calls=%async_computation.32 | async-start | bytes 368640 | tf_op jit(solution)/shard_map/reduce_scatter | solution.py:471
  779.5 256.3 %all-gather.28.cloned.1.call-start = ((), (), s32[]{:S(2)}) async-start(), calls=%async_computation.37 | async-start | bytes 1327104 | tf_op jit(solution)/shard_map/all_gather | solution.py:472
  805.7 112.6 %all-to-all-start.6 = ((bf16[8,2,576,128]{3,2,1,0:T(8,128)(2,1)}), bf16[8,2,576,128]{3,2,1,0:T(8,128)(2,1)S(1)}, u32[]{:S(2)}, u32[]{:S(2)}) async-start(bf16[8,2,576,128]{3,2,1,0:T(8,128)(2,1)} %bitcast_bitcast_fusion), calls=%async_computation.6 | async-start | bytes 4718592 | tf_op jit(solution)/shard_map/all_to_all | solution.py:414
  809.4 232.7 %all-gather.30.cloned.1.call-start = ((), (), s32[]{:S(2)}) async-start(), calls=%async_computation.40 | async-start | bytes 1327104 | tf_op jit(solution)/shard_map/all_gather | solution.py:472
  (40 other events, 441.0 us)
Sparse Core Ops, SparseCore 0:
  11.5 61.5 all-gather.17
  75.0 68.4 all-gather.31
  147.0 53.8 all-gather.13
  204.2 52.9 all-gather.15
  260.6 53.0 all-gather.19
  316.9 62.5 all-gather.21
  383.0 62.4 all-gather.23
  469.6 61.1 reduce-scatter.31
  534.4 36.7 reduce-scatter.27
  574.5 53.8 reduce-scatter.35
  632.5 59.0 reduce-scatter.15
  695.3 37.9 reduce-scatter.19
  737.0 42.4 reduce-scatter.23
  781.6 21.9 reduce-scatter.33
  805.7 17.5 reduce-scatter.29
  825.6 20.2 reduce-scatter.37
  848.6 19.6 reduce-scatter.39
  870.4 17.5 reduce-scatter.17
  890.4 17.4 reduce-scatter.21
  911.2 58.2 all-gather.25
  971.7 18.6 reduce-scatter.25
  992.3 22.5 all-gather.27
  1016.9 25.1 all-gather.29

commit v2 on v1

v2 whole, which is shorter than its diff:
```python
from functools import partial

import jax
import jax.numpy as jnp
from jax import lax
from jax.experimental import pallas as pl
from jax.experimental.pallas import tpu as pltpu
from jax.sharding import PartitionSpec as P

D = 768
HEADS = 12
HEAD_DIM = 64
HEAD_GROUPS = 4
GROUP_HEADS = HEADS // HEAD_GROUPS
GROUP_FEATS = GROUP_HEADS * HEAD_DIM

norm_eps = 1e-05
masked_score = -2e30
start_max = -1e30
score_scale = HEAD_DIM ** (-0.5)
key_tile = 256
row_tile = 256
vmem_bytes = 56 * 2**20

f32 = jnp.float32
half = jnp.bfloat16


def layer_norm(resid_in, gain_row, shift_row):
    center = resid_in - jnp.mean(resid_in, axis=-1, keepdims=True)
    variance = jnp.mean(center * center, axis=-1, keepdims=True)
    return center * lax.rsqrt(variance + norm_eps) * gain_row + shift_row


def contract(left_op, right_op, left_dim, right_dim):
    return lax.dot_general(
        left_op,
        right_op,
        (((left_dim,), (right_dim,)), ((), ())),
        preferred_element_type=f32,
    )


def dot_nn(left_op, right_op):
    return contract(left_op, right_op, 1, 0)


def dot_nt(left_op, right_op):
    return contract(left_op, right_op, 1, 1)


def dot_tn(left_op, right_op):
    return contract(left_op, right_op, 0, 0)


def dot_tt(left_op, right_op):
    return contract(left_op, right_op, 0, 1)


def col_sums(grad_low):
    return jnp.sum(grad_low.astype(f32), axis=0)


def normalize(resid):
    center = resid - jnp.mean(resid, axis=-1, keepdims=True)
    scale = lax.rsqrt(jnp.mean(center * center, axis=-1, keepdims=True) + norm_eps)
    return center * scale, scale


def norm_backward(incoming, gain_row, unit, scale):
    grad = incoming * gain_row
    mean_one = jnp.mean(grad, axis=-1, keepdims=True)
    mean_two = jnp.mean(grad * unit, axis=-1, keepdims=True)
    return (grad - mean_one - unit * mean_two) * scale


def row_sum(grad):
    return jnp.sum(grad, axis=0, keepdims=True)


def store_rows(packed_ref, n_doc, grad, cols):
    n_seq, rows = packed_ref.shape[:2]
    share = rows // n_doc
    for s in range(n_seq):
        mine = [grad[(z * n_seq + s) * share : (z * n_seq + s + 1) * share] for z in range(n_doc)]
        packed_ref[s, :, cols] = jnp.concatenate(mine, axis=0).astype(half)


def head_feats(head, block=0):
    start = block * GROUP_FEATS + head * HEAD_DIM
    return slice(start, start + HEAD_DIM)


def load_rows(place_ref, piece_refs, x_ref, sems):
    spread = place_ref.shape[0] // HEAD_GROUPS
    slots = x_ref.shape[0]
    rows_dev = x_ref.shape[1] // place_ref.shape[0]
    member = place_ref[0] % spread
    copies = []
    for i in range(place_ref.shape[0]):
        turn_m, turn_h = i // HEAD_GROUPS, i % HEAD_GROUPS
        if turn_m:
            piece = piece_refs[HEAD_GROUPS + turn_m - 1].at[turn_h]
        else:
            piece = piece_refs[turn_h].at[pl.ds(member * slots, slots)]
        first = pl.multiple_of(place_ref[i] * rows_dev, rows_dev)
        copies.append(
            pltpu.make_async_copy(piece, x_ref.at[:, pl.ds(first, rows_dev)], sems.at[i])
        )
    for copy in copies:
        copy.start()
    for copy in copies:
        copy.wait()


def self_forward_kernel(place_ref, w_ref, bias_ref, *rest):
    pieces, (proj_ref, mix_ref, att_ref, lse_ref, x_ref, sems) = rest[:-6], rest[-6:]
    slot = pl.program_id(0)

    @pl.when(slot == 0)
    def _():
        load_rows(place_ref, pieces, x_ref, sems)

    length = proj_ref.shape[1]
    rows_dev = att_ref.shape[3]
    rows = min(row_tile, length)
    for first in range(0, length, rows):
        part = dot_nn(x_ref[slot, first : first + rows, :], w_ref[...]) + bias_ref[0:1, :]
        proj_ref[:, first : first + rows] = part.astype(half).T
    for head in range(GROUP_HEADS):
        feats = head_feats(head)
        for first in range(0, length, rows):
            upto = first + rows
            cols = slice(first, upto)
            q_low = proj_ref[feats, cols] * jnp.asarray(score_scale, half)
            k_low = proj_ref[head_feats(head, 1), :upto]
            v_low = proj_ref[head_feats(head, 2), :upto]
            scores = dot_tn(k_low, q_low)
            key_pos = lax.broadcasted_iota(jnp.int32, scores.shape, 0)
            row_pos = first + lax.broadcasted_iota(jnp.int32, scores.shape, 1)
            scores = jnp.where(key_pos <= row_pos, scores, masked_score)
            top = jnp.max(scores, axis=0, keepdims=True)
            weight = jnp.exp(scores - top)
            total = jnp.sum(weight, axis=0, keepdims=True)
            mix = dot_nn(v_low, weight.astype(half)) / total
            mix_ref[0, feats, cols] = mix
            mix_low = mix.astype(half)
            for place in range(rows // rows_dev):
                att_ref[first // rows_dev + place, 0, feats, :] = mix_low[
                    :, place * rows_dev : (place + 1) * rows_dev
                ]
            lse_ref[0, head : head + 1, cols] = top + jnp.log(total)


def self_forward(places, w_part, bias, pieces, n_seq, *after):
    slots = pieces[0].shape[0] * HEAD_GROUPS // n_seq
    length = pieces[0].shape[1] * n_seq
    feats, rows_dev = w_part.shape[1], length // n_seq
    return pl.pallas_call(
        self_forward_kernel,
        grid_spec=pltpu.PrefetchScalarGridSpec(
            num_scalar_prefetch=1,
            grid=(slots,),
            in_specs=[
                pl.BlockSpec(w_part.shape, lambda s, *_: (0, 0)),
                pl.BlockSpec(bias.shape, lambda s, *_: (0, 0)),
            ]
            + [pl.BlockSpec(memory_space=pl.ANY)] * (len(pieces) + len(after)),
            out_specs=[
                pl.BlockSpec((feats, length), lambda s, *_: (0, s)),
                pl.BlockSpec((1, GROUP_FEATS, length), lambda s, *_: (s, 0, 0)),
                pl.BlockSpec((n_seq, 1, GROUP_FEATS, rows_dev), lambda s, *_: (0, s, 0, 0)),
                pl.BlockSpec((1, GROUP_HEADS, length), lambda s, *_: (s, 0, 0)),
            ],
            scratch_shapes=[
                pltpu.VMEM((slots, length, D), half),
                pltpu.SemaphoreType.DMA((n_seq,)),
            ],
        ),
        out_shape=[
            jax.ShapeDtypeStruct((feats, slots * length), half),
            jax.ShapeDtypeStruct((slots, GROUP_FEATS, length), f32),
            jax.ShapeDtypeStruct((n_seq, slots, GROUP_FEATS, rows_dev), half),
            jax.ShapeDtypeStruct((slots, GROUP_HEADS, length), f32),
        ],
        compiler_params=pltpu.CompilerParams(vmem_limit_bytes=vmem_bytes),
        name="self_forward",
    )(places, w_part, bias, *pieces, *after)


def self_backward_kernel(n_doc, place_ref, proj_ref, grad_ref, mix_ref, lse_ref, *rest):
    ins, (send_ref, w_grad_ref, sums_ref, dproj_ref, dk_ref, dv_ref, w_acc, x_ref, sems) = (
        rest[:-9],
        rest[-9:],
    )
    pieces = ins[: HEAD_GROUPS + place_ref.shape[0] // HEAD_GROUPS - 1]
    slot = pl.program_id(0)

    @pl.when(slot == 0)
    def _():
        load_rows(place_ref, pieces, x_ref, sems)
        w_acc[...] = jnp.zeros_like(w_acc)
        sums_ref[...] = jnp.zeros_like(sums_ref)

    length = proj_ref.shape[1]
    n_seq, rows_dev = grad_ref.shape[0], grad_ref.shape[3]
    rows = min(row_tile, length)
    dk_ref[...] = jnp.zeros_like(dk_ref)
    dv_ref[...] = jnp.zeros_like(dv_ref)
    for head in range(GROUP_HEADS):
        feats = head_feats(head)
        for first in range(0, length, rows):
            upto = first + rows
            cols = slice(first, upto)
            places = range(first // rows_dev, upto // rows_dev)
            q_low = proj_ref[feats, cols] * jnp.asarray(score_scale, half)
            k_low = proj_ref[head_feats(head, 1), :upto]
            v_low = proj_ref[head_feats(head, 2), :upto]
            g_low = jnp.concatenate([grad_ref[place, 0, feats, :] for place in places], axis=1)
            delta = jnp.sum(g_low.astype(f32) * mix_ref[0, feats, cols], axis=0, keepdims=True)
            scores = dot_tn(k_low, q_low)
            key_pos = lax.broadcasted_iota(jnp.int32, scores.shape, 0)
            row_pos = first + lax.broadcasted_iota(jnp.int32, scores.shape, 1)
            scores = jnp.where(key_pos <= row_pos, scores, masked_score)
            prob = jnp.exp(scores - lse_ref[0, head : head + 1, cols])
            grad_prob = dot_tn(v_low, g_low)
            grad_score = (prob * (grad_prob - delta)).astype(half)
            dv_ref[feats, :upto] += dot_nt(g_low, prob.astype(half))
            dk_ref[feats, :upto] += dot_nt(q_low, grad_score)
            dproj_ref[feats, cols] = (dot_nn(k_low, grad_score) * score_scale).astype(half)
    dproj_ref[GROUP_FEATS : 2 * GROUP_FEATS, :] = dk_ref[...].astype(half)
    dproj_ref[2 * GROUP_FEATS :, :] = dv_ref[...].astype(half)
    for place in range(n_seq):
        send_ref[place, 0] = dproj_ref[:, place * rows_dev : (place + 1) * rows_dev]
    for first in range(0, length, rows):
        turned = dproj_ref[:, first : first + rows].T
        sums_ref[0:1, :] += row_sum(turned.astype(f32))
        w_acc[...] += dot_tn(x_ref[slot, first : first + rows, :], turned)

    @pl.when(slot == pl.num_programs(0) - 1)
    def _():
        spread, stored, width = w_grad_ref.shape
        share = stored // n_doc
        feats = dproj_ref.shape[0]
        quarters = width // feats
        for m in range(spread):
            for q in range(quarters):
                mine = []
                for z in range(n_doc):
                    first = ((z * spread + m) * quarters + q) * share
                    mine.append(w_acc[first : first + share, :])
                w_grad_ref[m, :, q * feats : (q + 1) * feats] = jnp.concatenate(
                    mine, axis=0
                ).astype(half)


def self_backward(n_doc, places, proj, grad_mix, mix, lse, pieces, *after):
    n_seq, slots, _, rows_dev = grad_mix.shape
    feats, length = proj.shape[0], n_seq * rows_dev
    spread = n_seq // HEAD_GROUPS
    stored = D // n_seq
    return pl.pallas_call(
        partial(self_backward_kernel, n_doc),
        grid_spec=pltpu.PrefetchScalarGridSpec(
            num_scalar_prefetch=1,
            grid=(slots,),
            in_specs=[
                pl.BlockSpec((feats, length), lambda s, *_: (0, s)),
                pl.BlockSpec((n_seq, 1, GROUP_FEATS, rows_dev), lambda s, *_: (0, s, 0, 0)),
                pl.BlockSpec((1, GROUP_FEATS, length), lambda s, *_: (s, 0, 0)),
                pl.BlockSpec((1, GROUP_HEADS, length), lambda s, *_: (s, 0, 0)),
            ]
            + [pl.BlockSpec(memory_space=pl.ANY)] * (len(pieces) + len(after)),
            out_specs=[
                pl.BlockSpec((n_seq, 1, feats, rows_dev), lambda s, *_: (0, s, 0, 0)),
                pl.BlockSpec((spread, stored, HEAD_GROUPS * feats), lambda s, *_: (0, 0, 0)),
                pl.BlockSpec((8, feats), lambda s, *_: (0, 0)),
            ],
            scratch_shapes=[
                pltpu.VMEM((feats, length), half),
                pltpu.VMEM((GROUP_FEATS, length), f32),
                pltpu.VMEM((GROUP_FEATS, length), f32),
                pltpu.VMEM((D, feats), f32),
                pltpu.VMEM((slots, length, D), half),
                pltpu.SemaphoreType.DMA((n_seq,)),
            ],
        ),
        out_shape=[
            jax.ShapeDtypeStruct((n_seq, slots, feats, rows_dev), half),
            jax.ShapeDtypeStruct((spread, stored, HEAD_GROUPS * feats), half),
            jax.ShapeDtypeStruct((8, feats), f32),
        ],
        compiler_params=pltpu.CompilerParams(vmem_limit_bytes=vmem_bytes),
        name="self_backward",
    )(places, proj, grad_mix, mix, lse, *pieces, *after)


def enter_kernel(att_ref, x_ref, vec_ref, w_ref, norm_ref, unit_ref, scale_ref, send_ref, att_all):
    gather_att(att_ref, att_all)
    slots, rows_dev = send_ref.shape[1], send_ref.shape[3]
    rows = min(middle_rows, x_ref.shape[0])
    for first in range(0, x_ref.shape[0], rows):
        where = slice(first, first + rows)
        branch = dot_tn(att_all[:, where], w_ref[:, :D]) + vec_ref[0:1, :]
        unit, scale = normalize(x_ref[where, :].astype(f32) + branch)
        norm = unit * vec_ref[1:2, :] + vec_ref[2:3, :]
        norm_ref[where, :] = norm
        unit_ref[where, :] = unit
        scale_ref[where, :] = jnp.broadcast_to(scale, (rows, scale_ref.shape[1]))
        query = dot_nn(norm.astype(half), w_ref[:, D:]) + vec_ref[3:4, :]
        query = query.astype(half).T
        for group in range(HEAD_GROUPS):
            for place in range(rows // rows_dev):
                send_ref[group, first // rows_dev + place] = query[
                    group * GROUP_FEATS : (group + 1) * GROUP_FEATS,
                    place * rows_dev : (place + 1) * rows_dev,
                ]


def gather_att(att_ref, att_all):
    n_seq, member_slots, _, rows_dev = att_ref.shape
    spread = n_seq // HEAD_GROUPS
    for source in range(n_seq):
        group, m = source // spread, source % spread
        for inner in range(member_slots):
            slot = m * member_slots + inner
            att_all[
                group * GROUP_FEATS : (group + 1) * GROUP_FEATS,
                slot * rows_dev : (slot + 1) * rows_dev,
            ] = att_ref[source, inner]


def enter(att, x_low, vectors, w_pair, slots):
    rows_total, rows_dev = x_low.shape[0], att.shape[3]
    vmem = pl.BlockSpec(memory_space=pltpu.VMEM)
    return pl.pallas_call(
        enter_kernel,
        in_specs=[vmem] * 4,
        out_specs=[vmem] * 4,
        out_shape=[
            jax.ShapeDtypeStruct((rows_total, D), f32),
            jax.ShapeDtypeStruct((rows_total, D), f32),
            jax.ShapeDtypeStruct((rows_total, 128), f32),
            jax.ShapeDtypeStruct((HEAD_GROUPS, slots, GROUP_FEATS, rows_dev), half),
        ],
        scratch_shapes=[pltpu.VMEM((D, rows_total), half)],
        compiler_params=pltpu.CompilerParams(vmem_limit_bytes=vmem_bytes),
        name="enter",
    )(att, x_low, vectors, w_pair)


def leave_kernel(
    n_doc,
    query_ref,
    att_ref,
    resid_ref,
    norm_ref,
    unit_ref,
    scale_ref,
    vec_ref,
    w_ref,
    *rest,
):
    out_ref, send_ref, packed_ref, sums_ref, att_all, query_all, query_rows, low_rows = rest[-8:]
    slots, rows_dev = query_ref.shape[1], query_ref.shape[3]
    member_slots = att_ref.shape[1]
    spread = slots // member_slots
    rows_total = resid_ref.shape[0]
    rows = min(middle_rows, rows_total)
    gather_att(att_ref, att_all)
    for group in range(HEAD_GROUPS):
        for slot in range(slots):
            query_all[
                group * GROUP_FEATS : (group + 1) * GROUP_FEATS,
                slot * rows_dev : (slot + 1) * rows_dev,
            ] = query_ref[group, slot]
    sums_ref[...] = jnp.zeros_like(sums_ref)
    for first in range(0, rows_total, rows):
        where = slice(first, first + rows)
        query = query_all[:, where].T
        query_rows[where, :] = query
        sums_ref[3:4, :] += row_sum(query.astype(f32))
        incoming = resid_ref[where, :] + dot_nt(query, w_ref[:, D:])
        unit = unit_ref[where, :]
        sums_ref[0:1, :] += row_sum(incoming * unit)
        sums_ref[1:2, :] += row_sum(incoming)
        grad = norm_backward(incoming, vec_ref[1:2, :], unit, scale_ref[where, 0:1])
        out_ref[where, :] = grad
        grad_low = grad.astype(half)
        low_rows[where, :] = grad_low
        sums_ref[2:3, :] += row_sum(grad_low.astype(f32))
    grad_att = dot_nt(w_ref[:, :D], low_rows[...]).astype(half)
    for target in range(HEAD_GROUPS * spread):
        group, m = target // spread, target % spread
        for inner in range(member_slots):
            slot = m * member_slots + inner
            send_ref[target, inner] = grad_att[
                group * GROUP_FEATS : (group + 1) * GROUP_FEATS,
                slot * rows_dev : (slot + 1) * rows_dev,
            ]
    store_rows(packed_ref, n_doc, dot_nn(att_all[...], low_rows[...]), slice(0, D))
    grad = dot_tn(norm_ref[...].astype(half), query_rows[...])
    store_rows(packed_ref, n_doc, grad, slice(D, 2 * D))


def leave(n_doc, grad_query, att, resid, norm_one, unit, scale, vectors, w_pair, *after):
    rows_total, n_seq = resid.shape[0], att.shape[0]
    vmem = pl.BlockSpec(memory_space=pltpu.VMEM)
    return pl.pallas_call(
        partial(leave_kernel, n_doc),
        in_specs=[vmem] * 8 + [pl.BlockSpec(memory_space=pl.ANY)] * len(after),
        out_specs=[vmem] * 4,
        out_shape=[
            jax.ShapeDtypeStruct((rows_total, D), f32),
            jax.ShapeDtypeStruct(att.shape, half),
            jax.ShapeDtypeStruct((n_seq, D // n_seq, 2 * D), half),
            jax.ShapeDtypeStruct((8, D), f32),
        ],
        scratch_shapes=[
            pltpu.VMEM((D, rows_total), half),
            pltpu.VMEM((D, rows_total), half),
            pltpu.VMEM((rows_total, D), half),
            pltpu.VMEM((rows_total, D), half),
        ],
        compiler_params=pltpu.CompilerParams(vmem_limit_bytes=vmem_bytes),
        name="leave",
    )(grad_query, att, resid, norm_one, unit, scale, vectors, w_pair, *after)


def memory_kernel(n_doc, place_ref, mem_ref, rows_a_ref, rows_b_ref, rows_c_ref, *rest):
    pieces, (packed_ref, all_ref) = rest[: place_ref.shape[0]], rest[-2:]
    for turn, piece in enumerate(pieces):
        for kind in range(2):
            first = pl.multiple_of(kind * D + place_ref[turn] * GROUP_FEATS, GROUP_FEATS)
            all_ref[pl.ds(first, GROUP_FEATS), :] = piece[kind]
    turned = all_ref[...].T
    for kind in range(2):
        cols = slice(kind * D, (kind + 1) * D)
        store_rows(packed_ref, n_doc, dot_tn(mem_ref[...], turned[:, cols]), cols)
    value_sum = row_sum(turned[:, D:].astype(f32))
    small = [rows_a_ref[...], rows_b_ref[...], rows_c_ref[...], value_sum]
    used = sum(rows.shape[0] for rows in small)
    small.append(jnp.zeros((small_cols - used, D), f32))
    store_rows(
        packed_ref, n_doc, jnp.concatenate(small, axis=0).T, slice(2 * D, 2 * D + small_cols)
    )


small_cols = 128


def memory_backward(n_doc, n_seq, places, mem_low, rows_a, rows_b, rows_c, pieces, *after):
    tokens = mem_low.shape[0]
    vmem = pl.BlockSpec(memory_space=pltpu.VMEM)
    return pl.pallas_call(
        partial(memory_kernel, n_doc),
        grid_spec=pltpu.PrefetchScalarGridSpec(
            num_scalar_prefetch=1,
            grid=(1,),
            in_specs=[vmem] * (4 + len(pieces))
            + [pl.BlockSpec(memory_space=pl.ANY)] * len(after),
            out_specs=[vmem] * 2,
        ),
        out_shape=[
            jax.ShapeDtypeStruct((n_seq, D // n_seq, 2 * D + small_cols), half),
            jax.ShapeDtypeStruct((2 * D, tokens), half),
        ],
        compiler_params=pltpu.CompilerParams(vmem_limit_bytes=vmem_bytes),
        name="memory_backward",
    )(places, mem_low, rows_a, rows_b, rows_c, *pieces, *after)


def finish_kernel(
    n_seq,
    stack_n,
    in_ref,
    qkv_ref,
    out_ref,
    q_ref,
    kv_ref,
    small_ref,
    bias_ref,
    down_ref,
    ffn_ref,
    cross_ref,
):
    rows = in_ref.shape[0]
    share = rows // n_seq
    spread = n_seq // HEAD_GROUPS
    out_ref[...] = in_ref[:, :D].astype(f32)
    q_ref[...] = in_ref[:, D : 2 * D].astype(f32)
    kv_ref[...] = in_ref[:, 2 * D : 4 * D].astype(f32)
    small_ref[...] = in_ref[:, 4 * D : 4 * D + small_cols].astype(f32).T
    first_col = 4 * D + small_cols
    feats = 3 * GROUP_FEATS
    ff = ffn_ref.shape[1]
    down_col = first_col + HEAD_GROUPS * feats + small_cols
    ffn_col = down_col + stack_n * D
    ffn_ref[...] = in_ref[:, ffn_col : ffn_col + ff].astype(f32)
    cross_ref[...] = in_ref[:, ffn_col + ff :].astype(f32)
    for q in range(stack_n):
        mine = in_ref[:, down_col + q * D : down_col + (q + 1) * D].astype(f32)
        for s in range(n_seq):
            first = (s * stack_n + q) * share
            down_ref[first : first + share, :] = mine[s * share : (s + 1) * share]
    bias = jnp.zeros(bias_ref.shape, f32)
    wide = in_ref[:, first_col:down_col].astype(f32)
    for s in range(n_seq):
        group, m = s // spread, s % spread
        mine = wide[s * share : (s + 1) * share]
        for q in range(HEAD_GROUPS):
            first = (m * HEAD_GROUPS + q) * share
            for part in range(3):
                start = q * feats + part * GROUP_FEATS
                qkv_ref[
                    first : first + share,
                    part * D + group * GROUP_FEATS : part * D + (group + 1) * GROUP_FEATS,
                ] = mine[:, start : start + GROUP_FEATS]
        bias = bias + mine[:, HEAD_GROUPS * feats :]
    bias_ref[...] = bias


def finish(n_seq, stack_n, packed):
    rows = packed.shape[0]
    vmem = pl.BlockSpec(memory_space=pltpu.VMEM)
    return pl.pallas_call(
        partial(finish_kernel, n_seq, stack_n),
        in_specs=[vmem],
        out_specs=[vmem] * 9,
        out_shape=[
            jax.ShapeDtypeStruct((rows, 3 * D), f32),
            jax.ShapeDtypeStruct((rows, D), f32),
            jax.ShapeDtypeStruct((rows, D), f32),
            jax.ShapeDtypeStruct((rows, 2 * D), f32),
            jax.ShapeDtypeStruct((small_cols, rows), f32),
            jax.ShapeDtypeStruct((rows // n_seq, small_cols), f32),
            jax.ShapeDtypeStruct((rows * stack_n, D), f32),
            jax.ShapeDtypeStruct((rows, stack_n * D), f32),
            jax.ShapeDtypeStruct((rows, D), f32),
        ],
        compiler_params=pltpu.CompilerParams(vmem_limit_bytes=vmem_bytes),
        name="finish",
    )(packed)


def load_pieces(place_ref, piece_refs, kv_ref, sems):
    tokens = piece_refs[0].shape[2]
    copies = [
        pltpu.make_async_copy(
            piece,
            kv_ref.at[:, :, pl.ds(pl.multiple_of(place_ref[i] * tokens, tokens), tokens)],
            sems.at[i],
        )
        for i, piece in enumerate(piece_refs)
    ]
    for copy in copies:
        copy.start()
    for copy in copies:
        copy.wait()


def tiles_of(low, high):
    first = low // key_tile
    return first, jnp.where(high > low, (high + key_tile - 1) // key_tile, first)


def cross_forward_kernel(low_ref, high_ref, place_ref, q_ref, *rest):
    pieces, (mix_ref, att_ref, lse_ref, acc_ref, kv_ref, sems) = rest[:-6], rest[-6:]
    slot = pl.program_id(0)

    @pl.when(slot == 0)
    def _():
        load_pieces(place_ref, pieces, kv_ref, sems)

    low, high = low_ref[slot], high_ref[slot]
    rows_dev = q_ref.shape[3]
    q_low = jnp.concatenate([q_ref[i, 0] for i in range(HEAD_GROUPS)], axis=1)
    q_low = q_low * jnp.asarray(score_scale, half)
    rows = q_low.shape[1]
    acc_ref[...] = jnp.zeros_like(acc_ref)

    def step(tile, carry):
        tops, totals = carry
        start = pl.multiple_of(tile * key_tile, key_tile)
        key_pos = start + lax.broadcasted_iota(jnp.int32, (key_tile, rows), 0)
        counted = (key_pos >= low) & (key_pos < high)
        new_tops, new_totals = [], []
        for head in range(GROUP_HEADS):
            feats = head_feats(head)
            k_low = kv_ref[0, feats, pl.ds(start, key_tile)]
            v_low = kv_ref[1, feats, pl.ds(start, key_tile)]
            scores = jnp.where(counted, dot_tn(k_low, q_low[feats]), masked_score)
            top = jnp.maximum(tops[head], jnp.max(scores, axis=0, keepdims=True))
            weight = jnp.exp(scores - top)
            rescale = jnp.exp(tops[head] - top)
            new_totals.append(totals[head] * rescale + jnp.sum(weight, axis=0, keepdims=True))
            new_tops.append(top)
            acc_ref[feats, :] = acc_ref[feats, :] * rescale + dot_nn(v_low, weight.astype(half))
        return (tuple(new_tops), tuple(new_totals))

    init = (
        tuple(jnp.full((1, rows), start_max, f32) for _ in range(GROUP_HEADS)),
        tuple(jnp.zeros((1, rows), f32) for _ in range(GROUP_HEADS)),
    )
    tops, totals = lax.fori_loop(*tiles_of(low, high), step, init)
    for head in range(GROUP_HEADS):
        feats = head_feats(head)
        live = totals[head] > 0
        total = jnp.where(live, totals[head], 1.0)
        mix = acc_ref[feats, :] / total
        mix_ref[0, feats, :] = mix
        mix_low = mix.astype(half)
        for i in range(HEAD_GROUPS):
            att_ref[i, 0, feats, :] = mix_low[:, i * rows_dev : (i + 1) * rows_dev]
        lse_ref[0, head : head + 1, :] = jnp.where(live, tops[head] + jnp.log(total), 0.0)


def cross_forward(low, high, places, queries, pieces):
    groups, slots, feats, rows_dev = queries.shape
    rows = groups * rows_dev
    tokens = pieces[0].shape[2] * len(pieces)
    row_block = pl.BlockSpec((groups, 1, feats, rows_dev), lambda s, *_: (0, s, 0, 0))
    return pl.pallas_call(
        cross_forward_kernel,
        grid_spec=pltpu.PrefetchScalarGridSpec(
            num_scalar_prefetch=3,
            grid=(slots,),
            in_specs=[row_block] + [pl.BlockSpec(memory_space=pl.ANY)] * len(pieces),
            out_specs=[
                pl.BlockSpec((1, feats, rows), lambda s, *_: (s, 0, 0)),
                row_block,
                pl.BlockSpec((1, GROUP_HEADS, rows), lambda s, *_: (s, 0, 0)),
            ],
            scratch_shapes=[
                pltpu.VMEM((feats, rows), f32),
                pltpu.VMEM((2, feats, tokens), half),
                pltpu.SemaphoreType.DMA((len(pieces),)),
            ],
        ),
        out_shape=[
            jax.ShapeDtypeStruct((slots, feats, rows), f32),
            jax.ShapeDtypeStruct(queries.shape, half),
            jax.ShapeDtypeStruct((slots, GROUP_HEADS, rows), f32),
        ],
        compiler_params=pltpu.CompilerParams(vmem_limit_bytes=vmem_bytes),
        name="cross_forward",
    )(low, high, places, queries, *pieces)


def cross_backward_kernel(
    low_ref, high_ref, place_ref, q_ref, g_ref, mix_ref, lse_ref, *rest
):
    count = place_ref.shape[0]
    spread = count // HEAD_GROUPS
    pieces = rest[:count]
    dq_ref, *dkv_outs = rest[-5 - spread : -4]
    dkv_ref, acc_ref, kv_ref, sems = rest[-4:]
    member = place_ref[0] % spread
    slot = pl.program_id(0)

    @pl.when(slot == 0)
    def _():
        dkv_ref[...] = jnp.zeros_like(dkv_ref)
        load_pieces(place_ref, pieces, kv_ref, sems)

    low, high = low_ref[slot], high_ref[slot]
    rows_dev = q_ref.shape[3]
    tiles_dev = dkv_ref.shape[4] // key_tile
    q_low = jnp.concatenate([q_ref[i, 0] for i in range(HEAD_GROUPS)], axis=1)
    q_low = q_low * jnp.asarray(score_scale, half)
    g_low = jnp.concatenate([g_ref[i, 0] for i in range(HEAD_GROUPS)], axis=1)
    rows = q_low.shape[1]
    acc_ref[...] = jnp.zeros_like(acc_ref)
    product = g_low.astype(f32) * mix_ref[0]
    delta = [jnp.sum(product[head_feats(h)], axis=0, keepdims=True) for h in range(GROUP_HEADS)]
    lse = [lse_ref[0, h : h + 1, :] for h in range(GROUP_HEADS)]

    def step(tile, carry):
        start = pl.multiple_of(tile * key_tile, key_tile)
        owner = tile // tiles_dev
        turn, group = (owner - member + spread) % spread, owner // spread
        inside = pl.multiple_of(tile % tiles_dev * key_tile, key_tile)
        key_pos = start + lax.broadcasted_iota(jnp.int32, (key_tile, rows), 0)
        counted = (key_pos >= low) & (key_pos < high)
        for head in range(GROUP_HEADS):
            feats = head_feats(head)
            k_low = kv_ref[0, feats, pl.ds(start, key_tile)]
            v_low = kv_ref[1, feats, pl.ds(start, key_tile)]
            scores = jnp.where(counted, dot_tn(k_low, q_low[feats]), masked_score)
            prob = jnp.exp(scores - lse[head])
            grad_prob = dot_tn(v_low, g_low[feats])
            grad_score = (prob * (grad_prob - delta[head])).astype(half)
            dkv_ref[turn, group, 1, feats, pl.ds(inside, key_tile)] += dot_nt(
                g_low[feats], prob.astype(half)
            ).astype(half)
            dkv_ref[turn, group, 0, feats, pl.ds(inside, key_tile)] += dot_nt(
                q_low[feats], grad_score
            ).astype(half)
            acc_ref[feats, :] += dot_nn(k_low, grad_score)
        return carry

    lax.fori_loop(*tiles_of(low, high), step, 0)
    dq_low = (acc_ref[...] * score_scale).astype(half)
    for i in range(HEAD_GROUPS):
        dq_ref[i, 0] = dq_low[:, i * rows_dev : (i + 1) * rows_dev]

    @pl.when(slot == pl.num_programs(0) - 1)
    def _():
        copies = [
            pltpu.make_async_copy(dkv_ref.at[turn], out, sems.at[turn])
            for turn, out in enumerate(dkv_outs)
        ]
        for copy in copies:
            copy.start()
        for copy in copies:
            copy.wait()


def cross_backward(low, high, places, queries, grad_mix, mix, lse, pieces, *after):
    groups, slots, feats, rows_dev = queries.shape
    rows = groups * rows_dev
    tokens = pieces[0].shape[2]
    row_block = pl.BlockSpec((groups, 1, feats, rows_dev), lambda s, *_: (0, s, 0, 0))
    grad_shape = (len(pieces) // groups, groups, 2, feats, tokens)
    return pl.pallas_call(
        cross_backward_kernel,
        grid_spec=pltpu.PrefetchScalarGridSpec(
            num_scalar_prefetch=3,
            grid=(slots,),
            in_specs=[
                row_block,
                row_block,
                pl.BlockSpec((1, feats, rows), lambda s, *_: (s, 0, 0)),
                pl.BlockSpec((1, GROUP_HEADS, rows), lambda s, *_: (s, 0, 0)),
            ]
            + [pl.BlockSpec(memory_space=pl.ANY)] * (len(pieces) + len(after)),
            out_specs=[row_block] + [pl.BlockSpec(memory_space=pl.ANY)] * grad_shape[0],
            scratch_shapes=[
                pltpu.VMEM(grad_shape, half),
                pltpu.VMEM((feats, rows), f32),
                pltpu.VMEM((2, feats, tokens * len(pieces)), half),
                pltpu.SemaphoreType.DMA((len(pieces),)),
            ],
        ),
        out_shape=[
            jax.ShapeDtypeStruct(queries.shape, half),
        ]
        + [jax.ShapeDtypeStruct(grad_shape[1:], half)] * grad_shape[0],
        compiler_params=pltpu.CompilerParams(vmem_limit_bytes=vmem_bytes),
        name="cross_backward",
    )(low, high, places, queries, grad_mix, mix, lse, *pieces, *after)


middle_rows = 256


def middle_kernel(
    n_doc,
    n_seq,
    att_ref,
    norm_ref,
    out_grad_ref,
    vec_ref,
    bias_ref,
    *rest,
):
    weights = rest[:-17]
    out_ref, resid_ref, send_ref, packed_ref, sums_ref, bias_grad_ref = rest[-17:-11]
    att_all, w_cross, w_in, w_out, norm_low, active = rest[-11:-5]
    slope, low_three, hidden_grad, low_two, sems = rest[-5:]
    slots, rows_dev = att_ref.shape[1], att_ref.shape[3]
    rows_total = slots * rows_dev
    rows = min(middle_rows, rows_total)
    ff = w_out.shape[0]
    chunk = ff // n_doc
    copies = []

    def copy_block(block, block_col, target, row, col):
        rows = pl.ds(block * block_rows, block_rows)
        copies.append(
            pltpu.make_async_copy(
                w_ref.at[rows, pl.ds(block_col * D, D)],
                target.at[pl.ds(row, block_rows), pl.ds(col, D)],
                sems.at[len(copies)],
            )
        )

    blocks = n_doc * n_seq
    block_rows = ff // blocks
    if len(weights) == 1:
        (w_ref,) = weights
        for band in range(blocks // 4):
            row = band * block_rows
            copy_block(4 * band, 1, w_cross, row, 0)
            for at, (block_col, block) in enumerate([(2, 0), (1, 1), (2, 1), (1, 2)]):
                copy_block(4 * band + block, block_col, w_in, row, at * D)
        for block in range(blocks):
            copy_block(block, 0, w_out, block * block_rows, 0)
    else:
        for i, (weight, target) in enumerate(zip(weights, (w_cross, w_in, w_out))):
            copies.append(pltpu.make_async_copy(weight, target, sems.at[i]))
    for copy in copies:
        copy.start()
    for group in range(HEAD_GROUPS):
        for slot in range(slots):
            att_all[
                group * GROUP_FEATS : (group + 1) * GROUP_FEATS,
                slot * rows_dev : (slot + 1) * rows_dev,
            ] = att_ref[group, slot]
    sums_ref[...] = jnp.zeros_like(sums_ref)
    bias_grad_ref[...] = jnp.zeros_like(bias_grad_ref)
    for copy in copies:
        copy.wait()

    def row_block(block, carry):
        where = pl.ds(pl.multiple_of(block * rows, rows), rows)
        gain_two, shift_two = vec_ref[0:1, :], vec_ref[1:2, :]
        gain_three, shift_three = vec_ref[2:3, :], vec_ref[3:4, :]
        branch = dot_tn(att_all[:, where], w_cross[...]) + vec_ref[4:5, :]
        unit_two, scale_two = normalize(norm_ref[where, :] + branch)
        norm_two = unit_two * gain_two + shift_two
        norm_two_low = norm_two.astype(half)
        norm_low[where, :] = norm_two_low
        branch = vec_ref[5:6, :]
        for z in range(n_doc):
            cols = slice(z * chunk, (z + 1) * chunk)
            hidden = dot_nn(norm_two_low, w_in[:, cols]) + bias_ref[:, cols]
            below = 0.5 + 0.5 * lax.erf(hidden * (0.5**0.5))
            density = jnp.exp(-0.5 * hidden * hidden) * 0.3989422804014327
            slope[:, cols] = below + hidden * density
            active_low = (hidden * below).astype(half)
            active[where, cols] = active_low
            branch = branch + dot_nn(active_low, w_out[cols, :])
        unit_three, scale_three = normalize(norm_two + branch)
        out_ref[where, :] = (unit_three * gain_three + shift_three).astype(half)
        incoming = out_grad_ref[where, :].astype(f32)
        sums_ref[2:3, :] += row_sum(incoming * unit_three)
        sums_ref[3:4, :] += row_sum(incoming)
        grad_three = norm_backward(incoming, gain_three, unit_three, scale_three)
        grad_low = grad_three.astype(half)
        low_three[where, :] = grad_low
        sums_ref[5:6, :] += row_sum(grad_low.astype(f32))
        incoming = grad_three
        for z in range(n_doc):
            cols = slice(z * chunk, (z + 1) * chunk)
            hidden_low = (dot_nt(grad_low, w_out[cols, :]) * slope[:, cols]).astype(half)
            hidden_grad[where, cols] = hidden_low
            bias_grad_ref[:, cols] += row_sum(hidden_low.astype(f32))
            incoming = incoming + dot_nt(hidden_low, w_in[:, cols])
        sums_ref[0:1, :] += row_sum(incoming * unit_two)
        sums_ref[1:2, :] += row_sum(incoming)
        grad_two = norm_backward(incoming, gain_two, unit_two, scale_two)
        resid_ref[where, :] = grad_two
        grad_low = grad_two.astype(half)
        low_two[where, :] = grad_low
        sums_ref[4:5, :] += row_sum(grad_low.astype(f32))
        return carry

    lax.fori_loop(0, rows_total // rows, row_block, 0)

    grad_att = dot_nt(w_cross[...], low_two[...]).astype(half)
    for group in range(HEAD_GROUPS):
        for slot in range(slots):
            send_ref[group, slot] = grad_att[
                group * GROUP_FEATS : (group + 1) * GROUP_FEATS,
                slot * rows_dev : (slot + 1) * rows_dev,
            ]

    share = D // (n_doc * n_seq)
    stack_n = chunk // (share * n_seq)

    store_rows(packed_ref, n_doc, dot_nn(att_all[...], low_two[...]), slice(2 * ff, 2 * ff + D))
    for z in range(n_doc):
        cols = slice(z * chunk, (z + 1) * chunk)
        grad = dot_tn(norm_low[...], hidden_grad[:, cols])
        store_rows(packed_ref, n_doc, grad, slice(ff + z * chunk, ff + (z + 1) * chunk))
    for pair in range(n_doc // 2):
        grads = []
        for z in (2 * pair, 2 * pair + 1):
            cols = slice(z * chunk, (z + 1) * chunk)
            grads.append(dot_tn(active[:, cols], low_three[...]))
        for s in range(n_seq):
            for q in range(stack_n):
                first = (s * stack_n + q) * share
                mine = [grad[first : first + share] for grad in grads]
                packed_ref[
                    s, pair * 2 * share : (pair + 1) * 2 * share, q * D : (q + 1) * D
                ] = jnp.concatenate(mine, axis=0).astype(half)


def middle(n_doc, n_seq, att, norm_one, out_grad, vectors, bias, weights):
    groups, slots, feats, rows_dev = att.shape
    rows_total = slots * rows_dev
    ff = weights[-1].shape[0]
    share = D // (n_doc * n_seq)
    vmem = pl.BlockSpec(memory_space=pltpu.VMEM)
    hbm = pl.BlockSpec(memory_space=pl.ANY)
    return pl.pallas_call(
        partial(middle_kernel, n_doc, n_seq),
        in_specs=[vmem] * 5 + [hbm] * len(weights),
        out_specs=[vmem] * 6,
        out_shape=[
            jax.ShapeDtypeStruct((rows_total, D), half),
            jax.ShapeDtypeStruct((rows_total, D), f32),
            jax.ShapeDtypeStruct(att.shape, half),
            jax.ShapeDtypeStruct((n_seq, n_doc * share, 2 * ff + D), half),
            jax.ShapeDtypeStruct((8, D), f32),
            jax.ShapeDtypeStruct((1, ff), f32),
        ],
        scratch_shapes=[
            pltpu.VMEM((D, rows_total), half),
            pltpu.VMEM((D, D), half),
            pltpu.VMEM((D, ff), half),
            pltpu.VMEM((ff, D), half),
            pltpu.VMEM((rows_total, D), half),
            pltpu.VMEM((rows_total, ff), half),
            pltpu.VMEM((min(middle_rows, rows_total), ff), f32),
            pltpu.VMEM((rows_total, D), half),
            pltpu.VMEM((rows_total, ff), half),
            pltpu.VMEM((rows_total, D), half),
            pltpu.SemaphoreType.DMA((n_doc * n_seq * 9 // 4,)),
        ],
        compiler_params=pltpu.CompilerParams(vmem_limit_bytes=vmem_bytes),
        name="middle",
    )(att, norm_one, out_grad, vectors, bias, *weights)


def body(
    n_doc,
    n_seq,
    dec_input,
    memory,
    doc_lengths,
    doc_count,
    self_qkv,
    self_out,
    cross_q,
    cross_kv,
    cross_out,
    ffn_in,
    ffn_in_bias,
    ffn_out,
    norm_gains,
    biases,
    out_grad,
):
    seq_index = lax.axis_index("seq")
    doc_index = lax.axis_index("doc")
    slots_n, rows_dev = dec_input.shape[1:3]
    rows_total = slots_n * rows_dev
    mem_rows = memory.shape[1]
    spread = n_seq // HEAD_GROUPS
    head_group = seq_index // spread
    member = seq_index % spread
    member_slots = slots_n // spread
    dec_len = rows_dev * n_seq
    same_member = [[h * spread + m for h in range(HEAD_GROUPS)] for m in range(spread)]

    def swap_heads(blocks):
        return lax.all_to_all(blocks, "seq", 0, 0, axis_index_groups=same_member, tiled=True)

    def rotate_both(block, turn_h, turn_m):
        if turn_h == turn_m == 0:
            return block
        return lax.ppermute(
            block,
            "seq",
            [
                (
                    h * spread + m,
                    (h + turn_h) % HEAD_GROUPS * spread + (m + turn_m) % spread,
                )
                for h in range(HEAD_GROUPS)
                for m in range(spread)
            ],
        )

    def rotate_heads(block, turn):
        return rotate_both(block, turn, 0)

    def rotate_members(block, turn):
        return rotate_both(block, 0, turn)

    def rotate_doc(block, turn):
        return lax.ppermute(block, "doc", [(d, (d + turn) % n_doc) for d in range(n_doc)])

    def in_order(pieces, own, axis):
        count = len(pieces)
        shape = pieces[0].shape
        whole = jnp.zeros(shape[:axis] + (count,) + shape[axis:], pieces[0].dtype)
        for turn, piece in enumerate(pieces):
            whole = lax.dynamic_update_index_in_dim(whole, piece, (own - turn) % count, axis)
        return whole

    def send_turns(blocks, axis, count, own, rotate):
        got = []
        for turn in range(count):
            block = lax.dynamic_index_in_dim(blocks, (own + turn) % count, axis, keepdims=False)
            got.append(rotate(block, turn) if turn else block)
        return got

    part = self_qkv.shape[0]
    width = 3 * GROUP_FEATS
    qkv_piece = jnp.concatenate(
        [
            lax.dynamic_slice_in_dim(
                self_qkv, block * D + head_group * GROUP_FEATS, GROUP_FEATS, 1
            )
            for block in range(3)
        ],
        axis=1,
    )
    small = jnp.concatenate([norm_gains, biases, ffn_in_bias.reshape(-1, part)], axis=0)
    small_rows = small.shape[0]
    first_width = width
    pad_rows = -(-small_rows * part // first_width)
    first_rows = -(-(part + pad_rows) // (8 * spread)) * 8 * spread
    pad_rows = first_rows - part
    small = jnp.pad(small.reshape(-1), (0, pad_rows * first_width - small_rows * part))
    first_piece = jnp.concatenate(
        [qkv_piece, small.reshape(pad_rows, width)], axis=0
    )
    first_piece = lax.dynamic_slice_in_dim(
        first_piece.astype(half), member * (first_rows // spread), first_rows // spread, 0
    )

    def join_members(mine):
        pieces = [mine] + [rotate_members(mine, turn) for turn in range(1, spread)]
        return in_order(pieces, member, 1).reshape(n_doc, -1, mine.shape[2])

    first_piece = jnp.broadcast_to(first_piece[None], (n_doc,) + first_piece.shape)
    first_gather = join_members(lax.all_to_all(first_piece, "doc", 0, 0, tiled=True))
    w_qkv_part = first_gather[:, :part].reshape(D, width)
    small = first_gather[:, part:].reshape(n_doc, -1)[:, : small_rows * part]
    small = small.reshape(n_doc, small_rows, part).astype(f32)
    gains_f = small[:, :3].transpose(1, 0, 2).reshape(3, D)
    biases_f = small[:, 3:13].transpose(1, 0, 2).reshape(10, D)
    b_ffn_in = small[:, 13:].reshape(1, -1)

    share = part // n_seq
    ff = ffn_in.shape[1]
    stack_n = ffn_out.shape[0] // part
    member_rows = part // spread

    def gather_halves(*weights):
        piece = [
            lax.dynamic_slice_in_dim(weight, member * member_rows, member_rows, 0).astype(half)
            for weight in weights
        ]
        return lax.all_gather(jnp.concatenate(piece, axis=1), "doc", axis=0)

    w_cross_kv = join_members(gather_halves(cross_kv)).reshape(D, 2 * D)
    pair_halves = gather_halves(self_out, cross_q)

    block_rows, block_cols = divmod(seq_index, 4)

    def column_block(weight, first):
        return lax.dynamic_slice(
            weight, (block_rows * member_rows, first), (member_rows, D)
        ).astype(half)

    def first_cols(*starts):
        return jnp.stack(starts)[block_cols]

    left = jnp.where(
        block_cols == 0,
        column_block(cross_out, 0),
        jnp.where(
            block_cols == 3,
            column_block(self_qkv, D),
            column_block(ffn_in, first_cols(0, D, 3 * D, 0)),
        ),
    )
    right = jnp.where(
        block_cols < 2,
        column_block(ffn_in, first_cols(0, 2 * D, 0, 0)),
        column_block(self_qkv, first_cols(0, 0, 0, 2 * D)),
    )
    down = lax.dynamic_slice_in_dim(ffn_out, seq_index * member_rows, member_rows, 0).astype(half)
    w_blocks = lax.all_gather(
        jnp.concatenate([down, left, right], axis=1), ("doc", "seq"), axis=0, tiled=True
    )
    by_block = w_blocks.reshape(n_doc, spread, 4, member_rows, 3 * D)

    def columns(*blocks):
        found = [by_block[:, :, c, :, third * D : (third + 1) * D] for c, third in blocks]
        return jnp.concatenate(found, axis=3).reshape(D, -1)

    late_weights = [w_blocks]
    if member_rows % 16:
        late_weights = [
            columns((0, 1)),
            columns((0, 2), (1, 1), (1, 2), (2, 1)),
            w_blocks[:, :D],
        ]

    mem_low = memory[0]
    kv_bias = jnp.concatenate([jnp.zeros((D,), f32), biases_f[4]])
    mem_kv = (dot_tt(w_cross_kv, mem_low) + kv_bias[:, None]).astype(half)
    mem_kv = mem_kv.reshape(2, HEAD_GROUPS, GROUP_FEATS, mem_rows)
    pieces = send_turns(mem_kv, 1, HEAD_GROUPS, head_group, rotate_heads)
    pieces = pieces + [
        rotate_members(piece, turn) for turn in range(1, spread) for piece in pieces
    ]

    x_low = dec_input[0].reshape(rows_total, D)
    places = jnp.stack(
        [
            (head_group - turn_h) % HEAD_GROUPS * spread + (member - turn_m) % spread
            for turn_m in range(spread)
            for turn_h in range(HEAD_GROUPS)
        ]
    ).astype(jnp.int32)
    x_pieces = [rotate_heads(dec_input[0], turn) if turn else dec_input[0] for turn in range(HEAD_GROUPS)]
    for turn in range(1, spread):
        first_slot = (member + turn) % spread * member_slots
        blocks = [
            lax.dynamic_slice_in_dim(piece, first_slot, member_slots, 0)
            for piece in x_pieces[:HEAD_GROUPS]
        ]
        x_pieces.append(rotate_members(jnp.stack(blocks), turn))
    group_places = ((head_group - jnp.arange(HEAD_GROUPS)) % HEAD_GROUPS).astype(jnp.int32)
    zero_part = jnp.zeros((GROUP_FEATS,), f32)
    b_query = lax.dynamic_slice_in_dim(biases_f[0], head_group * GROUP_FEATS, GROUP_FEATS)
    b_value = lax.dynamic_slice_in_dim(biases_f[1], head_group * GROUP_FEATS, GROUP_FEATS)
    b_proj = jnp.concatenate([b_query, zero_part, b_value])[None]
    proj, self_mix, self_att_send, self_lse = self_forward(
        places, w_qkv_part, b_proj, x_pieces, n_seq, pieces[0]
    )

    def from_heads(blocks):
        feats = blocks.shape[2]
        got = blocks.reshape(HEAD_GROUPS, slots_n, feats // GROUP_FEATS, GROUP_FEATS, rows_dev)
        return got.transpose(2, 0, 3, 1, 4).reshape(HEAD_GROUPS * feats, rows_total)

    self_att = lax.all_to_all(self_att_send, "seq", 0, 0, tiled=True)
    pair_halves = lax.optimization_barrier((pair_halves, self_att_send))[0]
    w_pair = join_members(pair_halves).reshape(D, 2 * D)
    first_vectors = jnp.stack([biases_f[2], gains_f[0], biases_f[7], biases_f[3]])
    first_vectors = jnp.pad(first_vectors, ((0, 4), (0, 0)))
    norm_one, unit_one, scale_one, query_send = enter(
        self_att, x_low, first_vectors, w_pair, slots_n
    )

    lengths = doc_lengths[0]
    live_len = jnp.where(jnp.arange(slots_n) < doc_count[0], lengths, 0)
    key_high = jnp.minimum(jnp.cumsum(live_len), n_seq * mem_rows).astype(jnp.int32)
    key_low = jnp.concatenate([jnp.zeros((1,), jnp.int32), key_high[:-1]])
    query_part = swap_heads(query_send)
    cross_mix, cross_att_send, cross_lse = cross_forward(
        key_low, key_high, places, query_part, pieces
    )
    vectors = jnp.stack(
        [gains_f[1], biases_f[8], gains_f[2], biases_f[9], biases_f[5], biases_f[6]]
    )
    layer_out, grad_r2, grad_mix_send, late_packed, late_rows, grad_b_in = middle(
        n_doc,
        n_seq,
        swap_heads(cross_att_send),
        norm_one,
        out_grad[0].reshape(rows_total, D),
        jnp.pad(vectors, ((0, 2), (0, 0))),
        b_ffn_in,
        late_weights,
    )
    layer_out = layer_out.reshape(dec_input.shape)
    grad_g1, grad_c8, grad_g2, grad_c9, grad_b5, grad_b6 = late_rows[:6]

    def sum_over_seq(packed):
        packed = packed.reshape(D, packed.shape[2])
        return lax.psum_scatter(packed, "seq", scatter_dimension=0, tiled=True)

    def own_rows(packed):
        blocks = packed.reshape(n_doc, share, -1)
        pieces = send_turns(blocks, 0, n_doc, doc_index, rotate_doc)
        return sum(piece.astype(f32) for piece in pieces).astype(half)

    late_blocks = sum_over_seq(late_packed)
    grad_query_send, *grad_kv = cross_backward(
        key_low,
        key_high,
        places,
        query_part,
        swap_heads(grad_mix_send),
        cross_mix,
        cross_lse,
        pieces,
        late_packed,
    )
    grad_kv = [grad_kv[0]] + [
        rotate_members(grad_kv[turn], turn) for turn in range(1, spread)
    ]
    grad_kv_own = []
    for turn in range(HEAD_GROUPS):
        group = (head_group + turn) % HEAD_GROUPS
        total = sum(
            lax.dynamic_index_in_dim(piece, group, 0, keepdims=False).astype(f32)
            for piece in grad_kv
        ).astype(half)
        grad_kv_own.append(rotate_heads(total, turn) if turn else total)
    grad_r1, grad_att_send, pair_packed, first_rows_grad = leave(
        n_doc,
        swap_heads(grad_query_send),
        self_att,
        grad_r2,
        norm_one,
        unit_one,
        scale_one,
        first_vectors,
        w_pair,
        grad_kv_own[0],
    )
    pair_over_seq = sum_over_seq(pair_packed)
    grad_self_part = lax.all_to_all(grad_att_send, "seq", 0, 0, tiled=True)
    late_own = own_rows(lax.optimization_barrier((late_blocks, grad_r1))[0])
    mem_packed, grad_mem_kv = memory_backward(
        n_doc,
        n_seq,
        group_places,
        mem_low,
        first_rows_grad,
        late_rows,
        grad_b_in.reshape(n_doc, -1, part).transpose(1, 0, 2).reshape(-1, D),
        grad_kv_own,
        grad_self_part,
        late_blocks,
    )
    grad_proj_send, grad_part, part_sums = self_backward(
        n_doc,
        places,
        proj,
        grad_self_part,
        self_mix,
        self_lse,
        x_pieces,
        mem_packed,
        late_own,
    )
    grad_proj_got = lax.all_to_all(grad_proj_send, "seq", 0, 0, tiled=True)

    bias_rows = jnp.zeros((2, D), f32)
    bias_rows = lax.dynamic_update_slice(
        bias_rows,
        jnp.stack([part_sums[0, :GROUP_FEATS], part_sums[0, 2 * GROUP_FEATS :]]),
        (0, head_group * GROUP_FEATS),
    )
    lanes = -(-part // small_cols) * small_cols
    bias_rows = jnp.pad(bias_rows.reshape(2, n_doc, part), ((0, 0), (0, 0), (0, lanes - part)))
    bias_rows = bias_rows.transpose(1, 0, 2).reshape(n_doc, -1, small_cols)
    bias_used = bias_rows.shape[1]
    bias_rows = jnp.pad(bias_rows, ((0, 0), (0, share - bias_used), (0, 0)))
    bias_rows = bias_rows.reshape(1, n_doc * share, small_cols).astype(half)
    bias_rows = jnp.pad(bias_rows, ((0, spread - 1), (0, 0), (0, 0)))
    grad_part = jnp.concatenate([grad_part, bias_rows], axis=2)
    grad_part = send_turns(grad_part, 0, spread, member, rotate_members)
    grad_part = sum(piece.astype(f32) for piece in grad_part).astype(half)

    pair_own = own_rows(pair_over_seq)
    grads = jnp.concatenate([sum_over_seq(mem_packed), grad_part], axis=1)
    grads, grad_proj_got = lax.optimization_barrier((grads, grad_proj_got))
    (
        grad_w_qkv,
        grad_w_self_out,
        grad_w_cross_q,
        grad_w_cross_kv,
        small_grad,
        bias_sums,
        grad_w_down,
        grad_w_in,
        grad_w_cross_out,
    ) = finish(
        n_seq,
        stack_n,
        lax.all_gather(
            jnp.concatenate([pair_own, own_rows(grads), late_own], axis=1), "seq", axis=0, tiled=True
        ),
    )
    grad_proj = from_heads(grad_proj_got)
    memory_grad = dot_tt(grad_mem_kv, w_cross_kv)[None]
    w_qkv = columns((2, 2), (3, 1), (3, 2))
    input_grad = (grad_r1 + dot_tt(grad_proj, w_qkv)).reshape(dec_input.shape)
    grad_g0, grad_c7, grad_b2, grad_b3 = small_grad[:4]
    grad_g1, grad_c8, grad_g2, grad_c9, grad_b5, grad_b6 = small_grad[8:14]
    grad_b0, grad_b1 = bias_sums[:bias_used].reshape(2, lanes)[:, :part]
    grad_b4 = small_grad[16 + stack_n]
    return (
        layer_out,
        input_grad,
        memory_grad,
        grad_w_qkv,
        grad_w_self_out,
        grad_w_cross_q,
        grad_w_cross_kv,
        grad_w_cross_out,
        grad_w_in,
        small_grad[16 : 16 + stack_n].reshape(-1),
        grad_w_down,
        jnp.stack([grad_g0, grad_g1, grad_g2]),
        jnp.stack(
            [grad_b0, grad_b1, grad_b2, grad_b3, grad_b4, grad_b5, grad_b6]
            + [grad_c7, grad_c8, grad_c9]
        ),
    )


def solution(mesh):
    placed = (
        P("doc", None, "seq", None),
        P("doc", "seq", None),
        P("doc", None),
        P("doc"),
        P("doc", None),
        P("doc", None),
        P("doc", None),
        P("doc", None),
        P("doc", None),
        P("doc", None),
        P("doc"),
        P("doc", None),
        P(None, "doc"),
        P(None, "doc"),
        P("doc", None, "seq", None),
    )
    return jax.shard_map(
        partial(body, mesh.shape["doc"], mesh.shape["seq"]),
        mesh=mesh,
        in_specs=placed,
        out_specs=(
            P("doc", None, "seq", None),
            P("doc", None, "seq", None),
            P("doc", "seq", None),
            P("doc", None),
            P("doc", None),
            P("doc", None),
            P("doc", None),
            P("doc", None),
            P("doc", None),
            P("doc"),
            P("doc", None),
            P(None, "doc"),
            P(None, "doc"),
        ),
        check_vma=False,
    )
```

time: 1060 us -> 594 us (0.56)
  waiting for transfers between devices: 455 us -> 217 us
  blocking collectives: 125 us -> 11.7 us
  local copies, waits for them, and re-layouts: 156 us -> 44.3 us
  matrix products: 94 us -> 10.7 us
  Pallas kernels: 125 us -> 199 us
  other arithmetic: 43.2 us -> 22.1 us
  starting transfers between devices: 37.1 us -> 56.3 us
    all_gather x10 -> x4, waiting for transfers between devices: 211 us -> 26.6 us  [the longest x1 26.6 us: body(): lax.all_gather(jnp.concatenate([pair_own, own_rows(grads), late_own], axi...]
    reduce_scatter x13 -> x3, waiting for transfers between devices: 116 us -> 14 us  [sum_over_seq(): return lax.psum_scatter(packed, 'seq', scatter_dimension=0, tiled=True)]
    all_gather x6 -> x0, blocking collectives: 86.1 us -> none  [the longest x4 49.2 us: reduce_weight(): return lax.all_gather(over_doc, 'seq', axis=0, tiled=True).astype(f32)]
    dot_general x21 -> x3, matrix products: 94 us -> 10.7 us  [contract(): lax.dot_general(left_op, right_op, (((left_dim,), (right_dim,)), ((), ())...]
    pallas_call x2 -> x7, Pallas kernels: 27.2 us -> 98.1 us  [the longest x1 31.4 us: middle(): pl.pallas_call(partial(middle_kernel, n_doc, n_seq), in_specs=[vmem] * 5...]
    psum x1 -> x0, blocking collectives: 39.1 us -> none  [body(): small_grad = lax.psum(small_grad, ('doc', 'seq'))]
    ppermute x9 -> x28, waiting for transfers between devices: 80.8 us -> 110 us  [the longest x19 97.1 us: rotate_both(): lax.ppermute(block, 'seq', [(h * spread + m, (h + turn_h) % HEAD_GROUPS *...]
    convert_element_type x12 -> x3, local copies, waits for them, and re-layouts: 26.3 us -> 3.07 us  [the longest x2 3.04 us: gather_halves(): lax.dynamic_slice_in_dim(weight, member * member_rows, member_rows, 0)]
  transfers between devices with their start and end apart: 39 -> 42, of which waited for: 25 -> 18; matrix products, arithmetic and copies ran while one was open for 25% -> 11% of each run, Pallas kernels for 12% -> 28%
where the time goes in v2:
time: 594 us; the launch traced here: 583 us
  waiting for transfers between devices  217 us (37%)
  Pallas kernels  199 us (34%)
  starting transfers between devices  56.3 us (9%)
  local copies, waits for them, and re-layouts  44.3 us (7%)
  other arithmetic  22.1 us (4%)
  between operations  21.9 us (4%)
  blocking collectives  11.7 us (2%)
  matrix products  10.7 us (2%)
    ppermute x19, waiting for transfers between devices, rotate_both(): lax.ppermute(block, 'seq', [(h * spread + m, (h + turn_h) % HEAD_GROUPS *...  97.1 us
    pallas_call x1, Pallas kernels, cross_backward(): pl.pallas_call(cross_backward_kernel, grid_spec=pltpu.PrefetchScalarGridS...  54 us
    pallas_call x1, Pallas kernels, cross_forward(): pl.pallas_call(cross_forward_kernel, grid_spec=pltpu.PrefetchScalarGridSp...  46.6 us
    all_to_all x3, waiting for transfers between devices, swap_heads(): lax.all_to_all(blocks, 'seq', 0, 0, axis_index_groups=same_member, tiled=...  32.7 us
    pallas_call x1, Pallas kernels, middle(): pl.pallas_call(partial(middle_kernel, n_doc, n_seq), in_specs=[vmem] * 5...  31.4 us
    all_gather x1, waiting for transfers between devices, body(): lax.all_gather(jnp.concatenate([pair_own, own_rows(grads), late_own], axi...  26.6 us
    pallas_call x1, Pallas kernels, self_backward(): pl.pallas_call(partial(self_backward_kernel, n_doc), grid_spec=pltpu.Pref...  20.4 us
    all_to_all x1, waiting for transfers between devices, body(): lax.all_to_all(first_piece, 'doc', 0, 0, tiled=True)  20.3 us
  transfers between devices with their start and end apart: 42, of which 18 were waited for; matrix products, arithmetic and copies ran while one was open for 11% of the time, Pallas kernels for 28%

profile of v2, /device:TPU:0, one launch (start us, length us, event | category | flops | bytes accessed | tf_op | source)
XLA Modules:
  0.0 583.0 jit_solution(2731114194301359878)
XLA Ops:
  23.9 6.4 %all-to-all-start = ((bf16[4,104,576]{2,1,0:T(8,128)(2,1)}), bf16[4,104,576]{2,1,0:T(8,128)(2,1)}, u32[]{:S(2)}, u32[]{:S(2)}) async-start(bf16[4,104,576]{2,1,0:T(8,128)(2,1)} %broadcast_in_dim.49), calls=%async_computation | async-start | bytes 1064960 | tf_op jit(solution)/shard_map/all_to_all | solution.py:1032
  34.4 20.3 %all-to-all-done = bf16[4,104,576]{2,1,0:T(8,128)(2,1)} async-done(((bf16[4,104,576]{2,1,0:T(8,128)(2,1)}), bf16[4,104,576]{2,1,0:T(8,128)(2,1)}, u32[]{:S(2)}, u32[]{:S(2)}) %all-to-all-start) | async-done | bytes 479264 | tf_op jit(solution)/shard_map/all_to_all | solution.py:1032
  56.0 12.2 %collective-permute-done.2.rest_2_ = bf16[4,128,768]{2,1,0:T(8,128)(2,1)S(1)} collective-permute-done((bf16[4,128,768]{2,1,0:T(8,128)(2,1)S(1)}, bf16[4,128,768]{2,1,0:T(8,128)(2,1)S(1)}, u32[]{:S(2)}, u32[]{:S(2)}) %collective-permute-start.2) | collective-permute-done | bytes 786464 | tf_op jit(solution)/shard_map/ppermute | solution.py:965
  83.5 18.1 %self_forward.1 = (bf16[576,2048]{1,0:T(8,128)(2,1)}, f32[2,192,1024]{2,1,0:T(8,128)}, bf16[8,2,192,128]{3,2,1,0:T(8,128)(2,1)}, f32[2,3,1024]{2,1,0:T(4,128)}) custom-call(s32[8]{0:T(128)} %stack.64.place_ref, bf16[768,576]{1,0:T(8,128)(2,1)} %bitcast.164, f32[1,576]{1,0:T(1,128)} %broadcast_in_dim.53.bias_ref, bf16[4,128,768]{2,1,0:T(8,128)(2,1)} %bitcast.153, ...), custom_call_target="tpu_custom_call" | custom-call | tf_op jit(solution)/shard_map/self_forward/pallas_call | solution.py:159
  106.1 4.7 all-to-all-start.1
  112.4 16.1 %collective-permute-done.9.rest_3_ = bf16[2,192,1024]{2,1,0:T(8,128)(2,1)} collective-permute-done((bf16[2,192,1024]{2,1,0:T(8,128)(2,1)}, bf16[2,192,1024]{2,1,0:T(8,128)(2,1)}, u32[]{:S(2)}, u32[]{:S(2)}) %collective-permute-start.9) | collective-permute-done | bytes 786464 | tf_op jit(solution)/shard_map/ppermute | solution.py:965
  128.5 4.5 collective-permute-done.8.rest_2_
  132.9 19.7 %collective-permute-done.7.rest_1_ = bf16[2,192,1024]{2,1,0:T(8,128)(2,1)} collective-permute-done((bf16[2,192,1024]{2,1,0:T(8,128)(2,1)}, bf16[2,192,1024]{2,1,0:T(8,128)(2,1)}, u32[]{:S(2)}, u32[]{:S(2)}) %collective-permute-start.7) | collective-permute-done | bytes 786464 | tf_op jit(solution)/shard_map/ppermute | solution.py:965
  154.1 6.6 %all-to-all-done.1.att_ref = bf16[8,2,192,128]{3,2,1,0:T(8,128)(2,1)} async-done(((bf16[8,2,192,128]{3,2,1,0:T(8,128)(2,1)}), bf16[8,2,192,128]{3,2,1,0:T(8,128)(2,1)}, u32[]{:S(2)}, u32[]{:S(2)}) %all-to-all-start.1) | async-done | bytes 786464 | tf_op jit(solution)/shard_map/all_to_all | solution.py:1136
  160.6 6.1 %enter.1 = (f32[512,768]{1,0:T(8,128)}, f32[512,768]{1,0:T(8,128)}, f32[512,128]{1,0:T(8,128)}, bf16[4,4,192,128]{3,2,1,0:T(8,128)(2,1)}) custom-call(bf16[8,2,192,128]{3,2,1,0:T(8,128)(2,1)} %all-to-all-done.1.att_ref, bf16[512,768]{1,0:T(8,128)(2,1)} %bitcast.154, f32[8,768]{1,0:T(8,128)} %select_maximum_fusion.vec_ref, bf16[768,1536]{1,0:T(8,128)(2,1)} %bitcast.150), custom_call_target="tpu_custom_call" | custom-call | tf_op jit(solution)/shard_map/enter/pallas_call | solution.py:336
  166.7 4.2 all-to-all-start.2
  172.2 18.1 %all-to-all-done.2.q_ref = bf16[4,4,192,128]{3,2,1,0:T(8,128)(2,1)S(1)} async-done(((bf16[4,4,192,128]{3,2,1,0:T(8,128)(2,1)}), bf16[4,4,192,128]{3,2,1,0:T(8,128)(2,1)S(1)}, u32[]{:S(2)}, u32[]{:S(2)}) %all-to-all-start.2) | async-done | bytes 786464 | tf_op jit(solution)/shard_map/all_to_all | solution.py:960
  191.2 46.6 %cross_forward.1 = (f32[4,192,512]{2,1,0:T(8,128)}, bf16[4,4,192,128]{3,2,1,0:T(8,128)(2,1)}, f32[4,3,512]{2,1,0:T(4,128)}) custom-call(s32[4]{0:T(128)} %pad_add_fusion.low_ref, s32[4]{0:T(128)} %get-tuple-element.146.high_ref, s32[8]{0:T(128)} %stack.64.place_ref, bf16[4,4,192,128]{3,2,1,0:T(8,128)(2,1)} %copy-done.5, ...), custom_call_target="tpu_custom_call" | custom-call | tf_op jit(solution)/shard_map/cross_forward/pallas_call | solution.py:623
  244.1 5.3 all-to-all-done.3.att_ref
  250.3 31.4 %middle.1 = (bf16[512,768]{1,0:T(8,128)(2,1)}, f32[512,768]{1,0:T(8,128)}, bf16[4,4,192,128]{3,2,1,0:T(8,128)(2,1)}, bf16[8,96,6912]{2,1,0:T(8,128)(2,1)}, f32[8,768]{1,0:T(8,128)}, /*index=5*/f32[1,3072]{1,0:T(1,128)}) custom-call(bf16[4,4,192,128]{3,2,1,0:T(8,128)(2,1)} %copy-done.11, f32[512,768]{1,0:T(8,128)} %get-tuple-element.59.norm_ref, ...), custom_call_target="tpu_custom_call" | custom-call | tf_op jit(solution)/shard_map/middle/pallas_call | solution.py:898
  282.8 11.7 %all_to_all.40.g_ref = bf16[4,4,192,128]{3,2,1,0:T(8,128)(2,1)} all-to-all(bf16[4,4,192,128]{3,2,1,0:T(8,128)(2,1)S(1)} %copy-done.18), channel_id=1, replica_groups={{0,2,4,6},{1,3,5,7},{8,10,12,14},{9,11,13,15},{16,18,20,22},{17,19,21,2..., dimensions={0} | all-to-all | bytes 1572864 | tf_op jit(solution)/shard_map/all_to_all | solution.py:960
  294.5 54.0 %cross_backward.1 = (bf16[4,4,192,128]{3,2,1,0:T(8,128)(2,1)}, bf16[4,2,192,1024]{3,2,1,0:T(8,128)(2,1)}, bf16[4,2,192,1024]{3,2,1,0:T(8,128)(2,1)}) custom-call(s32[4]{0:T(128)} %pad_add_fusion.low_ref, s32[4]{0:T(128)} %get-tuple-element.146.high_ref, s32[8]{0:T(128)} %stack.64.place_ref, bf16[4,4,192,128]{3,2,1,0:T(8,128)(2,1)} %copy-done.5, ...), custom_call_target="tpu_custom_call" | custom-call | tf_op jit(solution)/shard_map/cross_backward/pallas_call | solution.py:725
  354.6 5.5 fusion.19
  360.1 9.3 %all-to-all-done.5.query_ref = bf16[4,4,192,128]{3,2,1,0:T(8,128)(2,1)S(1)} async-done(((bf16[4,4,192,128]{3,2,1,0:T(8,128)(2,1)}), bf16[4,4,192,128]{3,2,1,0:T(8,128)(2,1)S(1)}, u32[]{:S(2)}, u32[]{:S(2)}) %all-to-all-start.5) | async-done | bytes 786464 | tf_op jit(solution)/shard_map/all_to_all | solution.py:960
  370.2 8.4 %leave.1 = (f32[512,768]{1,0:T(8,128)}, bf16[8,2,192,128]{3,2,1,0:T(8,128)(2,1)}, bf16[8,96,1536]{2,1,0:T(8,128)(2,1)}, f32[8,768]{1,0:T(8,128)}) custom-call(bf16[4,4,192,128]{3,2,1,0:T(8,128)(2,1)} %copy-done.12, bf16[8,2,192,128]{3,2,1,0:T(8,128)(2,1)} %all-to-all-done.1.att_ref, f32[512,768]{1,0:T(8,128)} %get-tuple-element.66.resid_ref, ...), custom_call_target="tpu_custom_call" | custom-call | tf_op jit(solution)/shard_map/leave/pallas_call | solution.py:409
  392.4 25.3 %collective-permute-done.17.rest_3_ = bf16[2,192,1024]{2,1,0:T(8,128)(2,1)} collective-permute-done((bf16[2,192,1024]{2,1,0:T(8,128)(2,1)S(1)}, bf16[2,192,1024]{2,1,0:T(8,128)(2,1)}, u32[]{:S(2)}, u32[]{:S(2)}) %collective-permute-start.17) | collective-permute-done | bytes 786464 | tf_op jit(solution)/shard_map/ppermute | solution.py:965
  422.6 14.9 %collective-permute-done.15.rest_1_ = bf16[2,192,1024]{2,1,0:T(8,128)(2,1)} collective-permute-done((bf16[2,192,1024]{2,1,0:T(8,128)(2,1)S(1)}, bf16[2,192,1024]{2,1,0:T(8,128)(2,1)}, u32[]{:S(2)}, u32[]{:S(2)}) %collective-permute-start.15) | collective-permute-done | bytes 786464 | tf_op jit(solution)/shard_map/ppermute | solution.py:965
  437.5 7.4 %memory_backward.1 = (bf16[8,96,1664]{2,1,0:T(8,128)(2,1)}, bf16[1536,1024]{1,0:T(8,128)(2,1)}) custom-call(s32[4]{0:T(128)} %and_select_fusion.place_ref, bf16[1024,768]{1,0:T(8,128)(2,1)} %bitcast.172, f32[8,768]{1,0:T(8,128)} %get-tuple-element.72.rows_a_ref, f32[8,768]{1,0:T(8,128)} %get-tuple-element.73.rows_b_ref, f32[4,768]{1,0:T(4,128)} %reshape.224.rows_c_ref, ...), custom_call_target="tpu_custom_call" | custom-call | tf_op jit(solution)/shard_map/memory_backward/pallas_call | solution.py:455
  447.0 20.4 %self_backward.1 = (bf16[8,2,576,128]{3,2,1,0:T(8,128)(2,1)}, bf16[2,96,2304]{2,1,0:T(8,128)(2,1)}, f32[8,576]{1,0:T(8,128)}) custom-call(s32[8]{0:T(128)} %stack.64.place_ref, bf16[576,2048]{1,0:T(8,128)(2,1)} %get-tuple-element.77.proj_ref, bf16[8,2,192,128]{3,2,1,0:T(8,128)(2,1)} %copy-done.6, f32[2,192,1024]{2,1,0:T(8,128)} %get-tuple-element.78.mix_ref, ...), custom_call_target="tpu_custom_call" | custom-call | tf_op jit(solution)/shard_map/self_backward/pallas_call | solution.py:262
  468.5 3.6 all-to-all-start.7
  482.5 14.0 %reduce-scatter.6.cloned.1.call-done = bf16[96,1664]{1,0:T(8,128)(2,1)} async-done(((bf16[768,1664]{1,0:T(8,128)(2,1)}), bf16[96,1664]{1,0:T(8,128)(2,1)}) %reduce-scatter.6.cloned.1.call-update) | async-done | bytes 319504 | tf_op jit(solution)/shard_map/reduce_scatter | solution.py:1171
  497.7 7.2 %all-to-all-done.7 = bf16[8,2,576,128]{3,2,1,0:T(8,128)(2,1)S(1)} async-done(((bf16[8,2,576,128]{3,2,1,0:T(8,128)(2,1)}), bf16[8,2,576,128]{3,2,1,0:T(8,128)(2,1)S(1)}, u32[]{:S(2)}, u32[]{:S(2)}) %all-to-all-start.7) | async-done | bytes 2359328 | tf_op jit(solution)/shard_map/all_to_all | solution.py:1239
  510.6 4.2 collective-permute-done.25
  514.8 8.5 %collective-permute-done.26 = bf16[24,4096]{1,0:T(8,128)(2,1)S(1)} collective-permute-done((bf16[24,4096]{1,0:T(8,128)(2,1)S(1)}, bf16[24,4096]{1,0:T(8,128)(2,1)S(1)}, u32[]{:S(2)}, u32[]{:S(2)}) %collective-permute-start.26) | collective-permute-done | bytes 196640 | tf_op jit(solution)/shard_map/ppermute | solution.py:985
  528.0 4.3 convolution_bitcast_fusion
  537.4 26.6 %all-gather.9.cloned.1.call-done.in_ref = bf16[192,12544]{1,0:T(8,128)(2,1)} async-done(((bf16[24,12544]{1,0:T(8,128)(2,1)}), bf16[192,12544]{1,0:T(8,128)(2,1)}) %all-gather.9.cloned.1.call-update) | async-done | bytes 4816912 | tf_op jit(solution)/shard_map/all_gather | solution.py:1274
  564.0 6.3 %finish.1 = (f32[192,2304]{1,0:T(8,128)}, f32[192,768]{1,0:T(8,128)}, f32[192,768]{1,0:T(8,128)}, f32[192,1536]{1,0:T(8,128)}, f32[128,192]{1,0:T(8,128)}, /*ind...) custom-call(bf16[192,12544]{1,0:T(8,128)(2,1)} %all-gather.9.cloned.1.call-done.in_ref), custom_call_target="tpu_custom_call" | custom-call | tf_op jit(solution)/shard_map/finish/pallas_call | solution.py:526
  (243 shorter events, 109.3 us)
Async XLA Ops:
  7.2 64.6 %all-gather.11.cloned.1.call-start = ((), (), s32[]{:S(2)}) async-start(), calls=%async_computation.16 | async-start | bytes 1474560 | tf_op jit(solution)/shard_map/all_gather | solution.py:1050
  9.3 92.4 %all-gather.13.cloned.1.call-start = ((), (), s32[]{:S(2)}) async-start(), calls=%async_computation.17 | async-start | bytes 1474560 | tf_op jit(solution)/shard_map/all_gather | solution.py:1050
  11.2 238.2 %all-gather.7.cloned.1.call-start = ((), (), s32[]{:S(2)}) async-start(), calls=%async_computation.11 | async-start | bytes 14598144 | tf_op jit(solution)/shard_map/all_gather | solution.py:1080
  23.9 30.8 %all-to-all-start = ((bf16[4,104,576]{2,1,0:T(8,128)(2,1)}), bf16[4,104,576]{2,1,0:T(8,128)(2,1)}, u32[]{:S(2)}, u32[]{:S(2)}) async-start(bf16[4,104,576]{2,1,0:T(8,128)(2,1)} %broadcast_in_dim.49), calls=%async_computation | async-start | bytes 1064960 | tf_op jit(solution)/shard_map/all_to_all | solution.py:1032
  30.3 25.7 %collective-permute-start.3 = (bf16[4,128,768]{2,1,0:T(8,128)(2,1)S(1)}, bf16[4,128,768]{2,1,0:T(8,128)(2,1)S(1)}, u32[]{:S(2)}, u32[]{:S(2)}) collective-permute-start(bf16[4,128,768]{2,1,0:T(8,128)(2,1)S(1)} %bitcast.156), channel_id=1, source_target_pairs={{0,6},{1,7},{2,0},{3,1},{4,2},{5,3},{6,4},{7,5},{8,14},{9,15},{10,... | collective-permute-start | bytes 2359304 | tf_op jit(solution)/shard_map/ppermute | solution.py:965
  32.7 35.5 %collective-permute-start.2 = (bf16[4,128,768]{2,1,0:T(8,128)(2,1)S(1)}, bf16[4,128,768]{2,1,0:T(8,128)(2,1)S(1)}, u32[]{:S(2)}, u32[]{:S(2)}) collective-permute-start(bf16[4,128,768]{2,1,0:T(8,128)(2,1)S(1)} %bitcast.157), channel_id=1, source_target_pairs={{0,4},{1,5},{2,6},{3,7},{4,0},{5,1},{6,2},{7,3},{8,12},{9,13},{10,... | collective-permute-start | bytes 2359304 | tf_op jit(solution)/shard_map/ppermute | solution.py:965
  33.2 35.0 %collective-permute-start.1 = (bf16[4,128,768]{2,1,0:T(8,128)(2,1)S(1)}, bf16[4,128,768]{2,1,0:T(8,128)(2,1)S(1)}, u32[]{:S(2)}, u32[]{:S(2)}) collective-permute-start(bf16[4,128,768]{2,1,0:T(8,128)(2,1)S(1)} %bitcast.158), channel_id=1, source_target_pairs={{0,2},{1,3},{2,4},{3,5},{4,6},{5,7},{6,0},{7,1},{8,10},{9,11},{10,... | collective-permute-start | bytes 2359304 | tf_op jit(solution)/shard_map/ppermute | solution.py:965
  101.7 51.0 %collective-permute-start.6 = (bf16[4,96,1536]{2,1,0:T(8,128)(2,1)}, bf16[4,96,1536]{2,1,0:T(8,128)(2,1)}, u32[]{:S(2)}, u32[]{:S(2)}) collective-permute-start(bf16[4,96,1536]{2,1,0:T(8,128)(2,1)} %bitcast.176), channel_id=1, source_target_pairs={{0,1},{1,0},{2,3},{3,2},{4,5},{5,4},{6,7},{7,6},{8,9},{9,8},{10,11... | collective-permute-start | bytes 3538952 | tf_op jit(solution)/shard_map/ppermute | solution.py:965
  102.5 25.9 %collective-permute-start.9 = (bf16[2,192,1024]{2,1,0:T(8,128)(2,1)}, bf16[2,192,1024]{2,1,0:T(8,128)(2,1)}, u32[]{:S(2)}, u32[]{:S(2)}) collective-permute-start(bf16[2,192,1024]{2,1,0:T(8,128)(2,1)} %get-tuple-element.119), channel_id=1, source_target_pairs={{0,6},{1,7},{2,0},{3,1},{4,2},{5,3},{6,4},{7,5},{8,14},{9,15},{10,... | collective-permute-start | bytes 2359304 | tf_op jit(solution)/shard_map/ppermute | solution.py:965
  103.1 29.8 %collective-permute-start.8 = (bf16[2,192,1024]{2,1,0:T(8,128)(2,1)}, bf16[2,192,1024]{2,1,0:T(8,128)(2,1)}, u32[]{:S(2)}, u32[]{:S(2)}) collective-permute-start(bf16[2,192,1024]{2,1,0:T(8,128)(2,1)} %get-tuple-element.120), channel_id=1, source_target_pairs={{0,4},{1,5},{2,6},{3,7},{4,0},{5,1},{6,2},{7,3},{8,12},{9,13},{10,... | collective-permute-start | bytes 2359304 | tf_op jit(solution)/shard_map/ppermute | solution.py:965
  103.6 49.1 %collective-permute-start.7 = (bf16[2,192,1024]{2,1,0:T(8,128)(2,1)}, bf16[2,192,1024]{2,1,0:T(8,128)(2,1)}, u32[]{:S(2)}, u32[]{:S(2)}) collective-permute-start(bf16[2,192,1024]{2,1,0:T(8,128)(2,1)} %get-tuple-element.121), channel_id=1, source_target_pairs={{0,2},{1,3},{2,4},{3,5},{4,6},{5,7},{6,0},{7,1},{8,10},{9,11},{10,... | collective-permute-start | bytes 2359304 | tf_op jit(solution)/shard_map/ppermute | solution.py:965
  106.1 66.1 %collective-permute-start.10 = (bf16[2,192,1024]{2,1,0:T(8,128)(2,1)S(1)}, bf16[2,192,1024]{2,1,0:T(8,128)(2,1)}, u32[]{:S(2)}, u32[]{:S(2)}) collective-permute-start(bf16[2,192,1024]{2,1,0:T(8,128)(2,1)S(1)} %copy-done.3), channel_id=1, source_target_pairs={{0,1},{1,0},{2,3},{3,2},{4,5},{5,4},{6,7},{7,6},{8,9},{9,8},{10,11... | collective-permute-start | bytes 2359304 | tf_op jit(solution)/shard_map/ppermute | solution.py:965
  106.1 54.5 %all-to-all-start.1 = ((bf16[8,2,192,128]{3,2,1,0:T(8,128)(2,1)}), bf16[8,2,192,128]{3,2,1,0:T(8,128)(2,1)}, u32[]{:S(2)}, u32[]{:S(2)}) async-start(bf16[8,2,192,128]{3,2,1,0:T(8,128)(2,1)} %get-tuple-element.55), calls=%async_computation.1 | async-start | bytes 1572864 | tf_op jit(solution)/shard_map/all_to_all | solution.py:1136
  128.5 43.8 %collective-permute-start.13 = (bf16[2,192,1024]{2,1,0:T(8,128)(2,1)}, bf16[2,192,1024]{2,1,0:T(8,128)(2,1)}, u32[]{:S(2)}, u32[]{:S(2)}) collective-permute-start(bf16[2,192,1024]{2,1,0:T(8,128)(2,1)} %collective-permute-done.9.rest_3_), channel_id=1, source_target_pairs={{0,1},{1,0},{2,3},{3,2},{4,5},{5,4},{6,7},{7,6},{8,9},{9,8},{10,11... | collective-permute-start | bytes 2359304 | tf_op jit(solution)/shard_map/ppermute | solution.py:965
  132.9 39.3 %collective-permute-start.12 = (bf16[2,192,1024]{2,1,0:T(8,128)(2,1)}, bf16[2,192,1024]{2,1,0:T(8,128)(2,1)}, u32[]{:S(2)}, u32[]{:S(2)}) collective-permute-start(bf16[2,192,1024]{2,1,0:T(8,128)(2,1)} %collective-permute-done.8.rest_2_), channel_id=1, source_target_pairs={{0,1},{1,0},{2,3},{3,2},{4,5},{5,4},{6,7},{7,6},{8,9},{9,8},{10,11... | collective-permute-start | bytes 2359304 | tf_op jit(solution)/shard_map/ppermute | solution.py:965
  166.7 23.6 %all-to-all-start.2 = ((bf16[4,4,192,128]{3,2,1,0:T(8,128)(2,1)}), bf16[4,4,192,128]{3,2,1,0:T(8,128)(2,1)S(1)}, u32[]{:S(2)}, u32[]{:S(2)}) async-start(bf16[4,4,192,128]{3,2,1,0:T(8,128)(2,1)} %get-tuple-element.57), calls=%async_computation.2 | async-start | bytes 1572864 | tf_op jit(solution)/shard_map/all_to_all | solution.py:960
  241.3 144.9 %reduce-scatter.4.cloned.1.call-start = ((), (), s32[]{:S(2)}) async-start(), calls=%async_computation.12 | async-start | bytes 11943936 | tf_op jit(solution)/shard_map/reduce_scatter | solution.py:1171
  348.6 20.8 %all-to-all-start.5 = ((bf16[4,4,192,128]{3,2,1,0:T(8,128)(2,1)}), bf16[4,4,192,128]{3,2,1,0:T(8,128)(2,1)S(1)}, u32[]{:S(2)}, u32[]{:S(2)}) async-start(bf16[4,4,192,128]{3,2,1,0:T(8,128)(2,1)} %get-tuple-element.65), calls=%async_computation.5 | async-start | bytes 1572864 | tf_op jit(solution)/shard_map/all_to_all | solution.py:960
  352.1 122.6 %reduce-scatter.8.cloned.1.call-start = ((), (), s32[]{:S(2)}) async-start(), calls=%async_computation.14 | async-start | bytes 2654208 | tf_op jit(solution)/shard_map/reduce_scatter | solution.py:1171
  378.7 43.9 %all-to-all-start.6 = ((bf16[8,2,192,128]{3,2,1,0:T(8,128)(2,1)}), bf16[8,2,192,128]{3,2,1,0:T(8,128)(2,1)S(1)}, u32[]{:S(2)}, u32[]{:S(2)}) async-start(bf16[8,2,192,128]{3,2,1,0:T(8,128)(2,1)} %get-tuple-element.75), calls=%async_computation.6 | async-start | bytes 1572864 | tf_op jit(solution)/shard_map/all_to_all | solution.py:1214
  382.3 114.3 %reduce-scatter.6.cloned.1.call-start = ((), (), s32[]{:S(2)}) async-start(), calls=%async_computation.13 | async-start | bytes 2875392 | tf_op jit(solution)/shard_map/reduce_scatter | solution.py:1171
  382.3 35.4 %collective-permute-start.17 = (bf16[2,192,1024]{2,1,0:T(8,128)(2,1)S(1)}, bf16[2,192,1024]{2,1,0:T(8,128)(2,1)}, u32[]{:S(2)}, u32[]{:S(2)}) collective-permute-start(bf16[2,192,1024]{2,1,0:T(8,128)(2,1)S(1)} %get-tuple-element.113), channel_id=1, source_target_pairs={{0,6},{1,7},{2,0},{3,1},{4,2},{5,3},{6,4},{7,5},{8,14},{9,15},{10,... | collective-permute-start | bytes 2359304 | tf_op jit(solution)/shard_map/ppermute | solution.py:965
  385.1 37.5 %collective-permute-start.16 = (bf16[2,192,1024]{2,1,0:T(8,128)(2,1)S(1)}, bf16[2,192,1024]{2,1,0:T(8,128)(2,1)}, u32[]{:S(2)}, u32[]{:S(2)}) collective-permute-start(bf16[2,192,1024]{2,1,0:T(8,128)(2,1)S(1)} %get-tuple-element.114), channel_id=1, source_target_pairs={{0,4},{1,5},{2,6},{3,7},{4,0},{5,1},{6,2},{7,3},{8,12},{9,13},{10,... | collective-permute-start | bytes 2359304 | tf_op jit(solution)/shard_map/ppermute | solution.py:965
  385.7 51.8 %collective-permute-start.15 = (bf16[2,192,1024]{2,1,0:T(8,128)(2,1)S(1)}, bf16[2,192,1024]{2,1,0:T(8,128)(2,1)}, u32[]{:S(2)}, u32[]{:S(2)}) collective-permute-start(bf16[2,192,1024]{2,1,0:T(8,128)(2,1)S(1)} %get-tuple-element.115), channel_id=1, source_target_pairs={{0,2},{1,3},{2,4},{3,5},{4,6},{5,7},{6,0},{7,1},{8,10},{9,11},{10,... | collective-permute-start | bytes 2359304 | tf_op jit(solution)/shard_map/ppermute | solution.py:965
  388.4 56.6 %collective-permute-start.18 = (bf16[24,6912]{1,0:T(8,128)(2,1)}, bf16[24,6912]{1,0:T(8,128)(2,1)}, u32[]{:S(2)}, u32[]{:S(2)}) collective-permute-start(bf16[24,6912]{1,0:T(8,128)(2,1)} %get-tuple-element.126), channel_id=1, source_target_pairs={{0,8},{8,16},{16,24},{24,0},{1,9},{9,17},{17,25},{25,1},{2,10},{10... | collective-permute-start | bytes 995336 | tf_op jit(solution)/shard_map/ppermute | solution.py:985
  389.9 55.1 %collective-permute-start.20 = (bf16[24,6912]{1,0:T(8,128)(2,1)}, bf16[24,6912]{1,0:T(8,128)(2,1)}, u32[]{:S(2)}, u32[]{:S(2)}) collective-permute-start(bf16[24,6912]{1,0:T(8,128)(2,1)} %get-tuple-element.127), channel_id=1, source_target_pairs={{0,24},{8,0},{16,8},{24,16},{1,25},{9,1},{17,9},{25,17},{2,26},{10... | collective-permute-start | bytes 995336 | tf_op jit(solution)/shard_map/ppermute | solution.py:985
  417.7 27.3 %collective-permute-start.19 = (bf16[24,6912]{1,0:T(8,128)(2,1)S(1)}, bf16[24,6912]{1,0:T(8,128)(2,1)S(1)}, u32[]{:S(2)}, u32[]{:S(2)}) collective-permute-start(bf16[24,6912]{1,0:T(8,128)(2,1)S(1)} %get-tuple-element.128), channel_id=1, source_target_pairs={{0,16},{8,24},{16,0},{24,8},{1,17},{9,25},{17,1},{25,9},{2,18},{10... | collective-permute-start | bytes 995336 | tf_op jit(solution)/shard_map/ppermute | solution.py:985
  468.5 36.4 %all-to-all-start.7 = ((bf16[8,2,576,128]{3,2,1,0:T(8,128)(2,1)}), bf16[8,2,576,128]{3,2,1,0:T(8,128)(2,1)S(1)}, u32[]{:S(2)}, u32[]{:S(2)}) async-start(bf16[8,2,576,128]{3,2,1,0:T(8,128)(2,1)} %get-tuple-element.83), calls=%async_computation.9 | async-start | bytes 4718592 | tf_op jit(solution)/shard_map/all_to_all | solution.py:1239
  472.2 91.8 %all-gather.9.cloned.1.call-start = ((), (), s32[]{:S(2)}) async-start(), calls=%async_computation.15 | async-start | bytes 5419008 | tf_op jit(solution)/shard_map/all_gather | solution.py:1274
  476.3 32.8 %collective-permute-start.22 = (bf16[24,1536]{1,0:T(8,128)(2,1)}, bf16[24,1536]{1,0:T(8,128)(2,1)S(1)}, u32[]{:S(2)}, u32[]{:S(2)}) collective-permute-start(bf16[24,1536]{1,0:T(8,128)(2,1)} %get-tuple-element.132), channel_id=1, source_target_pairs={{0,8},{8,16},{16,24},{24,0},{1,9},{9,17},{17,25},{25,1},{2,10},{10... | collective-permute-start | bytes 221192 | tf_op jit(solution)/shard_map/ppermute | solution.py:985
  477.7 31.9 %collective-permute-start.24 = (bf16[24,1536]{1,0:T(8,128)(2,1)}, bf16[24,1536]{1,0:T(8,128)(2,1)}, u32[]{:S(2)}, u32[]{:S(2)}) collective-permute-start(bf16[24,1536]{1,0:T(8,128)(2,1)} %get-tuple-element.133), channel_id=1, source_target_pairs={{0,24},{8,0},{16,8},{24,16},{1,25},{9,1},{17,9},{25,17},{2,26},{10... | collective-permute-start | bytes 221192 | tf_op jit(solution)/shard_map/ppermute | solution.py:985
  480.1 29.4 %collective-permute-start.23 = (bf16[24,1536]{1,0:T(8,128)(2,1)}, bf16[24,1536]{1,0:T(8,128)(2,1)}, u32[]{:S(2)}, u32[]{:S(2)}) collective-permute-start(bf16[24,1536]{1,0:T(8,128)(2,1)} %get-tuple-element.134), channel_id=1, source_target_pairs={{0,16},{8,24},{16,0},{24,8},{1,17},{9,25},{17,1},{25,9},{2,18},{10... | collective-permute-start | bytes 221192 | tf_op jit(solution)/shard_map/ppermute | solution.py:985
  (40 other events, 430.5 us)
Sparse Core Ops, SparseCore 0:
  10.2 43.7 all-gather.10
  55.6 29.0 all-gather.12
  88.2 125.2 all-gather.6
  281.8 89.1 reduce-scatter.3
  378.8 60.2 reduce-scatter.7
  445.1 51.4 reduce-scatter.5
  524.4 39.4 all-gather.8

commit v3 on v2

--- a/solution.py
+++ b/solution.py
@@ -24,6 +24,10 @@
 
 f32 = jnp.float32
 half = jnp.bfloat16
+
+
+def cost_of(micros):
+    return pl.CostEstimate(flops=micros * 10**9, bytes_accessed=micros * 10**6, transcendentals=0)
 
 
 def layer_norm(resid_in, gain_row, shift_row):
@@ -184,6 +188,7 @@
             jax.ShapeDtypeStruct((slots, GROUP_HEADS, length), f32),
         ],
         compiler_params=pltpu.CompilerParams(vmem_limit_bytes=vmem_bytes),
+        cost_estimate=cost_of(18),
         name="self_forward",
     )(places, w_part, bias, *pieces, *after)
 
@@ -291,6 +296,7 @@
             jax.ShapeDtypeStruct((8, feats), f32),
         ],
         compiler_params=pltpu.CompilerParams(vmem_limit_bytes=vmem_bytes),
+        cost_estimate=cost_of(20),
         name="self_backward",
     )(places, proj, grad_mix, mix, lse, *pieces, *after)
 
@@ -345,6 +351,7 @@
         ],
         scratch_shapes=[pltpu.VMEM((D, rows_total), half)],
         compiler_params=pltpu.CompilerParams(vmem_limit_bytes=vmem_bytes),
+        cost_estimate=cost_of(6),
         name="enter",
     )(att, x_low, vectors, w_pair)
 
@@ -359,9 +366,19 @@
     scale_ref,
     vec_ref,
     w_ref,
-    *rest,
+    mem_ref,
+    rows_a_ref,
+    rows_b_ref,
+    rows_c_ref,
+    out_ref,
+    send_ref,
+    packed_ref,
+    att_all,
+    query_all,
+    query_rows,
+    low_rows,
+    sums_ref,
 ):
-    out_ref, send_ref, packed_ref, sums_ref, att_all, query_all, query_rows, low_rows = rest[-8:]
     slots, rows_dev = query_ref.shape[1], query_ref.shape[3]
     member_slots = att_ref.shape[1]
     spread = slots // member_slots
@@ -401,34 +418,42 @@
     store_rows(packed_ref, n_doc, dot_nn(att_all[...], low_rows[...]), slice(0, D))
     grad = dot_tn(norm_ref[...].astype(half), query_rows[...])
     store_rows(packed_ref, n_doc, grad, slice(D, 2 * D))
-
-
-def leave(n_doc, grad_query, att, resid, norm_one, unit, scale, vectors, w_pair, *after):
+    packed_ref[:, :, 2 * D : 4 * D] = mem_ref[...]
+    small = [sums_ref[...], rows_a_ref[...], rows_b_ref[...], rows_c_ref[0:1, :]]
+    used = sum(rows.shape[0] for rows in small)
+    small.append(jnp.zeros((small_cols - used, D), f32))
+    store_rows(
+        packed_ref, n_doc, jnp.concatenate(small, axis=0).T, slice(4 * D, 4 * D + small_cols)
+    )
+
+
+def leave(n_doc, grad_query, att, resid, norm_one, unit, scale, vectors, w_pair, *others):
     rows_total, n_seq = resid.shape[0], att.shape[0]
     vmem = pl.BlockSpec(memory_space=pltpu.VMEM)
     return pl.pallas_call(
         partial(leave_kernel, n_doc),
-        in_specs=[vmem] * 8 + [pl.BlockSpec(memory_space=pl.ANY)] * len(after),
-        out_specs=[vmem] * 4,
+        in_specs=[vmem] * (8 + len(others)),
+        out_specs=[vmem] * 3,
         out_shape=[
             jax.ShapeDtypeStruct((rows_total, D), f32),
             jax.ShapeDtypeStruct(att.shape, half),
-            jax.ShapeDtypeStruct((n_seq, D // n_seq, 2 * D), half),
-            jax.ShapeDtypeStruct((8, D), f32),
+            jax.ShapeDtypeStruct((n_seq, D // n_seq, 4 * D + small_cols), half),
         ],
         scratch_shapes=[
             pltpu.VMEM((D, rows_total), half),
             pltpu.VMEM((D, rows_total), half),
             pltpu.VMEM((rows_total, D), half),
             pltpu.VMEM((rows_total, D), half),
+            pltpu.VMEM((8, D), f32),
         ],
         compiler_params=pltpu.CompilerParams(vmem_limit_bytes=vmem_bytes),
+        cost_estimate=cost_of(8),
         name="leave",
-    )(grad_query, att, resid, norm_one, unit, scale, vectors, w_pair, *after)
-
-
-def memory_kernel(n_doc, place_ref, mem_ref, rows_a_ref, rows_b_ref, rows_c_ref, *rest):
-    pieces, (packed_ref, all_ref) = rest[: place_ref.shape[0]], rest[-2:]
+    )(grad_query, att, resid, norm_one, unit, scale, vectors, w_pair, *others)
+
+
+def memory_kernel(n_doc, place_ref, mem_ref, *rest):
+    pieces, (packed_ref, all_ref, sums_ref) = rest[: place_ref.shape[0]], rest[-3:]
     for turn, piece in enumerate(pieces):
         for kind in range(2):
             first = pl.multiple_of(kind * D + place_ref[turn] * GROUP_FEATS, GROUP_FEATS)
@@ -437,19 +462,13 @@
     for kind in range(2):
         cols = slice(kind * D, (kind + 1) * D)
         store_rows(packed_ref, n_doc, dot_tn(mem_ref[...], turned[:, cols]), cols)
-    value_sum = row_sum(turned[:, D:].astype(f32))
-    small = [rows_a_ref[...], rows_b_ref[...], rows_c_ref[...], value_sum]
-    used = sum(rows.shape[0] for rows in small)
-    small.append(jnp.zeros((small_cols - used, D), f32))
-    store_rows(
-        packed_ref, n_doc, jnp.concatenate(small, axis=0).T, slice(2 * D, 2 * D + small_cols)
-    )
+    sums_ref[...] = jnp.broadcast_to(row_sum(turned[:, D:].astype(f32)), sums_ref.shape)
 
 
 small_cols = 128
 
 
-def memory_backward(n_doc, n_seq, places, mem_low, rows_a, rows_b, rows_c, pieces, *after):
+def memory_backward(n_doc, n_seq, places, mem_low, pieces):
     tokens = mem_low.shape[0]
     vmem = pl.BlockSpec(memory_space=pltpu.VMEM)
     return pl.pallas_call(
@@ -457,32 +476,35 @@
         grid_spec=pltpu.PrefetchScalarGridSpec(
             num_scalar_prefetch=1,
             grid=(1,),
-            in_specs=[vmem] * (4 + len(pieces))
-            + [pl.BlockSpec(memory_space=pl.ANY)] * len(after),
-            out_specs=[vmem] * 2,
+            in_specs=[vmem] * (1 + len(pieces)),
+            out_specs=[vmem] * 3,
         ),
         out_shape=[
-            jax.ShapeDtypeStruct((n_seq, D // n_seq, 2 * D + small_cols), half),
+            jax.ShapeDtypeStruct((n_seq, D // n_seq, 2 * D), half),
             jax.ShapeDtypeStruct((2 * D, tokens), half),
+            jax.ShapeDtypeStruct((8, D), f32),
         ],
         compiler_params=pltpu.CompilerParams(vmem_limit_bytes=vmem_bytes),
+        cost_estimate=cost_of(7),
         name="memory_backward",
-    )(places, mem_low, rows_a, rows_b, rows_c, *pieces, *after)
+    )(places, mem_low, *pieces)
 
 
 def finish_kernel(
     n_seq,
     stack_n,
+    lanes,
     in_ref,
     qkv_ref,
     out_ref,
     q_ref,
     kv_ref,
-    small_ref,
-    bias_ref,
     down_ref,
     ffn_ref,
     cross_ref,
+    gains_ref,
+    biases_ref,
+    hidden_ref,
 ):
     rows = in_ref.shape[0]
     share = rows // n_seq
@@ -490,7 +512,7 @@
     out_ref[...] = in_ref[:, :D].astype(f32)
     q_ref[...] = in_ref[:, D : 2 * D].astype(f32)
     kv_ref[...] = in_ref[:, 2 * D : 4 * D].astype(f32)
-    small_ref[...] = in_ref[:, 4 * D : 4 * D + small_cols].astype(f32).T
+    small = in_ref[:, 4 * D : 4 * D + small_cols].astype(f32).T
     first_col = 4 * D + small_cols
     feats = 3 * GROUP_FEATS
     ff = ffn_ref.shape[1]
@@ -503,7 +525,7 @@
         for s in range(n_seq):
             first = (s * stack_n + q) * share
             down_ref[first : first + share, :] = mine[s * share : (s + 1) * share]
-    bias = jnp.zeros(bias_ref.shape, f32)
+    bias = jnp.zeros((share, small_cols), f32)
     wide = in_ref[:, first_col:down_col].astype(f32)
     for s in range(n_seq):
         group, m = s // spread, s % spread
@@ -517,28 +539,38 @@
                     part * D + group * GROUP_FEATS : part * D + (group + 1) * GROUP_FEATS,
                 ] = mine[:, start : start + GROUP_FEATS]
         bias = bias + mine[:, HEAD_GROUPS * feats :]
-    bias_ref[...] = bias
-
-
-def finish(n_seq, stack_n, packed):
+    for row, source in enumerate((0, 8, 10)):
+        gains_ref[row : row + 1, :] = small[source : source + 1]
+    for row, source in ((2, 2), (3, 3), (4, 16 + stack_n), (5, 12), (6, 13), (7, 1), (8, 9), (9, 11)):
+        biases_ref[row : row + 1, :] = small[source : source + 1]
+    hidden_ref[...] = small[16 : 16 + stack_n]
+    per_row = lanes // small_cols
+    for row in range(2):
+        found = [bias[row * per_row + i : row * per_row + i + 1] for i in range(per_row)]
+        biases_ref[row : row + 1, :] = jnp.concatenate(found, axis=1)[:, :rows]
+
+
+def finish(n_seq, stack_n, lanes, packed):
     rows = packed.shape[0]
     vmem = pl.BlockSpec(memory_space=pltpu.VMEM)
     return pl.pallas_call(
-        partial(finish_kernel, n_seq, stack_n),
+        partial(finish_kernel, n_seq, stack_n, lanes),
         in_specs=[vmem],
-        out_specs=[vmem] * 9,
+        out_specs=[vmem] * 10,
         out_shape=[
             jax.ShapeDtypeStruct((rows, 3 * D), f32),
             jax.ShapeDtypeStruct((rows, D), f32),
             jax.ShapeDtypeStruct((rows, D), f32),
             jax.ShapeDtypeStruct((rows, 2 * D), f32),
-            jax.ShapeDtypeStruct((small_cols, rows), f32),
-            jax.ShapeDtypeStruct((rows // n_seq, small_cols), f32),
             jax.ShapeDtypeStruct((rows * stack_n, D), f32),
             jax.ShapeDtypeStruct((rows, stack_n * D), f32),
             jax.ShapeDtypeStruct((rows, D), f32),
+            jax.ShapeDtypeStruct((3, rows), f32),
+            jax.ShapeDtypeStruct((10, rows), f32),
+            jax.ShapeDtypeStruct((stack_n, rows), f32),
         ],
         compiler_params=pltpu.CompilerParams(vmem_limit_bytes=vmem_bytes),
+        cost_estimate=cost_of(6),
         name="finish",
     )(packed)
 
@@ -643,6 +675,7 @@
             jax.ShapeDtypeStruct((slots, GROUP_HEADS, rows), f32),
         ],
         compiler_params=pltpu.CompilerParams(vmem_limit_bytes=vmem_bytes),
+        cost_estimate=cost_of(45),
         name="cross_forward",
     )(low, high, places, queries, *pieces)
 
@@ -747,6 +780,7 @@
         ]
         + [jax.ShapeDtypeStruct(grad_shape[1:], half)] * grad_shape[0],
         compiler_params=pltpu.CompilerParams(vmem_limit_bytes=vmem_bytes),
+        cost_estimate=cost_of(53),
         name="cross_backward",
     )(low, high, places, queries, grad_mix, mix, lse, *pieces, *after)
 
@@ -921,6 +955,7 @@
             pltpu.SemaphoreType.DMA((n_doc * n_seq * 9 // 4,)),
         ],
         compiler_params=pltpu.CompilerParams(vmem_limit_bytes=vmem_bytes),
+        cost_estimate=cost_of(31),
         name="middle",
     )(att, norm_one, out_grad, vectors, bias, *weights)
 
@@ -1060,7 +1095,7 @@
         ).astype(half)
 
     def first_cols(*starts):
-        return jnp.stack(starts)[block_cols]
+        return sum(jnp.where(block_cols == i, start, 0) for i, start in enumerate(starts) if start)
 
     left = jnp.where(
         block_cols == 0,
@@ -1133,6 +1168,9 @@
         got = blocks.reshape(HEAD_GROUPS, slots_n, feats // GROUP_FEATS, GROUP_FEATS, rows_dev)
         return got.transpose(2, 0, 3, 1, 4).reshape(HEAD_GROUPS * feats, rows_total)
 
+    self_att_send, *pieces[1:HEAD_GROUPS] = lax.optimization_barrier(
+        (self_att_send, *pieces[1:HEAD_GROUPS])
+    )
     self_att = lax.all_to_all(self_att_send, "seq", 0, 0, tiled=True)
     pair_halves = lax.optimization_barrier((pair_halves, self_att_send))[0]
     w_pair = join_members(pair_halves).reshape(D, 2 * D)
@@ -1198,7 +1236,14 @@
             for piece in grad_kv
         ).astype(half)
         grad_kv_own.append(rotate_heads(total, turn) if turn else total)
-    grad_r1, grad_att_send, pair_packed, first_rows_grad = leave(
+    late_own = own_rows(lax.optimization_barrier((late_blocks, grad_kv_own[0]))[0])
+    grad_query_send, late_own, *grad_kv_own = lax.optimization_barrier(
+        (grad_query_send, late_own, *grad_kv_own)
+    )
+    mem_packed, grad_mem_kv, value_rows = memory_backward(
+        n_doc, n_seq, group_places, mem_low, grad_kv_own
+    )
+    grad_r1, grad_att_send, packed = leave(
         n_doc,
         swap_heads(grad_query_send),
         self_att,
@@ -1208,23 +1253,13 @@
         scale_one,
         first_vectors,
         w_pair,
-        grad_kv_own[0],
-    )
-    pair_over_seq = sum_over_seq(pair_packed)
-    grad_self_part = lax.all_to_all(grad_att_send, "seq", 0, 0, tiled=True)
-    late_own = own_rows(lax.optimization_barrier((late_blocks, grad_r1))[0])
-    mem_packed, grad_mem_kv = memory_backward(
-        n_doc,
-        n_seq,
-        group_places,
-        mem_low,
-        first_rows_grad,
+        mem_packed,
         late_rows,
         grad_b_in.reshape(n_doc, -1, part).transpose(1, 0, 2).reshape(-1, D),
-        grad_kv_own,
-        grad_self_part,
-        late_blocks,
-    )
+        value_rows,
+    )
+    over_seq = sum_over_seq(packed)
+    grad_self_part = lax.all_to_all(grad_att_send, "seq", 0, 0, tiled=True)
     grad_proj_send, grad_part, part_sums = self_backward(
         n_doc,
         places,
@@ -1233,9 +1268,9 @@
         self_mix,
         self_lse,
         x_pieces,
-        mem_packed,
-        late_own,
-    )
+        packed,
+    )
+    grad_proj_send = lax.optimization_barrier((grad_proj_send, over_seq))[0]
     grad_proj_got = lax.all_to_all(grad_proj_send, "seq", 0, 0, tiled=True)
 
     bias_rows = jnp.zeros((2, D), f32)
@@ -1255,34 +1290,25 @@
     grad_part = send_turns(grad_part, 0, spread, member, rotate_members)
     grad_part = sum(piece.astype(f32) for piece in grad_part).astype(half)
 
-    pair_own = own_rows(pair_over_seq)
-    grads = jnp.concatenate([sum_over_seq(mem_packed), grad_part], axis=1)
-    grads, grad_proj_got = lax.optimization_barrier((grads, grad_proj_got))
+    grads = jnp.concatenate([over_seq, grad_part], axis=1)
+    owned = jnp.concatenate([own_rows(grads), late_own], axis=1)
+    param_grads = finish(n_seq, stack_n, lanes, lax.all_gather(owned, "seq", axis=0, tiled=True))
     (
         grad_w_qkv,
         grad_w_self_out,
         grad_w_cross_q,
         grad_w_cross_kv,
-        small_grad,
-        bias_sums,
         grad_w_down,
         grad_w_in,
         grad_w_cross_out,
-    ) = finish(
-        n_seq,
-        stack_n,
-        lax.all_gather(
-            jnp.concatenate([pair_own, own_rows(grads), late_own], axis=1), "seq", axis=0, tiled=True
-        ),
-    )
+        grad_gains,
+        grad_biases,
+        grad_b_hidden,
+    ) = param_grads
     grad_proj = from_heads(grad_proj_got)
     memory_grad = dot_tt(grad_mem_kv, w_cross_kv)[None]
     w_qkv = columns((2, 2), (3, 1), (3, 2))
     input_grad = (grad_r1 + dot_tt(grad_proj, w_qkv)).reshape(dec_input.shape)
-    grad_g0, grad_c7, grad_b2, grad_b3 = small_grad[:4]
-    grad_g1, grad_c8, grad_g2, grad_c9, grad_b5, grad_b6 = small_grad[8:14]
-    grad_b0, grad_b1 = bias_sums[:bias_used].reshape(2, lanes)[:, :part]
-    grad_b4 = small_grad[16 + stack_n]
     return (
         layer_out,
         input_grad,
@@ -1293,13 +1319,10 @@
         grad_w_cross_kv,
         grad_w_cross_out,
         grad_w_in,
-        small_grad[16 : 16 + stack_n].reshape(-1),
+        grad_b_hidden.reshape(-1),
         grad_w_down,
-        jnp.stack([grad_g0, grad_g1, grad_g2]),
-        jnp.stack(
-            [grad_b0, grad_b1, grad_b2, grad_b3, grad_b4, grad_b5, grad_b6]
-            + [grad_c7, grad_c8, grad_c9]
-        ),
+        grad_gains,
+        grad_biases,
     )
 
 

time: 594 us -> 564 us (0.949)
  local copies, waits for them, and re-layouts: 44.3 us -> 36.9 us
    ppermute x19, waiting for transfers between devices: 97.1 us -> 46.5 us  [rotate_both(): lax.ppermute(block, 'seq', [(h * spread + m, (h + turn_h) % HEAD_GROUPS *...]
    ppermute x9 -> x6, waiting for transfers between devices: 12.7 us -> 44.7 us  [rotate_doc(): lax.ppermute(block, 'doc', [(d, (d + turn) % n_doc) for d in range(n_doc)])]
    all_to_all x1, waiting for transfers between devices: 7.21 us -> 27.3 us  [body(): grad_proj_got = lax.all_to_all(grad_proj_send, 'seq', 0, 0, tiled=True)]
    all_to_all x3, waiting for transfers between devices: 32.7 us -> 14.3 us  [swap_heads(): lax.all_to_all(blocks, 'seq', 0, 0, axis_index_groups=same_member, tiled=...]
    all_gather x1, waiting for transfers between devices: 26.6 us -> 8.48 us  [body(): lax.all_gather(owned, 'seq', axis=0, tiled=True)]
    all_to_all x1, waiting for transfers between devices: 0.01 us -> 12.2 us  [body(): grad_self_part = lax.all_to_all(grad_att_send, 'seq', 0, 0, tiled=True)]
    all_to_all x1, waiting for transfers between devices: 6.55 us -> 14.8 us  [body(): self_att = lax.all_to_all(self_att_send, 'seq', 0, 0, tiled=True)]
    ppermute x9 -> x6, starting transfers between devices: 15.3 us -> 8.96 us  [rotate_doc(): lax.ppermute(block, 'doc', [(d, (d + turn) % n_doc) for d in range(n_doc)])]
  transfers between devices with their start and end apart: 42 -> 38, of which waited for: 18 -> 23; matrix products, arithmetic and copies ran while one was open for 11% -> 9% of each run, Pallas kernels for 28% -> 27%
where the time goes in v3:
time: 564 us; the launch traced here: 555 us
  waiting for transfers between devices  212 us (38%)
  Pallas kernels  200 us (35%)
  starting transfers between devices  51.1 us (9%)
  local copies, waits for them, and re-layouts  36.9 us (7%)
  other arithmetic  17.3 us (3%)
  between operations  16.2 us (3%)
  blocking collectives  11.7 us (2%)
  matrix products  9.54 us (2%)
    pallas_call x1, Pallas kernels, cross_backward(): pl.pallas_call(cross_backward_kernel, grid_spec=pltpu.PrefetchScalarGridS...  53.5 us
    pallas_call x1, Pallas kernels, cross_forward(): pl.pallas_call(cross_forward_kernel, grid_spec=pltpu.PrefetchScalarGridSp...  47.3 us
    ppermute x19, waiting for transfers between devices, rotate_both(): lax.ppermute(block, 'seq', [(h * spread + m, (h + turn_h) % HEAD_GROUPS *...  46.5 us
    ppermute x6, waiting for transfers between devices, rotate_doc(): lax.ppermute(block, 'doc', [(d, (d + turn) % n_doc) for d in range(n_doc)])  44.7 us
    pallas_call x1, Pallas kernels, middle(): pl.pallas_call(partial(middle_kernel, n_doc, n_seq), in_specs=[vmem] * 5...  31.5 us
    all_to_all x1, waiting for transfers between devices, body(): grad_proj_got = lax.all_to_all(grad_proj_send, 'seq', 0, 0, tiled=True)  27.3 us
    all_to_all x1, waiting for transfers between devices, body(): lax.all_to_all(first_piece, 'doc', 0, 0, tiled=True)  25.3 us
    pallas_call x1, Pallas kernels, self_backward(): pl.pallas_call(partial(self_backward_kernel, n_doc), grid_spec=pltpu.Pref...  20 us
  transfers between devices with their start and end apart: 38, of which 23 were waited for; matrix products, arithmetic and copies ran while one was open for 9% of the time, Pallas kernels for 27%

profile of v3, /device:TPU:0, one launch (start us, length us, event | category | flops | bytes accessed | tf_op | source)
XLA Modules:
  0.0 554.9 jit_solution(12037735484075635136)
XLA Ops:
  16.2 6.3 %all-to-all-start = ((bf16[4,104,576]{2,1,0:T(8,128)(2,1)}), bf16[4,104,576]{2,1,0:T(8,128)(2,1)S(1)}, u32[]{:S(2)}, u32[]{:S(2)}) async-start(bf16[4,104,576]{2,1,0:T(8,128)(2,1)} %broadcast_in_dim.49), calls=%async_computation | async-start | bytes 1064960 | tf_op jit(solution)/shard_map/all_to_all | solution.py:1067
  26.8 25.3 %all-to-all-done = bf16[4,104,576]{2,1,0:T(8,128)(2,1)S(1)} async-done(((bf16[4,104,576]{2,1,0:T(8,128)(2,1)}), bf16[4,104,576]{2,1,0:T(8,128)(2,1)S(1)}, u32[]{:S(2)}, u32[]{:S(2)}) %all-to-all-start) | async-done | bytes 479264 | tf_op jit(solution)/shard_map/all_to_all | solution.py:1067
  52.3 8.3 %collective-permute-done.2.rest_2_ = bf16[4,128,768]{2,1,0:T(8,128)(2,1)S(1)} collective-permute-done((bf16[4,128,768]{2,1,0:T(8,128)(2,1)S(1)}, bf16[4,128,768]{2,1,0:T(8,128)(2,1)S(1)}, u32[]{:S(2)}, u32[]{:S(2)}) %collective-permute-start.2) | collective-permute-done | bytes 786464 | tf_op jit(solution)/shard_map/ppermute | solution.py:1000
  75.9 17.9 %self_forward.1 = (bf16[576,2048]{1,0:T(8,128)(2,1)}, f32[2,192,1024]{2,1,0:T(8,128)}, bf16[8,2,192,128]{3,2,1,0:T(8,128)(2,1)}, f32[2,3,1024]{2,1,0:T(4,128)}) custom-call(s32[8]{0:T(128)} %stack.57.place_ref, bf16[768,576]{1,0:T(8,128)(2,1)} %bitcast.154, f32[1,576]{1,0:T(1,128)} %broadcast_in_dim.53.bias_ref, bf16[4,128,768]{2,1,0:T(8,128)(2,1)} %bitcast.156, ...), custom_call_target="tpu_custom_call" | custom-call | flops 17999998976 | bytes 18000000 | tf_op jit(solution)/shard_map/self_forward/pallas_call | solution.py:163
  93.9 8.6 %collective-permute-done.7.rest_2_ = bf16[2,192,1024]{2,1,0:T(8,128)(2,1)} collective-permute-done((bf16[2,192,1024]{2,1,0:T(8,128)(2,1)S(1)}, bf16[2,192,1024]{2,1,0:T(8,128)(2,1)}, u32[]{:S(2)}, u32[]{:S(2)}) %collective-permute-start.7) | collective-permute-done | bytes 786464 | tf_op jit(solution)/shard_map/ppermute | solution.py:1000
  102.5 10.6 %collective-permute-done.6.rest_1_ = bf16[2,192,1024]{2,1,0:T(8,128)(2,1)} collective-permute-done((bf16[2,192,1024]{2,1,0:T(8,128)(2,1)S(1)}, bf16[2,192,1024]{2,1,0:T(8,128)(2,1)}, u32[]{:S(2)}, u32[]{:S(2)}) %collective-permute-start.6) | collective-permute-done | bytes 786464 | tf_op jit(solution)/shard_map/ppermute | solution.py:1000
  115.9 4.7 all-to-all-start.1
  123.4 14.8 %all-to-all-done.1.att_ref = bf16[8,2,192,128]{3,2,1,0:T(8,128)(2,1)} async-done(((bf16[8,2,192,128]{3,2,1,0:T(8,128)(2,1)}), bf16[8,2,192,128]{3,2,1,0:T(8,128)(2,1)}, u32[]{:S(2)}, u32[]{:S(2)}) %all-to-all-start.1) | async-done | bytes 786464 | tf_op jit(solution)/shard_map/all_to_all | solution.py:1174
  138.1 6.1 %enter.1 = (f32[512,768]{1,0:T(8,128)}, f32[512,768]{1,0:T(8,128)}, f32[512,128]{1,0:T(8,128)}, bf16[4,4,192,128]{3,2,1,0:T(8,128)(2,1)}) custom-call(bf16[8,2,192,128]{3,2,1,0:T(8,128)(2,1)} %all-to-all-done.1.att_ref, bf16[512,768]{1,0:T(8,128)(2,1)} %bitcast.157, f32[8,768]{1,0:T(8,128)} %select_maximum_fusion.vec_ref, bf16[768,1536]{1,0:T(8,128)(2,1)} %bitcast.141), custom_call_target="tpu_custom_call" | custom-call | flops 6000000000 | bytes 6000000 | tf_op jit(solution)/shard_map/enter/pallas_call | solution.py:342
  149.1 6.7 %all-to-all-done.2.q_ref = bf16[4,4,192,128]{3,2,1,0:T(8,128)(2,1)S(1)} async-done(((bf16[4,4,192,128]{3,2,1,0:T(8,128)(2,1)}), bf16[4,4,192,128]{3,2,1,0:T(8,128)(2,1)S(1)}, u32[]{:S(2)}, u32[]{:S(2)}) %all-to-all-start.2) | async-done | bytes 786464 | tf_op jit(solution)/shard_map/all_to_all | solution.py:995
  156.6 47.3 %cross_forward.1 = (f32[4,192,512]{2,1,0:T(8,128)}, bf16[4,4,192,128]{3,2,1,0:T(8,128)(2,1)}, f32[4,3,512]{2,1,0:T(4,128)}) custom-call(s32[4]{0:T(128)} %pad_add_fusion.low_ref, s32[4]{0:T(128)} %get-tuple-element.154.high_ref, s32[8]{0:T(128)} %stack.57.place_ref, bf16[4,4,192,128]{3,2,1,0:T(8,128)(2,1)} %copy-done.12, ...), custom_call_target="tpu_custom_call" | custom-call | flops 44999999488 | bytes 45000000 | tf_op jit(solution)/shard_map/cross_forward/pallas_call | solution.py:655
  210.2 5.2 all-to-all-done.3.att_ref
  216.3 31.5 %middle.1 = (bf16[512,768]{1,0:T(8,128)(2,1)}, f32[512,768]{1,0:T(8,128)}, bf16[4,4,192,128]{3,2,1,0:T(8,128)(2,1)}, bf16[8,96,6912]{2,1,0:T(8,128)(2,1)}, f32[8,768]{1,0:T(8,128)}, /*index=5*/f32[1,3072]{1,0:T(1,128)}) custom-call(bf16[4,4,192,128]{3,2,1,0:T(8,128)(2,1)} %copy-done.13, f32[512,768]{1,0:T(8,128)} %get-tuple-element.73.norm_ref, ...), custom_call_target="tpu_custom_call" | custom-call | flops 31000000512 | bytes 31000000 | tf_op jit(solution)/shard_map/middle/pallas_call | solution.py:932
  249.0 11.7 %all_to_all.40.g_ref = bf16[4,4,192,128]{3,2,1,0:T(8,128)(2,1)} all-to-all(bf16[4,4,192,128]{3,2,1,0:T(8,128)(2,1)S(1)} %copy-done.16), channel_id=1, replica_groups={{0,2,4,6},{1,3,5,7},{8,10,12,14},{9,11,13,15},{16,18,20,22},{17,19,21,2..., dimensions={0} | all-to-all | bytes 1572864 | tf_op jit(solution)/shard_map/all_to_all | solution.py:995
  260.7 53.5 %cross_backward.1 = (bf16[4,4,192,128]{3,2,1,0:T(8,128)(2,1)}, bf16[4,2,192,1024]{3,2,1,0:T(8,128)(2,1)}, bf16[4,2,192,1024]{3,2,1,0:T(8,128)(2,1)}) custom-call(s32[4]{0:T(128)} %pad_add_fusion.low_ref, s32[4]{0:T(128)} %get-tuple-element.154.high_ref, s32[8]{0:T(128)} %stack.57.place_ref, bf16[4,4,192,128]{3,2,1,0:T(8,128)(2,1)} %copy-done.12, ...), custom_call_target="tpu_custom_call" | custom-call | flops 52999999488 | bytes 53000000 | tf_op jit(solution)/shard_map/cross_backward/pallas_call | solution.py:758
  314.3 5.8 %collective-permute-done.14 = bf16[4,2,192,1024]{3,2,1,0:T(8,128)(2,1)S(1)} collective-permute-done((bf16[4,2,192,1024]{3,2,1,0:T(8,128)(2,1)}, bf16[4,2,192,1024]{3,2,1,0:T(8,128)(2,1)S(1)}, u32[]{:S(2)}, u32[]{:S(2)}) %collective-permute-start.14) | collective-permute-done | bytes 3145760 | tf_op jit(solution)/shard_map/ppermute | solution.py:1000
  320.1 4.7 fusion.14
  324.8 5.9 %reduce-scatter.3.cloned.1.call-done = bf16[96,6912]{1,0:T(8,128)(2,1)} async-done(((bf16[768,6912]{1,0:T(8,128)(2,1)}), bf16[96,6912]{1,0:T(8,128)(2,1)}) %reduce-scatter.3.cloned.1.call-update) | async-done | bytes 1327120 | tf_op jit(solution)/shard_map/reduce_scatter | solution.py:1209
  349.9 14.9 %collective-permute-done.16 = bf16[24,6912]{1,0:T(8,128)(2,1)} collective-permute-done((bf16[24,6912]{1,0:T(8,128)(2,1)S(1)}, bf16[24,6912]{1,0:T(8,128)(2,1)}, u32[]{:S(2)}, u32[]{:S(2)}) %collective-permute-start.16) | collective-permute-done | bytes 331808 | tf_op jit(solution)/shard_map/ppermute | solution.py:1020
  366.1 9.4 %collective-permute-done.19.rest_2_ = bf16[2,192,1024]{2,1,0:T(8,128)(2,1)S(1)} collective-permute-done((bf16[2,192,1024]{2,1,0:T(8,128)(2,1)S(1)}, bf16[2,192,1024]{2,1,0:T(8,128)(2,1)S(1)}, u32[]{:S(2)}, u32[]{:S(2)}) %collective-permute-start.19) | collective-permute-done | bytes 786464 | tf_op jit(solution)/shard_map/ppermute | solution.py:1000
  381.0 7.4 %memory_backward.1 = (bf16[8,96,1536]{2,1,0:T(8,128)(2,1)}, bf16[1536,1024]{1,0:T(8,128)(2,1)}, f32[8,768]{1,0:T(8,128)}) custom-call(s32[4]{0:T(128)} %and_select_fusion.place_ref, bf16[1024,768]{1,0:T(8,128)(2,1)} %bitcast.164, bf16[2,192,1024]{2,1,0:T(8,128)(2,1)} %get-tuple-element.87.rest_0_, bf16[2,192,1024]{2,1,0:T(8,128)(2,1)} %copy-done.31, ...), custom_call_target="tpu_custom_call" | custom-call | flops 7000000000 | bytes 7000000 | tf_op jit(solution)/shard_map/memory_backward/pallas_call | solution.py:474
  391.7 9.9 %leave.1 = (f32[512,768]{1,0:T(8,128)}, bf16[8,2,192,128]{3,2,1,0:T(8,128)(2,1)}, bf16[8,96,3200]{2,1,0:T(8,128)(2,1)}) custom-call(bf16[4,4,192,128]{3,2,1,0:T(8,128)(2,1)} %copy-done.14, bf16[8,2,192,128]{3,2,1,0:T(8,128)(2,1)} %all-to-all-done.1.att_ref, f32[512,768]{1,0:T(8,128)} %get-tuple-element.84.resid_ref, f32[512,768]{1,0:T(8,128)} %get-tuple-element.73.norm_ref, ...), custom_call_target="tpu_custom_call" | custom-call | flops 8000000000 | bytes 8000000 | tf_op jit(solution)/shard_map/leave/pallas_call | solution.py:433
  405.5 12.2 %all-to-all-done.6.grad_ref = bf16[8,2,192,128]{3,2,1,0:T(8,128)(2,1)S(1)} async-done(((bf16[8,2,192,128]{3,2,1,0:T(8,128)(2,1)}), bf16[8,2,192,128]{3,2,1,0:T(8,128)(2,1)S(1)}, u32[]{:S(2)}, u32[]{:S(2)}) %all-to-all-start.6) | async-done | bytes 786464 | tf_op jit(solution)/shard_map/all_to_all | solution.py:1262
  418.6 20.0 %self_backward.1 = (bf16[8,2,576,128]{3,2,1,0:T(8,128)(2,1)}, bf16[2,96,2304]{2,1,0:T(8,128)(2,1)}, f32[8,576]{1,0:T(8,128)}) custom-call(s32[8]{0:T(128)} %stack.57.place_ref, bf16[576,2048]{1,0:T(8,128)(2,1)} %get-tuple-element.96.proj_ref, bf16[8,2,192,128]{3,2,1,0:T(8,128)(2,1)} %copy-done.15, f32[2,192,1024]{2,1,0:T(8,128)} %get-tuple-element.98.mix_ref, ...), custom_call_target="tpu_custom_call" | custom-call | flops 20000000000 | bytes 20000000 | tf_op jit(solution)/shard_map/self_backward/pallas_call | solution.py:267
  443.0 12.6 %reduce-scatter.5.cloned.1.call-done = bf16[96,3200]{1,0:T(8,128)(2,1)} async-done(((bf16[768,3200]{1,0:T(8,128)(2,1)}), bf16[96,3200]{1,0:T(8,128)(2,1)}) %reduce-scatter.5.cloned.1.call-update) | async-done | bytes 614416 | tf_op jit(solution)/shard_map/reduce_scatter | solution.py:1209
  461.3 6.8 %collective-permute-done.22 = bf16[24,5632]{1,0:T(8,128)(2,1)S(1)} collective-permute-done((bf16[24,5632]{1,0:T(8,128)(2,1)S(1)}, bf16[24,5632]{1,0:T(8,128)(2,1)S(1)}, u32[]{:S(2)}, u32[]{:S(2)}) %collective-permute-start.22) | collective-permute-done | bytes 270368 | tf_op jit(solution)/shard_map/ppermute | solution.py:1020
  472.1 12.2 %collective-permute-done.23 = bf16[24,5632]{1,0:T(8,128)(2,1)S(1)} collective-permute-done((bf16[24,5632]{1,0:T(8,128)(2,1)S(1)}, bf16[24,5632]{1,0:T(8,128)(2,1)S(1)}, u32[]{:S(2)}, u32[]{:S(2)}) %collective-permute-start.23) | collective-permute-done | bytes 270368 | tf_op jit(solution)/shard_map/ppermute | solution.py:1020
  489.3 4.1 fusion.31
  494.4 4.3 convolution_bitcast_fusion
  498.7 27.3 %all-to-all-done.7 = bf16[8,2,576,128]{3,2,1,0:T(8,128)(2,1)S(1)} async-done(((bf16[8,2,576,128]{3,2,1,0:T(8,128)(2,1)}), bf16[8,2,576,128]{3,2,1,0:T(8,128)(2,1)S(1)}, u32[]{:S(2)}, u32[]{:S(2)}) %all-to-all-start.7) | async-done | bytes 2359328 | tf_op jit(solution)/shard_map/all_to_all | solution.py:1274
  531.2 8.5 %all-gather.9.cloned.1.call-done.in_ref = bf16[192,12544]{1,0:T(8,128)(2,1)} async-done(((bf16[24,12544]{1,0:T(8,128)(2,1)}), bf16[192,12544]{1,0:T(8,128)(2,1)}) %all-gather.9.cloned.1.call-update) | async-done | bytes 4816912 | tf_op jit(solution)/shard_map/all_gather | solution.py:1295
  539.7 6.4 %finish.1 = (f32[192,2304]{1,0:T(8,128)}, f32[192,768]{1,0:T(8,128)}, f32[192,768]{1,0:T(8,128)}, f32[192,1536]{1,0:T(8,128)}, f32[768,768]{1,0:T(8,128)}, /*ind...) custom-call(bf16[192,12544]{1,0:T(8,128)(2,1)} %all-gather.9.cloned.1.call-, ...), custom_call_target="tpu_custom_call" | custom-call | flops 6000000000 | bytes 6000000 | tf_op jit(solution)/shard_map/finish/pallas_call | solution.py:556
  (231 shorter events, 107.8 us)
Async XLA Ops:
  7.2 56.3 %all-gather.11.cloned.1.call-start = ((), (), s32[]{:S(2)}) async-start(), calls=%async_computation.14 | async-start | bytes 1474560 | tf_op jit(solution)/shard_map/all_gather | solution.py:1085
  9.2 103.9 %all-gather.13.cloned.1.call-start = ((), (), s32[]{:S(2)}) async-start(), calls=%async_computation.15 | async-start | bytes 1474560 | tf_op jit(solution)/shard_map/all_gather | solution.py:1085
  11.2 204.3 %all-gather.7.cloned.1.call-start = ((), (), s32[]{:S(2)}) async-start(), calls=%async_computation.10 | async-start | bytes 14598144 | tf_op jit(solution)/shard_map/all_gather | solution.py:1115
  16.2 35.8 %all-to-all-start = ((bf16[4,104,576]{2,1,0:T(8,128)(2,1)}), bf16[4,104,576]{2,1,0:T(8,128)(2,1)S(1)}, u32[]{:S(2)}, u32[]{:S(2)}) async-start(bf16[4,104,576]{2,1,0:T(8,128)(2,1)} %broadcast_in_dim.49), calls=%async_computation | async-start | bytes 1064960 | tf_op jit(solution)/shard_map/all_to_all | solution.py:1067
  22.5 29.7 %collective-permute-start.3 = (bf16[4,128,768]{2,1,0:T(8,128)(2,1)S(1)}, bf16[4,128,768]{2,1,0:T(8,128)(2,1)S(1)}, u32[]{:S(2)}, u32[]{:S(2)}) collective-permute-start(bf16[4,128,768]{2,1,0:T(8,128)(2,1)S(1)} %bitcast.159), channel_id=1, source_target_pairs={{0,6},{1,7},{2,0},{3,1},{4,2},{5,3},{6,4},{7,5},{8,14},{9,15},{10,... | collective-permute-start | bytes 2359304 | tf_op jit(solution)/shard_map/ppermute | solution.py:1000
  25.0 35.6 %collective-permute-start.2 = (bf16[4,128,768]{2,1,0:T(8,128)(2,1)S(1)}, bf16[4,128,768]{2,1,0:T(8,128)(2,1)S(1)}, u32[]{:S(2)}, u32[]{:S(2)}) collective-permute-start(bf16[4,128,768]{2,1,0:T(8,128)(2,1)S(1)} %bitcast.160), channel_id=1, source_target_pairs={{0,4},{1,5},{2,6},{3,7},{4,0},{5,1},{6,2},{7,3},{8,12},{9,13},{10,... | collective-permute-start | bytes 2359304 | tf_op jit(solution)/shard_map/ppermute | solution.py:1000
  25.5 35.1 %collective-permute-start.1 = (bf16[4,128,768]{2,1,0:T(8,128)(2,1)S(1)}, bf16[4,128,768]{2,1,0:T(8,128)(2,1)}, u32[]{:S(2)}, u32[]{:S(2)}) collective-permute-start(bf16[4,128,768]{2,1,0:T(8,128)(2,1)S(1)} %bitcast.161), channel_id=1, source_target_pairs={{0,2},{1,3},{2,4},{3,5},{4,6},{5,7},{6,0},{7,1},{8,10},{9,11},{10,... | collective-permute-start | bytes 2359304 | tf_op jit(solution)/shard_map/ppermute | solution.py:1000
  62.1 13.8 %collective-permute-start.4 = (bf16[4,2,128,768]{3,2,1,0:T(8,128)(2,1)S(1)}, bf16[4,2,128,768]{3,2,1,0:T(8,128)(2,1)}, u32[]{:S(2)}, u32[]{:S(2)}) collective-permute-start(bf16[4,2,128,768]{3,2,1,0:T(8,128)(2,1)S(1)} %pad_maximum_fusion), channel_id=1, source_target_pairs={{0,1},{1,0},{2,3},{3,2},{4,5},{5,4},{6,7},{7,6},{8,9},{9,8},{10,11... | collective-permute-start | bytes 4718600 | tf_op jit(solution)/shard_map/ppermute | solution.py:1000
  73.4 20.5 %collective-permute-start.8 = (bf16[2,192,1024]{2,1,0:T(8,128)(2,1)S(1)}, bf16[2,192,1024]{2,1,0:T(8,128)(2,1)}, u32[]{:S(2)}, u32[]{:S(2)}) collective-permute-start(bf16[2,192,1024]{2,1,0:T(8,128)(2,1)S(1)} %get-tuple-element.139), channel_id=1, source_target_pairs={{0,6},{1,7},{2,0},{3,1},{4,2},{5,3},{6,4},{7,5},{8,14},{9,15},{10,... | collective-permute-start | bytes 2359304 | tf_op jit(solution)/shard_map/ppermute | solution.py:1000
  73.9 28.6 %collective-permute-start.7 = (bf16[2,192,1024]{2,1,0:T(8,128)(2,1)S(1)}, bf16[2,192,1024]{2,1,0:T(8,128)(2,1)}, u32[]{:S(2)}, u32[]{:S(2)}) collective-permute-start(bf16[2,192,1024]{2,1,0:T(8,128)(2,1)S(1)} %get-tuple-element.140), channel_id=1, source_target_pairs={{0,4},{1,5},{2,6},{3,7},{4,0},{5,1},{6,2},{7,3},{8,12},{9,13},{10,... | collective-permute-start | bytes 2359304 | tf_op jit(solution)/shard_map/ppermute | solution.py:1000
  75.0 38.1 %collective-permute-start.6 = (bf16[2,192,1024]{2,1,0:T(8,128)(2,1)S(1)}, bf16[2,192,1024]{2,1,0:T(8,128)(2,1)}, u32[]{:S(2)}, u32[]{:S(2)}) collective-permute-start(bf16[2,192,1024]{2,1,0:T(8,128)(2,1)S(1)} %get-tuple-element.141), channel_id=1, source_target_pairs={{0,2},{1,3},{2,4},{3,5},{4,6},{5,7},{6,0},{7,1},{8,10},{9,11},{10,... | collective-permute-start | bytes 2359304 | tf_op jit(solution)/shard_map/ppermute | solution.py:1000
  115.4 33.6 %collective-permute-start.10 = (bf16[2,192,1024]{2,1,0:T(8,128)(2,1)}, bf16[2,192,1024]{2,1,0:T(8,128)(2,1)}, u32[]{:S(2)}, u32[]{:S(2)}) collective-permute-start(bf16[2,192,1024]{2,1,0:T(8,128)(2,1)} %get-tuple-element.142.rest_5_.rest_0_), channel_id=1, source_target_pairs={{0,1},{1,0},{2,3},{3,2},{4,5},{5,4},{6,7},{7,6},{8,9},{9,8},{10,11... | collective-permute-start | bytes 2359304 | tf_op jit(solution)/shard_map/ppermute | solution.py:1000
  115.9 22.2 %all-to-all-start.1 = ((bf16[8,2,192,128]{3,2,1,0:T(8,128)(2,1)}), bf16[8,2,192,128]{3,2,1,0:T(8,128)(2,1)}, u32[]{:S(2)}, u32[]{:S(2)}) async-start(bf16[8,2,192,128]{3,2,1,0:T(8,128)(2,1)} %get-tuple-element.66), calls=%async_computation.1 | async-start | bytes 1572864 | tf_op jit(solution)/shard_map/all_to_all | solution.py:1174
  120.9 28.1 %collective-permute-start.13 = (bf16[2,192,1024]{2,1,0:T(8,128)(2,1)}, bf16[2,192,1024]{2,1,0:T(8,128)(2,1)S(1)}, u32[]{:S(2)}, u32[]{:S(2)}) collective-permute-start(bf16[2,192,1024]{2,1,0:T(8,128)(2,1)} %collective-permute-done.8.rest_3_), channel_id=1, source_target_pairs={{0,1},{1,0},{2,3},{3,2},{4,5},{5,4},{6,7},{7,6},{8,9},{9,8},{10,11... | collective-permute-start | bytes 2359304 | tf_op jit(solution)/shard_map/ppermute | solution.py:1000
  121.5 27.6 %collective-permute-start.12 = (bf16[2,192,1024]{2,1,0:T(8,128)(2,1)}, bf16[2,192,1024]{2,1,0:T(8,128)(2,1)}, u32[]{:S(2)}, u32[]{:S(2)}) collective-permute-start(bf16[2,192,1024]{2,1,0:T(8,128)(2,1)} %collective-permute-done.7.rest_2_), channel_id=1, source_target_pairs={{0,1},{1,0},{2,3},{3,2},{4,5},{5,4},{6,7},{7,6},{8,9},{9,8},{10,11... | collective-permute-start | bytes 2359304 | tf_op jit(solution)/shard_map/ppermute | solution.py:1000
  121.5 27.5 %collective-permute-start.11 = (bf16[2,192,1024]{2,1,0:T(8,128)(2,1)}, bf16[2,192,1024]{2,1,0:T(8,128)(2,1)}, u32[]{:S(2)}, u32[]{:S(2)}) collective-permute-start(bf16[2,192,1024]{2,1,0:T(8,128)(2,1)} %collective-permute-done.6.rest_1_), channel_id=1, source_target_pairs={{0,1},{1,0},{2,3},{3,2},{4,5},{5,4},{6,7},{7,6},{8,9},{9,8},{10,11... | collective-permute-start | bytes 2359304 | tf_op jit(solution)/shard_map/ppermute | solution.py:1000
  144.2 11.5 %all-to-all-start.2 = ((bf16[4,4,192,128]{3,2,1,0:T(8,128)(2,1)}), bf16[4,4,192,128]{3,2,1,0:T(8,128)(2,1)S(1)}, u32[]{:S(2)}, u32[]{:S(2)}) async-start(bf16[4,4,192,128]{3,2,1,0:T(8,128)(2,1)} %get-tuple-element.68), calls=%async_computation.2 | async-start | bytes 1572864 | tf_op jit(solution)/shard_map/all_to_all | solution.py:995
  203.9 11.5 %all-to-all-start.3 = ((bf16[4,4,192,128]{3,2,1,0:T(8,128)(2,1)}), bf16[4,4,192,128]{3,2,1,0:T(8,128)(2,1)S(1)}, u32[]{:S(2)}, u32[]{:S(2)}) async-start(bf16[4,4,192,128]{3,2,1,0:T(8,128)(2,1)} %get-tuple-element.72), calls=%async_computation.3 | async-start | bytes 1572864 | tf_op jit(solution)/shard_map/all_to_all | solution.py:995
  207.5 123.3 %reduce-scatter.3.cloned.1.call-start = ((), (), s32[]{:S(2)}) async-start(), calls=%async_computation.11 | async-start | bytes 11943936 | tf_op jit(solution)/shard_map/reduce_scatter | solution.py:1209
  332.0 12.6 %collective-permute-start.15 = (bf16[24,6912]{1,0:T(8,128)(2,1)S(1)}, bf16[24,6912]{1,0:T(8,128)(2,1)S(1)}, u32[]{:S(2)}, u32[]{:S(2)}) collective-permute-start(bf16[24,6912]{1,0:T(8,128)(2,1)S(1)} %get-tuple-element.146), channel_id=1, source_target_pairs={{0,8},{8,16},{16,24},{24,0},{1,9},{9,17},{17,25},{25,1},{2,10},{10... | collective-permute-start | bytes 995336 | tf_op jit(solution)/shard_map/ppermute | solution.py:1020
  333.5 16.4 %collective-permute-start.17 = (bf16[24,6912]{1,0:T(8,128)(2,1)S(1)}, bf16[24,6912]{1,0:T(8,128)(2,1)S(1)}, u32[]{:S(2)}, u32[]{:S(2)}) collective-permute-start(bf16[24,6912]{1,0:T(8,128)(2,1)S(1)} %get-tuple-element.147), channel_id=1, source_target_pairs={{0,24},{8,0},{16,8},{24,16},{1,25},{9,1},{17,9},{25,17},{2,26},{10... | collective-permute-start | bytes 995336 | tf_op jit(solution)/shard_map/ppermute | solution.py:1020
  335.9 28.9 %collective-permute-start.16 = (bf16[24,6912]{1,0:T(8,128)(2,1)S(1)}, bf16[24,6912]{1,0:T(8,128)(2,1)}, u32[]{:S(2)}, u32[]{:S(2)}) collective-permute-start(bf16[24,6912]{1,0:T(8,128)(2,1)S(1)} %get-tuple-element.148), channel_id=1, source_target_pairs={{0,16},{8,24},{16,0},{24,8},{1,17},{9,25},{17,1},{25,9},{2,18},{10... | collective-permute-start | bytes 995336 | tf_op jit(solution)/shard_map/ppermute | solution.py:1020
  339.0 27.1 %collective-permute-start.20 = (bf16[2,192,1024]{2,1,0:T(8,128)(2,1)}, bf16[2,192,1024]{2,1,0:T(8,128)(2,1)S(1)}, u32[]{:S(2)}, u32[]{:S(2)}) collective-permute-start(bf16[2,192,1024]{2,1,0:T(8,128)(2,1)} %get-tuple-element.133), channel_id=1, source_target_pairs={{0,6},{1,7},{2,0},{3,1},{4,2},{5,3},{6,4},{7,5},{8,14},{9,15},{10,... | collective-permute-start | bytes 2359304 | tf_op jit(solution)/shard_map/ppermute | solution.py:1000
  340.4 35.0 %collective-permute-start.19 = (bf16[2,192,1024]{2,1,0:T(8,128)(2,1)S(1)}, bf16[2,192,1024]{2,1,0:T(8,128)(2,1)S(1)}, u32[]{:S(2)}, u32[]{:S(2)}) collective-permute-start(bf16[2,192,1024]{2,1,0:T(8,128)(2,1)S(1)} %copy-done.11), channel_id=1, source_target_pairs={{0,4},{1,5},{2,6},{3,7},{4,0},{5,1},{6,2},{7,3},{8,12},{9,13},{10,... | collective-permute-start | bytes 2359304 | tf_op jit(solution)/shard_map/ppermute | solution.py:1000
  344.6 30.9 %collective-permute-start.18 = (bf16[2,192,1024]{2,1,0:T(8,128)(2,1)S(1)}, bf16[2,192,1024]{2,1,0:T(8,128)(2,1)S(1)}, u32[]{:S(2)}, u32[]{:S(2)}) collective-permute-start(bf16[2,192,1024]{2,1,0:T(8,128)(2,1)S(1)} %copy-done.10), channel_id=1, source_target_pairs={{0,2},{1,3},{2,4},{3,5},{4,6},{5,7},{6,0},{7,1},{8,10},{9,11},{10,... | collective-permute-start | bytes 2359304 | tf_op jit(solution)/shard_map/ppermute | solution.py:1000
  377.2 13.6 %all-to-all-start.5 = ((bf16[4,4,192,128]{3,2,1,0:T(8,128)(2,1)}), bf16[4,4,192,128]{3,2,1,0:T(8,128)(2,1)S(1)}, u32[]{:S(2)}, u32[]{:S(2)}) async-start(bf16[4,4,192,128]{3,2,1,0:T(8,128)(2,1)} %get-tuple-element.83), calls=%async_computation.6 | async-start | bytes 1572864 | tf_op jit(solution)/shard_map/all_to_all | solution.py:995
  380.7 74.8 %reduce-scatter.5.cloned.1.call-start = ((), (), s32[]{:S(2)}) async-start(), calls=%async_computation.12 | async-start | bytes 5529600 | tf_op jit(solution)/shard_map/reduce_scatter | solution.py:1209
  401.6 16.1 %all-to-all-start.6 = ((bf16[8,2,192,128]{3,2,1,0:T(8,128)(2,1)}), bf16[8,2,192,128]{3,2,1,0:T(8,128)(2,1)S(1)}, u32[]{:S(2)}, u32[]{:S(2)}) async-start(bf16[8,2,192,128]{3,2,1,0:T(8,128)(2,1)} %get-tuple-element.97), calls=%async_computation.7 | async-start | bytes 1572864 | tf_op jit(solution)/shard_map/all_to_all | solution.py:1262
  405.2 134.6 %all-gather.9.cloned.1.call-start = ((), (), s32[]{:S(2)}) async-start(), calls=%async_computation.13 | async-start | bytes 5419008 | tf_op jit(solution)/shard_map/all_gather | solution.py:1295
  458.4 13.7 %collective-permute-start.24 = (bf16[24,5632]{1,0:T(8,128)(2,1)S(1)}, bf16[24,5632]{1,0:T(8,128)(2,1)S(1)}, u32[]{:S(2)}, u32[]{:S(2)}) collective-permute-start(bf16[24,5632]{1,0:T(8,128)(2,1)S(1)} %get-tuple-element.150), channel_id=1, source_target_pairs={{0,24},{8,0},{16,8},{24,16},{1,25},{9,1},{17,9},{25,17},{2,26},{10... | collective-permute-start | bytes 811016 | tf_op jit(solution)/shard_map/ppermute | solution.py:1020
  460.7 23.6 %collective-permute-start.23 = (bf16[24,5632]{1,0:T(8,128)(2,1)S(1)}, bf16[24,5632]{1,0:T(8,128)(2,1)S(1)}, u32[]{:S(2)}, u32[]{:S(2)}) collective-permute-start(bf16[24,5632]{1,0:T(8,128)(2,1)S(1)} %get-tuple-element.151), channel_id=1, source_target_pairs={{0,16},{8,24},{16,0},{24,8},{1,17},{9,25},{17,1},{25,9},{2,18},{10... | collective-permute-start | bytes 811016 | tf_op jit(solution)/shard_map/ppermute | solution.py:1020
  485.3 40.6 %all-to-all-start.7 = ((bf16[8,2,576,128]{3,2,1,0:T(8,128)(2,1)}), bf16[8,2,576,128]{3,2,1,0:T(8,128)(2,1)S(1)}, u32[]{:S(2)}, u32[]{:S(2)}) async-start(bf16[8,2,576,128]{3,2,1,0:T(8,128)(2,1)} %get-tuple-element.102), calls=%async_computation.9 | async-start | bytes 4718592 | tf_op jit(solution)/shard_map/all_to_all | solution.py:1274
  (40 other events, 362.0 us)
Sparse Core Ops, SparseCore 0:
  10.2 44.7 all-gather.10
  57.1 29.2 all-gather.12
  89.9 115.4 all-gather.6
  248.0 82.6 reduce-scatter.2
  401.7 53.8 reduce-scatter.4
  485.5 54.2 all-gather.8

commit v4 on v3

--- a/solution.py
+++ b/solution.py
@@ -18,6 +18,7 @@
 masked_score = -2e30
 start_max = -1e30
 score_scale = HEAD_DIM ** (-0.5)
+forward_tile = 512
 key_tile = 256
 row_tile = 256
 vmem_bytes = 56 * 2**20
@@ -131,29 +132,38 @@
     for first in range(0, length, rows):
         part = dot_nn(x_ref[slot, first : first + rows, :], w_ref[...]) + bias_ref[0:1, :]
         proj_ref[:, first : first + rows] = part.astype(half).T
-    for head in range(GROUP_HEADS):
-        feats = head_feats(head)
-        for first in range(0, length, rows):
-            upto = first + rows
-            cols = slice(first, upto)
-            q_low = proj_ref[feats, cols] * jnp.asarray(score_scale, half)
-            k_low = proj_ref[head_feats(head, 1), :upto]
-            v_low = proj_ref[head_feats(head, 2), :upto]
-            scores = dot_tn(k_low, q_low)
-            key_pos = lax.broadcasted_iota(jnp.int32, scores.shape, 0)
-            row_pos = first + lax.broadcasted_iota(jnp.int32, scores.shape, 1)
-            scores = jnp.where(key_pos <= row_pos, scores, masked_score)
-            top = jnp.max(scores, axis=0, keepdims=True)
-            weight = jnp.exp(scores - top)
-            total = jnp.sum(weight, axis=0, keepdims=True)
-            mix = dot_nn(v_low, weight.astype(half)) / total
-            mix_ref[0, feats, cols] = mix
-            mix_low = mix.astype(half)
-            for place in range(rows // rows_dev):
-                att_ref[first // rows_dev + place, 0, feats, :] = mix_low[
-                    :, place * rows_dev : (place + 1) * rows_dev
-                ]
-            lse_ref[0, head : head + 1, cols] = top + jnp.log(total)
+    def score(head, first):
+        upto = first + rows
+        q_low = proj_ref[head_feats(head), first:upto] * jnp.asarray(score_scale, half)
+        scores = dot_tn(proj_ref[head_feats(head, 1), :upto], q_low)
+        key_pos = lax.broadcasted_iota(jnp.int32, scores.shape, 0)
+        row_pos = first + lax.broadcasted_iota(jnp.int32, scores.shape, 1)
+        return jnp.where(key_pos <= row_pos, scores, masked_score)
+
+    def store(head, first, weight_low, top, total):
+        feats, cols = head_feats(head), slice(first, first + rows)
+        mix = dot_nn(proj_ref[head_feats(head, 2), : first + rows], weight_low) / total
+        mix_ref[0, feats, cols] = mix
+        mix_low = mix.astype(half)
+        for place in range(rows // rows_dev):
+            att_ref[first // rows_dev + place, 0, feats, :] = mix_low[
+                :, place * rows_dev : (place + 1) * rows_dev
+            ]
+        lse_ref[0, head : head + 1, cols] = top + jnp.log(total)
+
+    parts = [(head, first) for first in range(0, length, rows) for head in range(GROUP_HEADS)]
+    ahead, waiting = score(*parts[0]), None
+    for i, part in enumerate(parts):
+        scores = ahead
+        if i + 1 < len(parts):
+            ahead = score(*parts[i + 1])
+        top = jnp.max(scores, axis=0, keepdims=True)
+        weight = jnp.exp(scores - top)
+        total = jnp.sum(weight, axis=0, keepdims=True)
+        if waiting is not None:
+            store(*waiting)
+        waiting = (*part, weight.astype(half), top, total)
+    store(*waiting)
 
 
 def self_forward(places, w_part, bias, pieces, n_seq, *after):
@@ -212,27 +222,38 @@
     rows = min(row_tile, length)
     dk_ref[...] = jnp.zeros_like(dk_ref)
     dv_ref[...] = jnp.zeros_like(dv_ref)
-    for head in range(GROUP_HEADS):
-        feats = head_feats(head)
-        for first in range(0, length, rows):
-            upto = first + rows
-            cols = slice(first, upto)
-            places = range(first // rows_dev, upto // rows_dev)
-            q_low = proj_ref[feats, cols] * jnp.asarray(score_scale, half)
-            k_low = proj_ref[head_feats(head, 1), :upto]
-            v_low = proj_ref[head_feats(head, 2), :upto]
-            g_low = jnp.concatenate([grad_ref[place, 0, feats, :] for place in places], axis=1)
-            delta = jnp.sum(g_low.astype(f32) * mix_ref[0, feats, cols], axis=0, keepdims=True)
-            scores = dot_tn(k_low, q_low)
-            key_pos = lax.broadcasted_iota(jnp.int32, scores.shape, 0)
-            row_pos = first + lax.broadcasted_iota(jnp.int32, scores.shape, 1)
-            scores = jnp.where(key_pos <= row_pos, scores, masked_score)
-            prob = jnp.exp(scores - lse_ref[0, head : head + 1, cols])
-            grad_prob = dot_tn(v_low, g_low)
-            grad_score = (prob * (grad_prob - delta)).astype(half)
-            dv_ref[feats, :upto] += dot_nt(g_low, prob.astype(half))
-            dk_ref[feats, :upto] += dot_nt(q_low, grad_score)
-            dproj_ref[feats, cols] = (dot_nn(k_low, grad_score) * score_scale).astype(half)
+    def products(head, first):
+        upto = first + rows
+        feats, cols = head_feats(head), slice(first, upto)
+        places = range(first // rows_dev, upto // rows_dev)
+        q_low = proj_ref[feats, cols] * jnp.asarray(score_scale, half)
+        g_low = jnp.concatenate([grad_ref[place, 0, feats, :] for place in places], axis=1)
+        delta = jnp.sum(g_low.astype(f32) * mix_ref[0, feats, cols], axis=0, keepdims=True)
+        scores = dot_tn(proj_ref[head_feats(head, 1), :upto], q_low)
+        key_pos = lax.broadcasted_iota(jnp.int32, scores.shape, 0)
+        row_pos = first + lax.broadcasted_iota(jnp.int32, scores.shape, 1)
+        scores = jnp.where(key_pos <= row_pos, scores, masked_score)
+        return scores, dot_tn(proj_ref[head_feats(head, 2), :upto], g_low), q_low, g_low, delta
+
+    def add(head, first, q_low, g_low, prob_low, grad_score):
+        feats, upto = head_feats(head), first + rows
+        dv_ref[feats, :upto] += dot_nt(g_low, prob_low)
+        dk_ref[feats, :upto] += dot_nt(q_low, grad_score)
+        grad_query = dot_nn(proj_ref[head_feats(head, 1), :upto], grad_score) * score_scale
+        dproj_ref[feats, first:upto] = grad_query.astype(half)
+
+    parts = [(head, first) for first in range(0, length, rows) for head in range(GROUP_HEADS)]
+    ahead, waiting = products(*parts[0]), None
+    for i, (head, first) in enumerate(parts):
+        scores, grad_prob, q_low, g_low, delta = ahead
+        if i + 1 < len(parts):
+            ahead = products(*parts[i + 1])
+        prob = jnp.exp(scores - lse_ref[0, head : head + 1, first : first + rows])
+        grad_score = (prob * (grad_prob - delta)).astype(half)
+        if waiting is not None:
+            add(*waiting)
+        waiting = (head, first, q_low, g_low, prob.astype(half), grad_score)
+    add(*waiting)
     dproj_ref[GROUP_FEATS : 2 * GROUP_FEATS, :] = dk_ref[...].astype(half)
     dproj_ref[2 * GROUP_FEATS :, :] = dv_ref[...].astype(half)
     for place in range(n_seq):
@@ -591,9 +612,9 @@
         copy.wait()
 
 
-def tiles_of(low, high):
-    first = low // key_tile
-    return first, jnp.where(high > low, (high + key_tile - 1) // key_tile, first)
+def tiles_of(low, high, tile):
+    first = low // tile
+    return first, jnp.where(high > low, (high + tile - 1) // tile, first)
 
 
 def cross_forward_kernel(low_ref, high_ref, place_ref, q_ref, *rest):
@@ -613,28 +634,42 @@
 
     def step(tile, carry):
         tops, totals = carry
-        start = pl.multiple_of(tile * key_tile, key_tile)
-        key_pos = start + lax.broadcasted_iota(jnp.int32, (key_tile, rows), 0)
+        start = pl.multiple_of(tile * forward_tile, forward_tile)
+        keys = pl.ds(start, forward_tile)
+        key_pos = start + lax.broadcasted_iota(jnp.int32, (forward_tile, rows), 0)
         counted = (key_pos >= low) & (key_pos < high)
+
+        def score(head):
+            feats = head_feats(head)
+            return jnp.where(counted, dot_tn(kv_ref[0, feats, keys], q_low[feats]), masked_score)
+
+        def add(head, weight_low, rescale):
+            feats = head_feats(head)
+            mixed = dot_nn(kv_ref[1, feats, keys], weight_low)
+            acc_ref[feats, :] = acc_ref[feats, :] * rescale + mixed
+
         new_tops, new_totals = [], []
+        ahead, waiting = score(0), None
         for head in range(GROUP_HEADS):
-            feats = head_feats(head)
-            k_low = kv_ref[0, feats, pl.ds(start, key_tile)]
-            v_low = kv_ref[1, feats, pl.ds(start, key_tile)]
-            scores = jnp.where(counted, dot_tn(k_low, q_low[feats]), masked_score)
+            scores = ahead
+            if head + 1 < GROUP_HEADS:
+                ahead = score(head + 1)
             top = jnp.maximum(tops[head], jnp.max(scores, axis=0, keepdims=True))
             weight = jnp.exp(scores - top)
             rescale = jnp.exp(tops[head] - top)
             new_totals.append(totals[head] * rescale + jnp.sum(weight, axis=0, keepdims=True))
             new_tops.append(top)
-            acc_ref[feats, :] = acc_ref[feats, :] * rescale + dot_nn(v_low, weight.astype(half))
+            if waiting is not None:
+                add(*waiting)
+            waiting = (head, weight.astype(half), rescale)
+        add(*waiting)
         return (tuple(new_tops), tuple(new_totals))
 
     init = (
         tuple(jnp.full((1, rows), start_max, f32) for _ in range(GROUP_HEADS)),
         tuple(jnp.zeros((1, rows), f32) for _ in range(GROUP_HEADS)),
     )
-    tops, totals = lax.fori_loop(*tiles_of(low, high), step, init)
+    tops, totals = lax.fori_loop(*tiles_of(low, high, forward_tile), step, init)
     for head in range(GROUP_HEADS):
         feats = head_feats(head)
         live = totals[head] > 0
@@ -675,7 +710,7 @@
             jax.ShapeDtypeStruct((slots, GROUP_HEADS, rows), f32),
         ],
         compiler_params=pltpu.CompilerParams(vmem_limit_bytes=vmem_bytes),
-        cost_estimate=cost_of(45),
+        cost_estimate=cost_of(33),
         name="cross_forward",
     )(low, high, places, queries, *pieces)
 
@@ -715,24 +750,36 @@
         inside = pl.multiple_of(tile % tiles_dev * key_tile, key_tile)
         key_pos = start + lax.broadcasted_iota(jnp.int32, (key_tile, rows), 0)
         counted = (key_pos >= low) & (key_pos < high)
+        keys = pl.ds(start, key_tile)
+
+        def products(head):
+            feats = head_feats(head)
+            scores = dot_tn(kv_ref[0, feats, keys], q_low[feats])
+            return scores, dot_tn(kv_ref[1, feats, keys], g_low[feats])
+
+        def add(head, prob_low, grad_score):
+            feats = head_feats(head)
+            own_keys = (feats, pl.ds(inside, key_tile))
+            grad_values = dot_nt(prob_low, g_low[feats]).T
+            grad_keys = dot_nt(grad_score, q_low[feats]).T
+            dkv_ref[(turn, group, 1, *own_keys)] += grad_values.astype(half)
+            dkv_ref[(turn, group, 0, *own_keys)] += grad_keys.astype(half)
+            acc_ref[feats, :] += dot_nn(kv_ref[0, feats, keys], grad_score)
+
+        ahead, waiting = products(0), None
         for head in range(GROUP_HEADS):
-            feats = head_feats(head)
-            k_low = kv_ref[0, feats, pl.ds(start, key_tile)]
-            v_low = kv_ref[1, feats, pl.ds(start, key_tile)]
-            scores = jnp.where(counted, dot_tn(k_low, q_low[feats]), masked_score)
-            prob = jnp.exp(scores - lse[head])
-            grad_prob = dot_tn(v_low, g_low[feats])
+            scores, grad_prob = ahead
+            if head + 1 < GROUP_HEADS:
+                ahead = products(head + 1)
+            prob = jnp.exp(jnp.where(counted, scores, masked_score) - lse[head])
             grad_score = (prob * (grad_prob - delta[head])).astype(half)
-            dkv_ref[turn, group, 1, feats, pl.ds(inside, key_tile)] += dot_nt(
-                g_low[feats], prob.astype(half)
-            ).astype(half)
-            dkv_ref[turn, group, 0, feats, pl.ds(inside, key_tile)] += dot_nt(
-                q_low[feats], grad_score
-            ).astype(half)
-            acc_ref[feats, :] += dot_nn(k_low, grad_score)
+            if waiting is not None:
+                add(*waiting)
+            waiting = (head, prob.astype(half), grad_score)
+        add(*waiting)
         return carry
 
-    lax.fori_loop(*tiles_of(low, high), step, 0)
+    lax.fori_loop(*tiles_of(low, high, key_tile), step, 0)
     dq_low = (acc_ref[...] * score_scale).astype(half)
     for i in range(HEAD_GROUPS):
         dq_ref[i, 0] = dq_low[:, i * rows_dev : (i + 1) * rows_dev]
@@ -780,7 +827,7 @@
         ]
         + [jax.ShapeDtypeStruct(grad_shape[1:], half)] * grad_shape[0],
         compiler_params=pltpu.CompilerParams(vmem_limit_bytes=vmem_bytes),
-        cost_estimate=cost_of(53),
+        cost_estimate=cost_of(49),
         name="cross_backward",
     )(low, high, places, queries, grad_mix, mix, lse, *pieces, *after)
 
@@ -1236,10 +1283,8 @@
             for piece in grad_kv
         ).astype(half)
         grad_kv_own.append(rotate_heads(total, turn) if turn else total)
-    late_own = own_rows(lax.optimization_barrier((late_blocks, grad_kv_own[0]))[0])
-    grad_query_send, late_own, *grad_kv_own = lax.optimization_barrier(
-        (grad_query_send, late_own, *grad_kv_own)
-    )
+    late_own = own_rows(lax.optimization_barrier((late_blocks, grad_kv_own[2]))[0])
+    grad_query_send, *grad_kv_own = lax.optimization_barrier((grad_query_send, *grad_kv_own))
     mem_packed, grad_mem_kv, value_rows = memory_backward(
         n_doc, n_seq, group_places, mem_low, grad_kv_own
     )
@@ -1269,6 +1314,7 @@
         self_lse,
         x_pieces,
         packed,
+        late_own,
     )
     grad_proj_send = lax.optimization_barrier((grad_proj_send, over_seq))[0]
     grad_proj_got = lax.all_to_all(grad_proj_send, "seq", 0, 0, tiled=True)

time: 564 us -> 544 us (0.965)
  Pallas kernels: 200 us -> 176 us
    ppermute x19, waiting for transfers between devices: 46.5 us -> 73.5 us  [rotate_both(): lax.ppermute(block, 'seq', [(h * spread + m, (h + turn_h) % HEAD_GROUPS *...]
    reduce_scatter x2, waiting for transfers between devices: 18.6 us -> 0.04 us  [sum_over_seq(): return lax.psum_scatter(packed, 'seq', scatter_dimension=0, tiled=True)]
    pallas_call x1, Pallas kernels: 47.3 us -> 34.1 us  [cross_forward(): pl.pallas_call(cross_forward_kernel, grid_spec=pltpu.PrefetchScalarGridSp...]
    all_to_all x1, waiting for transfers between devices: 12.2 us -> 0.01 us  [body(): grad_self_part = lax.all_to_all(grad_att_send, 'seq', 0, 0, tiled=True)]
  transfers between devices with their start and end apart: 38 -> 38, of which waited for: 23 -> 23; matrix products, arithmetic and copies ran while one was open for 9% -> 10% of each run, Pallas kernels for 27% -> 26%
where the time goes in v4:
time: 544 us; the launch traced here: 536 us
  waiting for transfers between devices  214 us (39%)
  Pallas kernels  176 us (32%)
  starting transfers between devices  49.1 us (9%)
  local copies, waits for them, and re-layouts  37.1 us (7%)
  other arithmetic  18.8 us (3%)
  between operations  16.1 us (3%)
  blocking collectives  15.1 us (3%)
  matrix products  9.53 us (2%)
    ppermute x19, waiting for transfers between devices, rotate_both(): lax.ppermute(block, 'seq', [(h * spread + m, (h + turn_h) % HEAD_GROUPS *...  73.5 us
    pallas_call x1, Pallas kernels, cross_backward(): pl.pallas_call(cross_backward_kernel, grid_spec=pltpu.PrefetchScalarGridS...  49 us
    ppermute x6, waiting for transfers between devices, rotate_doc(): lax.ppermute(block, 'doc', [(d, (d + turn) % n_doc) for d in range(n_doc)])  45.6 us
    pallas_call x1, Pallas kernels, cross_forward(): pl.pallas_call(cross_forward_kernel, grid_spec=pltpu.PrefetchScalarGridSp...  34.1 us
    pallas_call x1, Pallas kernels, middle(): pl.pallas_call(partial(middle_kernel, n_doc, n_seq), in_specs=[vmem] * 5...  31.5 us
    all_to_all x1, waiting for transfers between devices, body(): grad_proj_got = lax.all_to_all(grad_proj_send, 'seq', 0, 0, tiled=True)  28 us
    all_to_all x1, waiting for transfers between devices, body(): lax.all_to_all(first_piece, 'doc', 0, 0, tiled=True)  25.3 us
    pallas_call x1, Pallas kernels, self_backward(): pl.pallas_call(partial(self_backward_kernel, n_doc), grid_spec=pltpu.Pref...  18.2 us
  transfers between devices with their start and end apart: 38, of which 23 were waited for; matrix products, arithmetic and copies ran while one was open for 10% of the time, Pallas kernels for 26%

profile of v4, /device:TPU:0, one launch (start us, length us, event | category | flops | bytes accessed | tf_op | source)
XLA Modules:
  0.0 535.5 jit_solution(4246862682526965915)
XLA Ops:
  16.2 6.3 %all-to-all-start = ((bf16[4,104,576]{2,1,0:T(8,128)(2,1)}), bf16[4,104,576]{2,1,0:T(8,128)(2,1)S(1)}, u32[]{:S(2)}, u32[]{:S(2)}) async-start(bf16[4,104,576]{2,1,0:T(8,128)(2,1)} %broadcast_in_dim.49), calls=%async_computation | async-start | bytes 1064960 | tf_op jit(solution)/shard_map/all_to_all | solution.py:1114
  26.7 25.3 %all-to-all-done = bf16[4,104,576]{2,1,0:T(8,128)(2,1)S(1)} async-done(((bf16[4,104,576]{2,1,0:T(8,128)(2,1)}), bf16[4,104,576]{2,1,0:T(8,128)(2,1)S(1)}, u32[]{:S(2)}, u32[]{:S(2)}) %all-to-all-start) | async-done | bytes 479264 | tf_op jit(solution)/shard_map/all_to_all | solution.py:1114
  53.3 7.4 %collective-permute-done.2.rest_2_ = bf16[4,128,768]{2,1,0:T(8,128)(2,1)} collective-permute-done((bf16[4,128,768]{2,1,0:T(8,128)(2,1)S(1)}, bf16[4,128,768]{2,1,0:T(8,128)(2,1)}, u32[]{:S(2)}, u32[]{:S(2)}) %collective-permute-start.2) | collective-permute-done | bytes 786464 | tf_op jit(solution)/shard_map/ppermute | solution.py:1047
  77.8 13.5 %self_forward.1 = (bf16[576,2048]{1,0:T(8,128)(2,1)}, f32[2,192,1024]{2,1,0:T(8,128)}, bf16[8,2,192,128]{3,2,1,0:T(8,128)(2,1)}, f32[2,3,1024]{2,1,0:T(4,128)}) custom-call(s32[8]{0:T(128)} %stack.57.place_ref, bf16[768,576]{1,0:T(8,128)(2,1)} %bitcast.154, f32[1,576]{1,0:T(1,128)} %broadcast_in_dim.53.bias_ref, bf16[4,128,768]{2,1,0:T(8,128)(2,1)} %bitcast.156, ...), custom_call_target="tpu_custom_call" | custom-call | flops 17999998976 | bytes 18000000 | tf_op jit(solution)/shard_map/self_forward/pallas_call | solution.py:173
  91.3 4.5 collective-permute-done.8.rest_3_
  95.8 6.7 %collective-permute-done.7.rest_2_ = bf16[2,192,1024]{2,1,0:T(8,128)(2,1)} collective-permute-done((bf16[2,192,1024]{2,1,0:T(8,128)(2,1)S(1)}, bf16[2,192,1024]{2,1,0:T(8,128)(2,1)}, u32[]{:S(2)}, u32[]{:S(2)}) %collective-permute-start.7) | collective-permute-done | bytes 786464 | tf_op jit(solution)/shard_map/ppermute | solution.py:1047
  102.6 12.5 %collective-permute-done.6.rest_1_ = bf16[2,192,1024]{2,1,0:T(8,128)(2,1)} collective-permute-done((bf16[2,192,1024]{2,1,0:T(8,128)(2,1)S(1)}, bf16[2,192,1024]{2,1,0:T(8,128)(2,1)}, u32[]{:S(2)}, u32[]{:S(2)}) %collective-permute-start.6) | collective-permute-done | bytes 786464 | tf_op jit(solution)/shard_map/ppermute | solution.py:1047
  118.6 4.7 all-to-all-start.1
  126.0 15.4 %all-to-all-done.1.att_ref = bf16[8,2,192,128]{3,2,1,0:T(8,128)(2,1)} async-done(((bf16[8,2,192,128]{3,2,1,0:T(8,128)(2,1)}), bf16[8,2,192,128]{3,2,1,0:T(8,128)(2,1)}, u32[]{:S(2)}, u32[]{:S(2)}) %all-to-all-start.1) | async-done | bytes 786464 | tf_op jit(solution)/shard_map/all_to_all | solution.py:1221
  141.5 6.1 %enter.1 = (f32[512,768]{1,0:T(8,128)}, f32[512,768]{1,0:T(8,128)}, f32[512,128]{1,0:T(8,128)}, bf16[4,4,192,128]{3,2,1,0:T(8,128)(2,1)}) custom-call(bf16[8,2,192,128]{3,2,1,0:T(8,128)(2,1)} %all-to-all-done.1.att_ref, bf16[512,768]{1,0:T(8,128)(2,1)} %bitcast.157, f32[8,768]{1,0:T(8,128)} %select_maximum_fusion.vec_ref, bf16[768,1536]{1,0:T(8,128)(2,1)} %bitcast.141), custom_call_target="tpu_custom_call" | custom-call | flops 6000000000 | bytes 6000000 | tf_op jit(solution)/shard_map/enter/pallas_call | solution.py:363
  152.5 6.5 %all-to-all-done.2.q_ref = bf16[4,4,192,128]{3,2,1,0:T(8,128)(2,1)S(1)} async-done(((bf16[4,4,192,128]{3,2,1,0:T(8,128)(2,1)}), bf16[4,4,192,128]{3,2,1,0:T(8,128)(2,1)S(1)}, u32[]{:S(2)}, u32[]{:S(2)}) %all-to-all-start.2) | async-done | bytes 786464 | tf_op jit(solution)/shard_map/all_to_all | solution.py:1042
  159.9 34.1 %cross_forward.1 = (f32[4,192,512]{2,1,0:T(8,128)}, bf16[4,4,192,128]{3,2,1,0:T(8,128)(2,1)}, f32[4,3,512]{2,1,0:T(4,128)}) custom-call(s32[4]{0:T(128)} %pad_add_fusion.low_ref, s32[4]{0:T(128)} %get-tuple-element.152.high_ref, s32[8]{0:T(128)} %stack.57.place_ref, bf16[4,4,192,128]{3,2,1,0:T(8,128)(2,1)} %copy-done.11, ...), custom_call_target="tpu_custom_call" | custom-call | flops 32999999488 | bytes 33000000 | tf_op jit(solution)/shard_map/cross_forward/pallas_call | solution.py:690
  200.4 5.2 all-to-all-done.3.att_ref
  208.1 31.5 %middle.1 = (bf16[512,768]{1,0:T(8,128)(2,1)}, f32[512,768]{1,0:T(8,128)}, bf16[4,4,192,128]{3,2,1,0:T(8,128)(2,1)}, bf16[8,96,6912]{2,1,0:T(8,128)(2,1)}, f32[8,768]{1,0:T(8,128)}, /*index=5*/f32[1,3072]{1,0:T(1,128)}) custom-call(bf16[4,4,192,128]{3,2,1,0:T(8,128)(2,1)} %copy-done.12, f32[512,768]{1,0:T(8,128)} %get-tuple-element.72.norm_ref, ...), custom_call_target="tpu_custom_call" | custom-call | flops 31000000512 | bytes 31000000 | tf_op jit(solution)/shard_map/middle/pallas_call | solution.py:979
  240.8 15.1 %all_to_all.40.g_ref = bf16[4,4,192,128]{3,2,1,0:T(8,128)(2,1)} all-to-all(bf16[4,4,192,128]{3,2,1,0:T(8,128)(2,1)S(1)} %copy-done.15), channel_id=1, replica_groups={{0,2,4,6},{1,3,5,7},{8,10,12,14},{9,11,13,15},{16,18,20,22},{17,19,21,2..., dimensions={0} | all-to-all | bytes 1572864 | tf_op jit(solution)/shard_map/all_to_all | solution.py:1042
  255.9 49.0 %cross_backward.1 = (bf16[4,4,192,128]{3,2,1,0:T(8,128)(2,1)}, bf16[4,2,192,1024]{3,2,1,0:T(8,128)(2,1)}, bf16[4,2,192,1024]{3,2,1,0:T(8,128)(2,1)}) custom-call(s32[4]{0:T(128)} %pad_add_fusion.low_ref, s32[4]{0:T(128)} %get-tuple-element.152.high_ref, s32[8]{0:T(128)} %stack.57.place_ref, bf16[4,4,192,128]{3,2,1,0:T(8,128)(2,1)} %copy-done.11, ...), custom_call_target="tpu_custom_call" | custom-call | flops 49000001536 | bytes 49000000 | tf_op jit(solution)/shard_map/cross_backward/pallas_call | solution.py:805
  305.0 5.9 %collective-permute-done.14 = bf16[4,2,192,1024]{3,2,1,0:T(8,128)(2,1)S(1)} collective-permute-done((bf16[4,2,192,1024]{3,2,1,0:T(8,128)(2,1)}, bf16[4,2,192,1024]{3,2,1,0:T(8,128)(2,1)S(1)}, u32[]{:S(2)}, u32[]{:S(2)}) %collective-permute-start.14) | collective-permute-done | bytes 3145760 | tf_op jit(solution)/shard_map/ppermute | solution.py:1047
  310.9 4.3 fusion.14
  320.4 15.8 %collective-permute-done.17.rest_3_ = bf16[2,192,1024]{2,1,0:T(8,128)(2,1)S(1)} collective-permute-done((bf16[2,192,1024]{2,1,0:T(8,128)(2,1)S(1)}, bf16[2,192,1024]{2,1,0:T(8,128)(2,1)S(1)}, u32[]{:S(2)}, u32[]{:S(2)}) %collective-permute-start.17) | collective-permute-done | bytes 786464 | tf_op jit(solution)/shard_map/ppermute | solution.py:1047
  336.2 17.6 %collective-permute-done.15.rest_1_ = bf16[2,192,1024]{2,1,0:T(8,128)(2,1)} collective-permute-done((bf16[2,192,1024]{2,1,0:T(8,128)(2,1)S(1)}, bf16[2,192,1024]{2,1,0:T(8,128)(2,1)}, u32[]{:S(2)}, u32[]{:S(2)}) %collective-permute-start.15) | collective-permute-done | bytes 786464 | tf_op jit(solution)/shard_map/ppermute | solution.py:1047
  357.5 7.3 %memory_backward.1 = (bf16[8,96,1536]{2,1,0:T(8,128)(2,1)}, bf16[1536,1024]{1,0:T(8,128)(2,1)}, f32[8,768]{1,0:T(8,128)}) custom-call(s32[4]{0:T(128)} %and_select_fusion.place_ref, bf16[1024,768]{1,0:T(8,128)(2,1)} %bitcast.164, bf16[2,192,1024]{2,1,0:T(8,128)(2,1)} %get-tuple-element.85.rest_0_, bf16[2,192,1024]{2,1,0:T(8,128)(2,1)} %collective-permute-done.15.rest_1_, ...), custom_call_target="tpu_custom_call" | custom-call | flops 7000000000 | bytes 7000000 | tf_op jit(solution)/shard_map/memory_backward/pallas_call | solution.py:495
  369.2 9.9 %leave.1 = (f32[512,768]{1,0:T(8,128)}, bf16[8,2,192,128]{3,2,1,0:T(8,128)(2,1)}, bf16[8,96,3200]{2,1,0:T(8,128)(2,1)}) custom-call(bf16[4,4,192,128]{3,2,1,0:T(8,128)(2,1)} %copy-done.14, bf16[8,2,192,128]{3,2,1,0:T(8,128)(2,1)} %all-to-all-done.1.att_ref, f32[512,768]{1,0:T(8,128)} %get-tuple-element.82.resid_ref, f32[512,768]{1,0:T(8,128)} %get-tuple-element.72.norm_ref, ...), custom_call_target="tpu_custom_call" | custom-call | flops 8000000000 | bytes 8000000 | tf_op jit(solution)/shard_map/leave/pallas_call | solution.py:454
  388.8 4.2 collective-permute-done.18
  393.1 4.5 collective-permute-done.20
  397.6 14.8 %collective-permute-done.19 = bf16[24,6912]{1,0:T(8,128)(2,1)S(1)} collective-permute-done((bf16[24,6912]{1,0:T(8,128)(2,1)S(1)}, bf16[24,6912]{1,0:T(8,128)(2,1)S(1)}, u32[]{:S(2)}, u32[]{:S(2)}) %collective-permute-start.19) | collective-permute-done | bytes 331808 | tf_op jit(solution)/shard_map/ppermute | solution.py:1067
  415.1 18.2 %self_backward.1 = (bf16[8,2,576,128]{3,2,1,0:T(8,128)(2,1)}, bf16[2,96,2304]{2,1,0:T(8,128)(2,1)}, f32[8,576]{1,0:T(8,128)}) custom-call(s32[8]{0:T(128)} %stack.57.place_ref, bf16[576,2048]{1,0:T(8,128)(2,1)} %get-tuple-element.94.proj_ref, bf16[8,2,192,128]{3,2,1,0:T(8,128)(2,1)} %copy-done.13, f32[2,192,1024]{2,1,0:T(8,128)} %get-tuple-element.96.mix_ref, ...), custom_call_target="tpu_custom_call" | custom-call | flops 20000000000 | bytes 20000000 | tf_op jit(solution)/shard_map/self_backward/pallas_call | solution.py:288
  442.9 7.3 %collective-permute-done.22 = bf16[24,5632]{1,0:T(8,128)(2,1)S(1)} collective-permute-done((bf16[24,5632]{1,0:T(8,128)(2,1)S(1)}, bf16[24,5632]{1,0:T(8,128)(2,1)S(1)}, u32[]{:S(2)}, u32[]{:S(2)}) %collective-permute-start.22) | collective-permute-done | bytes 270368 | tf_op jit(solution)/shard_map/ppermute | solution.py:1067
  454.3 10.7 %collective-permute-done.23 = bf16[24,5632]{1,0:T(8,128)(2,1)S(1)} collective-permute-done((bf16[24,5632]{1,0:T(8,128)(2,1)S(1)}, bf16[24,5632]{1,0:T(8,128)(2,1)S(1)}, u32[]{:S(2)}, u32[]{:S(2)}) %collective-permute-start.23) | collective-permute-done | bytes 270368 | tf_op jit(solution)/shard_map/ppermute | solution.py:1067
  474.9 4.3 convolution_bitcast_fusion
  479.2 28.0 %all-to-all-done.7 = bf16[8,2,576,128]{3,2,1,0:T(8,128)(2,1)S(1)} async-done(((bf16[8,2,576,128]{3,2,1,0:T(8,128)(2,1)}), bf16[8,2,576,128]{3,2,1,0:T(8,128)(2,1)S(1)}, u32[]{:S(2)}, u32[]{:S(2)}) %all-to-all-start.7) | async-done | bytes 2359328 | tf_op jit(solution)/shard_map/all_to_all | solution.py:1320
  512.6 7.8 %all-gather.9.cloned.1.call-done.in_ref = bf16[192,12544]{1,0:T(8,128)(2,1)} async-done(((bf16[24,12544]{1,0:T(8,128)(2,1)}), bf16[192,12544]{1,0:T(8,128)(2,1)}) %all-gather.9.cloned.1.call-update) | async-done | bytes 4816912 | tf_op jit(solution)/shard_map/all_gather | solution.py:1341
  520.4 6.4 %finish.1 = (f32[192,2304]{1,0:T(8,128)}, f32[192,768]{1,0:T(8,128)}, f32[192,768]{1,0:T(8,128)}, f32[192,1536]{1,0:T(8,128)}, f32[768,768]{1,0:T(8,128)}, /*ind...) custom-call(bf16[192,12544]{1,0:T(8,128)(2,1)} %all-gather.9.cloned.1.call-, ...), custom_call_target="tpu_custom_call" | custom-call | flops 6000000000 | bytes 6000000 | tf_op jit(solution)/shard_map/finish/pallas_call | solution.py:577
  (227 shorter events, 108.2 us)
Async XLA Ops:
  7.2 58.2 %all-gather.11.cloned.1.call-start = ((), (), s32[]{:S(2)}) async-start(), calls=%async_computation.14 | async-start | bytes 1474560 | tf_op jit(solution)/shard_map/all_gather | solution.py:1132
  9.2 105.8 %all-gather.13.cloned.1.call-start = ((), (), s32[]{:S(2)}) async-start(), calls=%async_computation.15 | async-start | bytes 1474560 | tf_op jit(solution)/shard_map/all_gather | solution.py:1132
  11.2 196.9 %all-gather.7.cloned.1.call-start = ((), (), s32[]{:S(2)}) async-start(), calls=%async_computation.10 | async-start | bytes 14598144 | tf_op jit(solution)/shard_map/all_gather | solution.py:1162
  16.2 35.8 %all-to-all-start = ((bf16[4,104,576]{2,1,0:T(8,128)(2,1)}), bf16[4,104,576]{2,1,0:T(8,128)(2,1)S(1)}, u32[]{:S(2)}, u32[]{:S(2)}) async-start(bf16[4,104,576]{2,1,0:T(8,128)(2,1)} %broadcast_in_dim.49), calls=%async_computation | async-start | bytes 1064960 | tf_op jit(solution)/shard_map/all_to_all | solution.py:1114
  22.5 29.7 %collective-permute-start.3 = (bf16[4,128,768]{2,1,0:T(8,128)(2,1)S(1)}, bf16[4,128,768]{2,1,0:T(8,128)(2,1)}, u32[]{:S(2)}, u32[]{:S(2)}) collective-permute-start(bf16[4,128,768]{2,1,0:T(8,128)(2,1)S(1)} %bitcast.159), channel_id=1, source_target_pairs={{0,6},{1,7},{2,0},{3,1},{4,2},{5,3},{6,4},{7,5},{8,14},{9,15},{10,... | collective-permute-start | bytes 2359304 | tf_op jit(solution)/shard_map/ppermute | solution.py:1047
  25.0 35.7 %collective-permute-start.2 = (bf16[4,128,768]{2,1,0:T(8,128)(2,1)S(1)}, bf16[4,128,768]{2,1,0:T(8,128)(2,1)}, u32[]{:S(2)}, u32[]{:S(2)}) collective-permute-start(bf16[4,128,768]{2,1,0:T(8,128)(2,1)S(1)} %bitcast.160), channel_id=1, source_target_pairs={{0,4},{1,5},{2,6},{3,7},{4,0},{5,1},{6,2},{7,3},{8,12},{9,13},{10,... | collective-permute-start | bytes 2359304 | tf_op jit(solution)/shard_map/ppermute | solution.py:1047
  25.5 36.2 %collective-permute-start.1 = (bf16[4,128,768]{2,1,0:T(8,128)(2,1)S(1)}, bf16[4,128,768]{2,1,0:T(8,128)(2,1)}, u32[]{:S(2)}, u32[]{:S(2)}) collective-permute-start(bf16[4,128,768]{2,1,0:T(8,128)(2,1)S(1)} %bitcast.161), channel_id=1, source_target_pairs={{0,2},{1,3},{2,4},{3,5},{4,6},{5,7},{6,0},{7,1},{8,10},{9,11},{10,... | collective-permute-start | bytes 2359304 | tf_op jit(solution)/shard_map/ppermute | solution.py:1047
  52.1 12.1 %collective-permute-start = (bf16[4,104,576]{2,1,0:T(8,128)(2,1)S(1)}, bf16[4,104,576]{2,1,0:T(8,128)(2,1)S(1)}, u32[]{:S(2)}, u32[]{:S(2)}) collective-permute-start(bf16[4,104,576]{2,1,0:T(8,128)(2,1)S(1)} %all-to-all-done), channel_id=1, source_target_pairs={{0,1},{1,0},{2,3},{3,2},{4,5},{5,4},{6,7},{7,6},{8,9},{9,8},{10,11... | collective-permute-start | bytes 1437704 | tf_op jit(solution)/shard_map/ppermute | solution.py:1047
  64.1 13.7 %collective-permute-start.4 = (bf16[4,2,128,768]{3,2,1,0:T(8,128)(2,1)}, bf16[4,2,128,768]{3,2,1,0:T(8,128)(2,1)}, u32[]{:S(2)}, u32[]{:S(2)}) collective-permute-start(bf16[4,2,128,768]{3,2,1,0:T(8,128)(2,1)} %pad_maximum_fusion), channel_id=1, source_target_pairs={{0,1},{1,0},{2,3},{3,2},{4,5},{5,4},{6,7},{7,6},{8,9},{9,8},{10,11... | collective-permute-start | bytes 4718600 | tf_op jit(solution)/shard_map/ppermute | solution.py:1047
  75.3 20.5 %collective-permute-start.8 = (bf16[2,192,1024]{2,1,0:T(8,128)(2,1)S(1)}, bf16[2,192,1024]{2,1,0:T(8,128)(2,1)}, u32[]{:S(2)}, u32[]{:S(2)}) collective-permute-start(bf16[2,192,1024]{2,1,0:T(8,128)(2,1)S(1)} %get-tuple-element.137), channel_id=1, source_target_pairs={{0,6},{1,7},{2,0},{3,1},{4,2},{5,3},{6,4},{7,5},{8,14},{9,15},{10,... | collective-permute-start | bytes 2359304 | tf_op jit(solution)/shard_map/ppermute | solution.py:1047
  75.8 26.7 %collective-permute-start.7 = (bf16[2,192,1024]{2,1,0:T(8,128)(2,1)S(1)}, bf16[2,192,1024]{2,1,0:T(8,128)(2,1)}, u32[]{:S(2)}, u32[]{:S(2)}) collective-permute-start(bf16[2,192,1024]{2,1,0:T(8,128)(2,1)S(1)} %get-tuple-element.138), channel_id=1, source_target_pairs={{0,4},{1,5},{2,6},{3,7},{4,0},{5,1},{6,2},{7,3},{8,12},{9,13},{10,... | collective-permute-start | bytes 2359304 | tf_op jit(solution)/shard_map/ppermute | solution.py:1047
  76.3 38.7 %collective-permute-start.6 = (bf16[2,192,1024]{2,1,0:T(8,128)(2,1)S(1)}, bf16[2,192,1024]{2,1,0:T(8,128)(2,1)}, u32[]{:S(2)}, u32[]{:S(2)}) collective-permute-start(bf16[2,192,1024]{2,1,0:T(8,128)(2,1)S(1)} %get-tuple-element.139), channel_id=1, source_target_pairs={{0,2},{1,3},{2,4},{3,5},{4,6},{5,7},{6,0},{7,1},{8,10},{9,11},{10,... | collective-permute-start | bytes 2359304 | tf_op jit(solution)/shard_map/ppermute | solution.py:1047
  118.1 34.4 %collective-permute-start.10 = (bf16[2,192,1024]{2,1,0:T(8,128)(2,1)}, bf16[2,192,1024]{2,1,0:T(8,128)(2,1)}, u32[]{:S(2)}, u32[]{:S(2)}) collective-permute-start(bf16[2,192,1024]{2,1,0:T(8,128)(2,1)} %get-tuple-element.140.rest_5_.rest_0_), channel_id=1, source_target_pairs={{0,1},{1,0},{2,3},{3,2},{4,5},{5,4},{6,7},{7,6},{8,9},{9,8},{10,11... | collective-permute-start | bytes 2359304 | tf_op jit(solution)/shard_map/ppermute | solution.py:1047
  118.6 22.9 %all-to-all-start.1 = ((bf16[8,2,192,128]{3,2,1,0:T(8,128)(2,1)}), bf16[8,2,192,128]{3,2,1,0:T(8,128)(2,1)}, u32[]{:S(2)}, u32[]{:S(2)}) async-start(bf16[8,2,192,128]{3,2,1,0:T(8,128)(2,1)} %get-tuple-element.65), calls=%async_computation.1 | async-start | bytes 1572864 | tf_op jit(solution)/shard_map/all_to_all | solution.py:1221
  123.6 28.9 %collective-permute-start.13 = (bf16[2,192,1024]{2,1,0:T(8,128)(2,1)}, bf16[2,192,1024]{2,1,0:T(8,128)(2,1)S(1)}, u32[]{:S(2)}, u32[]{:S(2)}) collective-permute-start(bf16[2,192,1024]{2,1,0:T(8,128)(2,1)} %collective-permute-done.8.rest_3_), channel_id=1, source_target_pairs={{0,1},{1,0},{2,3},{3,2},{4,5},{5,4},{6,7},{7,6},{8,9},{9,8},{10,11... | collective-permute-start | bytes 2359304 | tf_op jit(solution)/shard_map/ppermute | solution.py:1047
  124.1 28.4 %collective-permute-start.12 = (bf16[2,192,1024]{2,1,0:T(8,128)(2,1)}, bf16[2,192,1024]{2,1,0:T(8,128)(2,1)}, u32[]{:S(2)}, u32[]{:S(2)}) collective-permute-start(bf16[2,192,1024]{2,1,0:T(8,128)(2,1)} %collective-permute-done.7.rest_2_), channel_id=1, source_target_pairs={{0,1},{1,0},{2,3},{3,2},{4,5},{5,4},{6,7},{7,6},{8,9},{9,8},{10,11... | collective-permute-start | bytes 2359304 | tf_op jit(solution)/shard_map/ppermute | solution.py:1047
  124.2 28.3 %collective-permute-start.11 = (bf16[2,192,1024]{2,1,0:T(8,128)(2,1)}, bf16[2,192,1024]{2,1,0:T(8,128)(2,1)}, u32[]{:S(2)}, u32[]{:S(2)}) collective-permute-start(bf16[2,192,1024]{2,1,0:T(8,128)(2,1)} %collective-permute-done.6.rest_1_), channel_id=1, source_target_pairs={{0,1},{1,0},{2,3},{3,2},{4,5},{5,4},{6,7},{7,6},{8,9},{9,8},{10,11... | collective-permute-start | bytes 2359304 | tf_op jit(solution)/shard_map/ppermute | solution.py:1047
  194.1 11.5 %all-to-all-start.3 = ((bf16[4,4,192,128]{3,2,1,0:T(8,128)(2,1)}), bf16[4,4,192,128]{3,2,1,0:T(8,128)(2,1)S(1)}, u32[]{:S(2)}, u32[]{:S(2)}) async-start(bf16[4,4,192,128]{3,2,1,0:T(8,128)(2,1)} %get-tuple-element.71), calls=%async_computation.3 | async-start | bytes 1572864 | tf_op jit(solution)/shard_map/all_to_all | solution.py:1042
  197.6 181.6 %reduce-scatter.3.cloned.1.call-start = ((), (), s32[]{:S(2)}) async-start(), calls=%async_computation.11 | async-start | bytes 11943936 | tf_op jit(solution)/shard_map/reduce_scatter | solution.py:1256
  315.2 21.0 %collective-permute-start.17 = (bf16[2,192,1024]{2,1,0:T(8,128)(2,1)S(1)}, bf16[2,192,1024]{2,1,0:T(8,128)(2,1)S(1)}, u32[]{:S(2)}, u32[]{:S(2)}) collective-permute-start(bf16[2,192,1024]{2,1,0:T(8,128)(2,1)S(1)} %get-tuple-element.131), channel_id=1, source_target_pairs={{0,6},{1,7},{2,0},{3,1},{4,2},{5,3},{6,4},{7,5},{8,14},{9,15},{10,... | collective-permute-start | bytes 2359304 | tf_op jit(solution)/shard_map/ppermute | solution.py:1047
  316.0 20.2 %collective-permute-start.16 = (bf16[2,192,1024]{2,1,0:T(8,128)(2,1)S(1)}, bf16[2,192,1024]{2,1,0:T(8,128)(2,1)}, u32[]{:S(2)}, u32[]{:S(2)}) collective-permute-start(bf16[2,192,1024]{2,1,0:T(8,128)(2,1)S(1)} %get-tuple-element.132), channel_id=1, source_target_pairs={{0,4},{1,5},{2,6},{3,7},{4,0},{5,1},{6,2},{7,3},{8,12},{9,13},{10,... | collective-permute-start | bytes 2359304 | tf_op jit(solution)/shard_map/ppermute | solution.py:1047
  317.3 36.5 %collective-permute-start.15 = (bf16[2,192,1024]{2,1,0:T(8,128)(2,1)S(1)}, bf16[2,192,1024]{2,1,0:T(8,128)(2,1)}, u32[]{:S(2)}, u32[]{:S(2)}) collective-permute-start(bf16[2,192,1024]{2,1,0:T(8,128)(2,1)S(1)} %get-tuple-element.133), channel_id=1, source_target_pairs={{0,2},{1,3},{2,4},{3,5},{4,6},{5,7},{6,0},{7,1},{8,10},{9,11},{10,... | collective-permute-start | bytes 2359304 | tf_op jit(solution)/shard_map/ppermute | solution.py:1047
  353.8 14.6 %all-to-all-start.5 = ((bf16[4,4,192,128]{3,2,1,0:T(8,128)(2,1)}), bf16[4,4,192,128]{3,2,1,0:T(8,128)(2,1)S(1)}, u32[]{:S(2)}, u32[]{:S(2)}) async-start(bf16[4,4,192,128]{3,2,1,0:T(8,128)(2,1)} %get-tuple-element.81), calls=%async_computation.5 | async-start | bytes 1572864 | tf_op jit(solution)/shard_map/all_to_all | solution.py:1042
  357.3 80.5 %reduce-scatter.5.cloned.1.call-start = ((), (), s32[]{:S(2)}) async-start(), calls=%async_computation.12 | async-start | bytes 5529600 | tf_op jit(solution)/shard_map/reduce_scatter | solution.py:1256
  380.4 12.6 %collective-permute-start.18 = (bf16[24,6912]{1,0:T(8,128)(2,1)S(1)}, bf16[24,6912]{1,0:T(8,128)(2,1)S(1)}, u32[]{:S(2)}, u32[]{:S(2)}) collective-permute-start(bf16[24,6912]{1,0:T(8,128)(2,1)S(1)} %get-tuple-element.144), channel_id=1, source_target_pairs={{0,8},{8,16},{16,24},{24,0},{1,9},{9,17},{17,25},{25,1},{2,10},{10... | collective-permute-start | bytes 995336 | tf_op jit(solution)/shard_map/ppermute | solution.py:1067
  382.0 15.6 %collective-permute-start.20 = (bf16[24,6912]{1,0:T(8,128)(2,1)S(1)}, bf16[24,6912]{1,0:T(8,128)(2,1)S(1)}, u32[]{:S(2)}, u32[]{:S(2)}) collective-permute-start(bf16[24,6912]{1,0:T(8,128)(2,1)S(1)} %get-tuple-element.145), channel_id=1, source_target_pairs={{0,24},{8,0},{16,8},{24,16},{1,25},{9,1},{17,9},{25,17},{2,26},{10... | collective-permute-start | bytes 995336 | tf_op jit(solution)/shard_map/ppermute | solution.py:1067
  384.3 28.1 %collective-permute-start.19 = (bf16[24,6912]{1,0:T(8,128)(2,1)S(1)}, bf16[24,6912]{1,0:T(8,128)(2,1)S(1)}, u32[]{:S(2)}, u32[]{:S(2)}) collective-permute-start(bf16[24,6912]{1,0:T(8,128)(2,1)S(1)} %get-tuple-element.146), channel_id=1, source_target_pairs={{0,16},{8,24},{16,0},{24,8},{1,17},{9,25},{17,1},{25,9},{2,18},{10... | collective-permute-start | bytes 995336 | tf_op jit(solution)/shard_map/ppermute | solution.py:1067
  385.0 29.3 %all-to-all-start.6 = ((bf16[8,2,192,128]{3,2,1,0:T(8,128)(2,1)}), bf16[8,2,192,128]{3,2,1,0:T(8,128)(2,1)S(1)}, u32[]{:S(2)}, u32[]{:S(2)}) async-start(bf16[8,2,192,128]{3,2,1,0:T(8,128)(2,1)} %get-tuple-element.95), calls=%async_computation.6 | async-start | bytes 1572864 | tf_op jit(solution)/shard_map/all_to_all | solution.py:1307
  388.5 131.9 %all-gather.9.cloned.1.call-start = ((), (), s32[]{:S(2)}) async-start(), calls=%async_computation.13 | async-start | bytes 5419008 | tf_op jit(solution)/shard_map/all_gather | solution.py:1341
  439.1 15.2 %collective-permute-start.24 = (bf16[24,5632]{1,0:T(8,128)(2,1)S(1)}, bf16[24,5632]{1,0:T(8,128)(2,1)S(1)}, u32[]{:S(2)}, u32[]{:S(2)}) collective-permute-start(bf16[24,5632]{1,0:T(8,128)(2,1)S(1)} %get-tuple-element.148), channel_id=1, source_target_pairs={{0,24},{8,0},{16,8},{24,16},{1,25},{9,1},{17,9},{25,17},{2,26},{10... | collective-permute-start | bytes 811016 | tf_op jit(solution)/shard_map/ppermute | solution.py:1067
  442.9 22.1 %collective-permute-start.23 = (bf16[24,5632]{1,0:T(8,128)(2,1)S(1)}, bf16[24,5632]{1,0:T(8,128)(2,1)S(1)}, u32[]{:S(2)}, u32[]{:S(2)}) collective-permute-start(bf16[24,5632]{1,0:T(8,128)(2,1)S(1)} %get-tuple-element.149), channel_id=1, source_target_pairs={{0,16},{8,24},{16,0},{24,8},{1,17},{9,25},{17,1},{25,9},{2,18},{10... | collective-permute-start | bytes 811016 | tf_op jit(solution)/shard_map/ppermute | solution.py:1067
  466.0 41.2 %all-to-all-start.7 = ((bf16[8,2,576,128]{3,2,1,0:T(8,128)(2,1)}), bf16[8,2,576,128]{3,2,1,0:T(8,128)(2,1)S(1)}, u32[]{:S(2)}, u32[]{:S(2)}) async-start(bf16[8,2,576,128]{3,2,1,0:T(8,128)(2,1)} %get-tuple-element.101), calls=%async_computation.9 | async-start | bytes 4718592 | tf_op jit(solution)/shard_map/all_to_all | solution.py:1320
  (38 other events, 391.9 us)
Sparse Core Ops, SparseCore 0:
  10.2 44.7 all-gather.10
  57.1 29.2 all-gather.12
  89.9 118.1 all-gather.6
  239.8 81.9 reduce-scatter.2
  379.2 54.8 reduce-scatter.4
  466.1 54.2 all-gather.8

commit v5 on v4

--- a/solution.py
+++ b/solution.py
@@ -1124,15 +1124,19 @@
     stack_n = ffn_out.shape[0] // part
     member_rows = part // spread
 
-    def gather_halves(*weights):
+    def own_halves(*weights):
         piece = [
             lax.dynamic_slice_in_dim(weight, member * member_rows, member_rows, 0).astype(half)
             for weight in weights
         ]
-        return lax.all_gather(jnp.concatenate(piece, axis=1), "doc", axis=0)
-
-    w_cross_kv = join_members(gather_halves(cross_kv)).reshape(D, 2 * D)
-    pair_halves = gather_halves(self_out, cross_q)
+        return jnp.concatenate(piece, axis=1)
+
+    kv_halves = lax.all_gather(own_halves(cross_kv), "doc", axis=0)
+    w_cross_kv = join_members(kv_halves).reshape(D, 2 * D)
+    pair_halves = own_halves(self_out, cross_q)
+    pair_halves = jnp.broadcast_to(pair_halves[None], (n_doc,) + pair_halves.shape)
+    pair_halves, first_gather = lax.optimization_barrier((pair_halves, first_gather))
+    pair_halves = lax.all_to_all(pair_halves, "doc", 0, 0, tiled=True)
 
     block_rows, block_cols = divmod(seq_index, 4)
 

time: 544 us -> 557 us (1.024)
  waiting for transfers between devices: 214 us -> 229 us
    all_to_all x3, waiting for transfers between devices: 15.3 us -> 29.7 us  [swap_heads(): lax.all_to_all(blocks, 'seq', 0, 0, axis_index_groups=same_member, tiled=...]
    ppermute x19, waiting for transfers between devices: 73.5 us -> 85 us  [rotate_both(): lax.ppermute(block, 'seq', [(h * spread + m, (h + turn_h) % HEAD_GROUPS *...]
  transfers between devices with their start and end apart: 38 -> 38, of which waited for: 23 -> 22; matrix products, arithmetic and copies ran while one was open for 10% -> 10% of each run, Pallas kernels for 26% -> 24%
where the time goes in v5:
time: 557 us; the launch traced here: 548 us
  waiting for transfers between devices  229 us (41%)
  Pallas kernels  171 us (31%)
  starting transfers between devices  54.2 us (10%)
  local copies, waits for them, and re-layouts  37.9 us (7%)
  other arithmetic  16.8 us (3%)
  between operations  16 us (3%)
  blocking collectives  13.9 us (2%)
  matrix products  9.53 us (2%)
    ppermute x19, waiting for transfers between devices, rotate_both(): lax.ppermute(block, 'seq', [(h * spread + m, (h + turn_h) % HEAD_GROUPS *...  85 us
    pallas_call x1, Pallas kernels, cross_backward(): pl.pallas_call(cross_backward_kernel, grid_spec=pltpu.PrefetchScalarGridS...  48 us
    ppermute x6, waiting for transfers between devices, rotate_doc(): lax.ppermute(block, 'doc', [(d, (d + turn) % n_doc) for d in range(n_doc)])  45.6 us
    pallas_call x1, Pallas kernels, middle(): pl.pallas_call(partial(middle_kernel, n_doc, n_seq), in_specs=[vmem] * 5...  31.5 us
    pallas_call x1, Pallas kernels, cross_forward(): pl.pallas_call(cross_forward_kernel, grid_spec=pltpu.PrefetchScalarGridSp...  29.8 us
    all_to_all x3, waiting for transfers between devices, swap_heads(): lax.all_to_all(blocks, 'seq', 0, 0, axis_index_groups=same_member, tiled=...  29.7 us
    all_to_all x1, waiting for transfers between devices, body(): grad_proj_got = lax.all_to_all(grad_proj_send, 'seq', 0, 0, tiled=True)  28 us
    all_to_all x1, waiting for transfers between devices, body(): lax.all_to_all(first_piece, 'doc', 0, 0, tiled=True)  23 us
  transfers between devices with their start and end apart: 38, of which 22 were waited for; matrix products, arithmetic and copies ran while one was open for 10% of the time, Pallas kernels for 24%

profile of v5, /device:TPU:0, one launch (start us, length us, event | category | flops | bytes accessed | tf_op | source)
XLA Modules:
  0.0 548.2 jit_solution(1783265733016962245)
XLA Ops:
  14.3 6.3 %all-to-all-start = ((bf16[4,104,576]{2,1,0:T(8,128)(2,1)}), bf16[4,104,576]{2,1,0:T(8,128)(2,1)S(1)}, u32[]{:S(2)}, u32[]{:S(2)}) async-start(bf16[4,104,576]{2,1,0:T(8,128)(2,1)} %broadcast_in_dim.55), calls=%async_computation | async-start | bytes 1064960 | tf_op jit(solution)/shard_map/all_to_all | solution.py:1114
  26.1 23.0 %all-to-all-done = bf16[4,104,576]{2,1,0:T(8,128)(2,1)S(1)} async-done(((bf16[4,104,576]{2,1,0:T(8,128)(2,1)}), bf16[4,104,576]{2,1,0:T(8,128)(2,1)S(1)}, u32[]{:S(2)}, u32[]{:S(2)}) %all-to-all-start) | async-done | bytes 479264 | tf_op jit(solution)/shard_map/all_to_all | solution.py:1114
  50.3 8.5 %collective-permute-done.2.rest_2_ = bf16[4,128,768]{2,1,0:T(8,128)(2,1)} collective-permute-done((bf16[4,128,768]{2,1,0:T(8,128)(2,1)S(1)}, bf16[4,128,768]{2,1,0:T(8,128)(2,1)}, u32[]{:S(2)}, u32[]{:S(2)}) %collective-permute-start.2) | collective-permute-done | bytes 786464 | tf_op jit(solution)/shard_map/ppermute | solution.py:1047
  63.4 4.8 all-to-all-start.2
  79.9 13.3 %self_forward.1 = (bf16[576,2048]{1,0:T(8,128)(2,1)}, f32[2,192,1024]{2,1,0:T(8,128)}, bf16[8,2,192,128]{3,2,1,0:T(8,128)(2,1)}, f32[2,3,1024]{2,1,0:T(4,128)}) custom-call(s32[8]{0:T(128)} %stack.57.place_ref, bf16[768,576]{1,0:T(8,128)(2,1)} %bitcast.151, f32[1,576]{1,0:T(1,128)} %broadcast_in_dim.59.bias_ref, bf16[4,128,768]{2,1,0:T(8,128)(2,1)} %bitcast.153, ...), custom_call_target="tpu_custom_call" | custom-call | flops 17999998976 | bytes 18000000 | tf_op jit(solution)/shard_map/self_forward/pallas_call | solution.py:173
  93.2 4.6 collective-permute-done.8.rest_3_
  97.9 10.1 %collective-permute-done.7.rest_2_ = bf16[2,192,1024]{2,1,0:T(8,128)(2,1)} collective-permute-done((bf16[2,192,1024]{2,1,0:T(8,128)(2,1)S(1)}, bf16[2,192,1024]{2,1,0:T(8,128)(2,1)}, u32[]{:S(2)}, u32[]{:S(2)}) %collective-permute-start.7) | collective-permute-done | bytes 786464 | tf_op jit(solution)/shard_map/ppermute | solution.py:1047
  108.0 13.7 %collective-permute-done.6.rest_1_ = bf16[2,192,1024]{2,1,0:T(8,128)(2,1)} collective-permute-done((bf16[2,192,1024]{2,1,0:T(8,128)(2,1)S(1)}, bf16[2,192,1024]{2,1,0:T(8,128)(2,1)}, u32[]{:S(2)}, u32[]{:S(2)}) %collective-permute-start.6) | collective-permute-done | bytes 786464 | tf_op jit(solution)/shard_map/ppermute | solution.py:1047
  124.5 4.7 all-to-all-start.1
  131.9 9.9 %all-to-all-done.1.att_ref = bf16[8,2,192,128]{3,2,1,0:T(8,128)(2,1)} async-done(((bf16[8,2,192,128]{3,2,1,0:T(8,128)(2,1)}), bf16[8,2,192,128]{3,2,1,0:T(8,128)(2,1)}, u32[]{:S(2)}, u32[]{:S(2)}) %all-to-all-start.1) | async-done | bytes 786464 | tf_op jit(solution)/shard_map/all_to_all | solution.py:1225
  141.8 6.1 %enter.1 = (f32[512,768]{1,0:T(8,128)}, f32[512,768]{1,0:T(8,128)}, f32[512,128]{1,0:T(8,128)}, bf16[4,4,192,128]{3,2,1,0:T(8,128)(2,1)}) custom-call(bf16[8,2,192,128]{3,2,1,0:T(8,128)(2,1)} %all-to-all-done.1.att_ref, bf16[512,768]{1,0:T(8,128)(2,1)} %bitcast.154, f32[8,768]{1,0:T(8,128)} %select_maximum_fusion.vec_ref, bf16[768,1536]{1,0:T(8,128)(2,1)} %bitcast.140), custom_call_target="tpu_custom_call" | custom-call | flops 6000000000 | bytes 6000000 | tf_op jit(solution)/shard_map/enter/pallas_call | solution.py:363
  152.8 18.8 %all-to-all-done.3.q_ref = bf16[4,4,192,128]{3,2,1,0:T(8,128)(2,1)S(1)} async-done(((bf16[4,4,192,128]{3,2,1,0:T(8,128)(2,1)}), bf16[4,4,192,128]{3,2,1,0:T(8,128)(2,1)S(1)}, u32[]{:S(2)}, u32[]{:S(2)}) %all-to-all-start.3) | async-done | bytes 786464 | tf_op jit(solution)/shard_map/all_to_all | solution.py:1042
  172.4 29.8 %cross_forward.1 = (f32[4,192,512]{2,1,0:T(8,128)}, bf16[4,4,192,128]{3,2,1,0:T(8,128)(2,1)}, f32[4,3,512]{2,1,0:T(4,128)}) custom-call(s32[4]{0:T(128)} %pad_add_fusion.low_ref, s32[4]{0:T(128)} %get-tuple-element.154.high_ref, s32[8]{0:T(128)} %stack.57.place_ref, bf16[4,4,192,128]{3,2,1,0:T(8,128)(2,1)} %copy-done.10, ...), custom_call_target="tpu_custom_call" | custom-call | flops 32999999488 | bytes 33000000 | tf_op jit(solution)/shard_map/cross_forward/pallas_call | solution.py:690
  208.5 7.5 %all-to-all-done.4.att_ref = bf16[4,4,192,128]{3,2,1,0:T(8,128)(2,1)S(1)} async-done(((bf16[4,4,192,128]{3,2,1,0:T(8,128)(2,1)}), bf16[4,4,192,128]{3,2,1,0:T(8,128)(2,1)S(1)}, u32[]{:S(2)}, u32[]{:S(2)}) %all-to-all-start.4) | async-done | bytes 786464 | tf_op jit(solution)/shard_map/all_to_all | solution.py:1042
  216.9 31.5 %middle.1 = (bf16[512,768]{1,0:T(8,128)(2,1)}, f32[512,768]{1,0:T(8,128)}, bf16[4,4,192,128]{3,2,1,0:T(8,128)(2,1)}, bf16[8,96,6912]{2,1,0:T(8,128)(2,1)}, f32[8,768]{1,0:T(8,128)}, /*index=5*/f32[1,3072]{1,0:T(1,128)}) custom-call(bf16[4,4,192,128]{3,2,1,0:T(8,128)(2,1)} %copy-done.11, f32[512,768]{1,0:T(8,128)} %get-tuple-element.74.norm_ref, ...), custom_call_target="tpu_custom_call" | custom-call | flops 31000000512 | bytes 31000000 | tf_op jit(solution)/shard_map/middle/pallas_call | solution.py:979
  249.6 13.9 %all_to_all.45.g_ref = bf16[4,4,192,128]{3,2,1,0:T(8,128)(2,1)} all-to-all(bf16[4,4,192,128]{3,2,1,0:T(8,128)(2,1)S(1)} %copy-done.14), channel_id=1, replica_groups={{0,2,4,6},{1,3,5,7},{8,10,12,14},{9,11,13,15},{16,18,20,22},{17,19,21,2..., dimensions={0} | all-to-all | bytes 1572864 | tf_op jit(solution)/shard_map/all_to_all | solution.py:1042
  263.5 48.0 %cross_backward.1 = (bf16[4,4,192,128]{3,2,1,0:T(8,128)(2,1)}, bf16[4,2,192,1024]{3,2,1,0:T(8,128)(2,1)}, bf16[4,2,192,1024]{3,2,1,0:T(8,128)(2,1)}) custom-call(s32[4]{0:T(128)} %pad_add_fusion.low_ref, s32[4]{0:T(128)} %get-tuple-element.154.high_ref, s32[8]{0:T(128)} %stack.57.place_ref, bf16[4,4,192,128]{3,2,1,0:T(8,128)(2,1)} %copy-done.10, ...), custom_call_target="tpu_custom_call" | custom-call | flops 49000001536 | bytes 49000000 | tf_op jit(solution)/shard_map/cross_backward/pallas_call | solution.py:805
  311.5 5.9 %collective-permute-done.14 = bf16[4,2,192,1024]{3,2,1,0:T(8,128)(2,1)S(1)} collective-permute-done((bf16[4,2,192,1024]{3,2,1,0:T(8,128)(2,1)}, bf16[4,2,192,1024]{3,2,1,0:T(8,128)(2,1)S(1)}, u32[]{:S(2)}, u32[]{:S(2)}) %collective-permute-start.14) | collective-permute-done | bytes 3145760 | tf_op jit(solution)/shard_map/ppermute | solution.py:1047
  317.4 4.3 fusion.14
  327.5 21.7 %collective-permute-done.17.rest_3_ = bf16[2,192,1024]{2,1,0:T(8,128)(2,1)S(1)} collective-permute-done((bf16[2,192,1024]{2,1,0:T(8,128)(2,1)S(1)}, bf16[2,192,1024]{2,1,0:T(8,128)(2,1)S(1)}, u32[]{:S(2)}, u32[]{:S(2)}) %collective-permute-start.17) | collective-permute-done | bytes 786464 | tf_op jit(solution)/shard_map/ppermute | solution.py:1047
  349.1 17.6 %collective-permute-done.15.rest_1_ = bf16[2,192,1024]{2,1,0:T(8,128)(2,1)} collective-permute-done((bf16[2,192,1024]{2,1,0:T(8,128)(2,1)S(1)}, bf16[2,192,1024]{2,1,0:T(8,128)(2,1)}, u32[]{:S(2)}, u32[]{:S(2)}) %collective-permute-start.15) | collective-permute-done | bytes 786464 | tf_op jit(solution)/shard_map/ppermute | solution.py:1047
  370.5 7.3 %memory_backward.1 = (bf16[8,96,1536]{2,1,0:T(8,128)(2,1)}, bf16[1536,1024]{1,0:T(8,128)(2,1)}, f32[8,768]{1,0:T(8,128)}) custom-call(s32[4]{0:T(128)} %and_select_fusion.place_ref, bf16[1024,768]{1,0:T(8,128)(2,1)} %bitcast.161, bf16[2,192,1024]{2,1,0:T(8,128)(2,1)} %get-tuple-element.87.rest_0_, bf16[2,192,1024]{2,1,0:T(8,128)(2,1)} %collective-permute-done.15.rest_1_, ...), custom_call_target="tpu_custom_call" | custom-call | flops 7000000000 | bytes 7000000 | tf_op jit(solution)/shard_map/memory_backward/pallas_call | solution.py:495
  382.2 9.9 %leave.1 = (f32[512,768]{1,0:T(8,128)}, bf16[8,2,192,128]{3,2,1,0:T(8,128)(2,1)}, bf16[8,96,3200]{2,1,0:T(8,128)(2,1)}) custom-call(bf16[4,4,192,128]{3,2,1,0:T(8,128)(2,1)} %copy-done.13, bf16[8,2,192,128]{3,2,1,0:T(8,128)(2,1)} %all-to-all-done.1.att_ref, f32[512,768]{1,0:T(8,128)} %get-tuple-element.84.resid_ref, f32[512,768]{1,0:T(8,128)} %get-tuple-element.74.norm_ref, ...), custom_call_target="tpu_custom_call" | custom-call | flops 8000000000 | bytes 8000000 | tf_op jit(solution)/shard_map/leave/pallas_call | solution.py:454
  406.0 4.5 collective-permute-done.20
  410.5 14.8 %collective-permute-done.19 = bf16[24,6912]{1,0:T(8,128)(2,1)S(1)} collective-permute-done((bf16[24,6912]{1,0:T(8,128)(2,1)S(1)}, bf16[24,6912]{1,0:T(8,128)(2,1)S(1)}, u32[]{:S(2)}, u32[]{:S(2)}) %collective-permute-start.19) | collective-permute-done | bytes 331808 | tf_op jit(solution)/shard_map/ppermute | solution.py:1067
  428.1 18.2 %self_backward.1 = (bf16[8,2,576,128]{3,2,1,0:T(8,128)(2,1)}, bf16[2,96,2304]{2,1,0:T(8,128)(2,1)}, f32[8,576]{1,0:T(8,128)}) custom-call(s32[8]{0:T(128)} %stack.57.place_ref, bf16[576,2048]{1,0:T(8,128)(2,1)} %get-tuple-element.96.proj_ref, bf16[8,2,192,128]{3,2,1,0:T(8,128)(2,1)} %copy-done.12, f32[2,192,1024]{2,1,0:T(8,128)} %get-tuple-element.98.mix_ref, ...), custom_call_target="tpu_custom_call" | custom-call | flops 20000000000 | bytes 20000000 | tf_op jit(solution)/shard_map/self_backward/pallas_call | solution.py:288
  455.9 7.3 %collective-permute-done.22 = bf16[24,5632]{1,0:T(8,128)(2,1)S(1)} collective-permute-done((bf16[24,5632]{1,0:T(8,128)(2,1)S(1)}, bf16[24,5632]{1,0:T(8,128)(2,1)S(1)}, u32[]{:S(2)}, u32[]{:S(2)}) %collective-permute-start.22) | collective-permute-done | bytes 270368 | tf_op jit(solution)/shard_map/ppermute | solution.py:1067
  467.2 10.7 %collective-permute-done.23 = bf16[24,5632]{1,0:T(8,128)(2,1)S(1)} collective-permute-done((bf16[24,5632]{1,0:T(8,128)(2,1)S(1)}, bf16[24,5632]{1,0:T(8,128)(2,1)S(1)}, u32[]{:S(2)}, u32[]{:S(2)}) %collective-permute-start.23) | collective-permute-done | bytes 270368 | tf_op jit(solution)/shard_map/ppermute | solution.py:1067
  487.9 4.3 convolution_bitcast_fusion
  492.2 28.0 %all-to-all-done.8 = bf16[8,2,576,128]{3,2,1,0:T(8,128)(2,1)S(1)} async-done(((bf16[8,2,576,128]{3,2,1,0:T(8,128)(2,1)}), bf16[8,2,576,128]{3,2,1,0:T(8,128)(2,1)S(1)}, u32[]{:S(2)}, u32[]{:S(2)}) %all-to-all-start.8) | async-done | bytes 2359328 | tf_op jit(solution)/shard_map/all_to_all | solution.py:1324
  525.5 7.9 %all-gather.7.cloned.1.call-done.in_ref = bf16[192,12544]{1,0:T(8,128)(2,1)} async-done(((bf16[24,12544]{1,0:T(8,128)(2,1)}), bf16[192,12544]{1,0:T(8,128)(2,1)}) %all-gather.7.cloned.1.call-update) | async-done | bytes 4816912 | tf_op jit(solution)/shard_map/all_gather | solution.py:1345
  533.4 6.4 %finish.1 = (f32[192,2304]{1,0:T(8,128)}, f32[192,768]{1,0:T(8,128)}, f32[192,768]{1,0:T(8,128)}, f32[192,1536]{1,0:T(8,128)}, f32[768,768]{1,0:T(8,128)}, /*ind...) custom-call(bf16[192,12544]{1,0:T(8,128)(2,1)} %all-gather.7.cloned.1.call-, ...), custom_call_target="tpu_custom_call" | custom-call | flops 6000000000 | bytes 6000000 | tf_op jit(solution)/shard_map/finish/pallas_call | solution.py:577
  (217 shorter events, 108.9 us)
Async XLA Ops:
  7.2 61.2 %all-gather.9.cloned.1.call-start = ((), (), s32[]{:S(2)}) async-start(), calls=%async_computation.15 | async-start | bytes 1474560 | tf_op jit(solution)/shard_map/all_gather | solution.py:1134
  9.3 206.8 %all-gather.5.cloned.1.call-start = ((), (), s32[]{:S(2)}) async-start(), calls=%async_computation.11 | async-start | bytes 14598144 | tf_op jit(solution)/shard_map/all_gather | solution.py:1166
  14.3 34.7 %all-to-all-start = ((bf16[4,104,576]{2,1,0:T(8,128)(2,1)}), bf16[4,104,576]{2,1,0:T(8,128)(2,1)S(1)}, u32[]{:S(2)}, u32[]{:S(2)}) async-start(bf16[4,104,576]{2,1,0:T(8,128)(2,1)} %broadcast_in_dim.55), calls=%async_computation | async-start | bytes 1064960 | tf_op jit(solution)/shard_map/all_to_all | solution.py:1114
  20.6 28.6 %collective-permute-start.3 = (bf16[4,128,768]{2,1,0:T(8,128)(2,1)S(1)}, bf16[4,128,768]{2,1,0:T(8,128)(2,1)}, u32[]{:S(2)}, u32[]{:S(2)}) collective-permute-start(bf16[4,128,768]{2,1,0:T(8,128)(2,1)S(1)} %bitcast.156), channel_id=1, source_target_pairs={{0,6},{1,7},{2,0},{3,1},{4,2},{5,3},{6,4},{7,5},{8,14},{9,15},{10,... | collective-permute-start | bytes 2359304 | tf_op jit(solution)/shard_map/ppermute | solution.py:1047
  23.1 35.7 %collective-permute-start.2 = (bf16[4,128,768]{2,1,0:T(8,128)(2,1)S(1)}, bf16[4,128,768]{2,1,0:T(8,128)(2,1)}, u32[]{:S(2)}, u32[]{:S(2)}) collective-permute-start(bf16[4,128,768]{2,1,0:T(8,128)(2,1)S(1)} %bitcast.157), channel_id=1, source_target_pairs={{0,4},{1,5},{2,6},{3,7},{4,0},{5,1},{6,2},{7,3},{8,12},{9,13},{10,... | collective-permute-start | bytes 2359304 | tf_op jit(solution)/shard_map/ppermute | solution.py:1047
  23.6 36.2 %collective-permute-start.1 = (bf16[4,128,768]{2,1,0:T(8,128)(2,1)S(1)}, bf16[4,128,768]{2,1,0:T(8,128)(2,1)}, u32[]{:S(2)}, u32[]{:S(2)}) collective-permute-start(bf16[4,128,768]{2,1,0:T(8,128)(2,1)S(1)} %bitcast.158), channel_id=1, source_target_pairs={{0,2},{1,3},{2,4},{3,5},{4,6},{5,7},{6,0},{7,1},{8,10},{9,11},{10,... | collective-permute-start | bytes 2359304 | tf_op jit(solution)/shard_map/ppermute | solution.py:1047
  61.1 18.9 %collective-permute-start.4 = (bf16[4,2,128,768]{3,2,1,0:T(8,128)(2,1)S(1)}, bf16[4,2,128,768]{3,2,1,0:T(8,128)(2,1)}, u32[]{:S(2)}, u32[]{:S(2)}) collective-permute-start(bf16[4,2,128,768]{3,2,1,0:T(8,128)(2,1)S(1)} %pad_maximum_fusion), channel_id=1, source_target_pairs={{0,1},{1,0},{2,3},{3,2},{4,5},{5,4},{6,7},{7,6},{8,9},{9,8},{10,11... | collective-permute-start | bytes 4718600 | tf_op jit(solution)/shard_map/ppermute | solution.py:1047
  63.4 58.4 %all-to-all-start.2 = ((bf16[4,96,1536]{2,1,0:T(8,128)(2,1)}), bf16[4,96,1536]{2,1,0:T(8,128)(2,1)S(1)}, u32[]{:S(2)}, u32[]{:S(2)}) async-start(bf16[4,96,1536]{2,1,0:T(8,128)(2,1)} %broadcast_in_dim.62), calls=%async_computation.2 | async-start | bytes 2359296 | tf_op jit(solution)/shard_map/all_to_all | solution.py:1139
  77.4 20.5 %collective-permute-start.8 = (bf16[2,192,1024]{2,1,0:T(8,128)(2,1)S(1)}, bf16[2,192,1024]{2,1,0:T(8,128)(2,1)}, u32[]{:S(2)}, u32[]{:S(2)}) collective-permute-start(bf16[2,192,1024]{2,1,0:T(8,128)(2,1)S(1)} %get-tuple-element.139), channel_id=1, source_target_pairs={{0,6},{1,7},{2,0},{3,1},{4,2},{5,3},{6,4},{7,5},{8,14},{9,15},{10,... | collective-permute-start | bytes 2359304 | tf_op jit(solution)/shard_map/ppermute | solution.py:1047
  77.9 30.1 %collective-permute-start.7 = (bf16[2,192,1024]{2,1,0:T(8,128)(2,1)S(1)}, bf16[2,192,1024]{2,1,0:T(8,128)(2,1)}, u32[]{:S(2)}, u32[]{:S(2)}) collective-permute-start(bf16[2,192,1024]{2,1,0:T(8,128)(2,1)S(1)} %get-tuple-element.140), channel_id=1, source_target_pairs={{0,4},{1,5},{2,6},{3,7},{4,0},{5,1},{6,2},{7,3},{8,12},{9,13},{10,... | collective-permute-start | bytes 2359304 | tf_op jit(solution)/shard_map/ppermute | solution.py:1047
  78.4 43.3 %collective-permute-start.6 = (bf16[2,192,1024]{2,1,0:T(8,128)(2,1)S(1)}, bf16[2,192,1024]{2,1,0:T(8,128)(2,1)}, u32[]{:S(2)}, u32[]{:S(2)}) collective-permute-start(bf16[2,192,1024]{2,1,0:T(8,128)(2,1)S(1)} %get-tuple-element.141), channel_id=1, source_target_pairs={{0,2},{1,3},{2,4},{3,5},{4,6},{5,7},{6,0},{7,1},{8,10},{9,11},{10,... | collective-permute-start | bytes 2359304 | tf_op jit(solution)/shard_map/ppermute | solution.py:1047
  124.0 28.8 %collective-permute-start.10 = (bf16[2,192,1024]{2,1,0:T(8,128)(2,1)}, bf16[2,192,1024]{2,1,0:T(8,128)(2,1)}, u32[]{:S(2)}, u32[]{:S(2)}) collective-permute-start(bf16[2,192,1024]{2,1,0:T(8,128)(2,1)} %get-tuple-element.142.rest_5_.rest_0_), channel_id=1, source_target_pairs={{0,1},{1,0},{2,3},{3,2},{4,5},{5,4},{6,7},{7,6},{8,9},{9,8},{10,11... | collective-permute-start | bytes 2359304 | tf_op jit(solution)/shard_map/ppermute | solution.py:1047
  124.5 17.3 %all-to-all-start.1 = ((bf16[8,2,192,128]{3,2,1,0:T(8,128)(2,1)}), bf16[8,2,192,128]{3,2,1,0:T(8,128)(2,1)}, u32[]{:S(2)}, u32[]{:S(2)}) async-start(bf16[8,2,192,128]{3,2,1,0:T(8,128)(2,1)} %get-tuple-element.66), calls=%async_computation.1 | async-start | bytes 1572864 | tf_op jit(solution)/shard_map/all_to_all | solution.py:1225
  129.5 23.2 %collective-permute-start.13 = (bf16[2,192,1024]{2,1,0:T(8,128)(2,1)}, bf16[2,192,1024]{2,1,0:T(8,128)(2,1)}, u32[]{:S(2)}, u32[]{:S(2)}) collective-permute-start(bf16[2,192,1024]{2,1,0:T(8,128)(2,1)} %collective-permute-done.8.rest_3_), channel_id=1, source_target_pairs={{0,1},{1,0},{2,3},{3,2},{4,5},{5,4},{6,7},{7,6},{8,9},{9,8},{10,11... | collective-permute-start | bytes 2359304 | tf_op jit(solution)/shard_map/ppermute | solution.py:1047
  130.0 22.7 %collective-permute-start.12 = (bf16[2,192,1024]{2,1,0:T(8,128)(2,1)}, bf16[2,192,1024]{2,1,0:T(8,128)(2,1)}, u32[]{:S(2)}, u32[]{:S(2)}) collective-permute-start(bf16[2,192,1024]{2,1,0:T(8,128)(2,1)} %collective-permute-done.7.rest_2_), channel_id=1, source_target_pairs={{0,1},{1,0},{2,3},{3,2},{4,5},{5,4},{6,7},{7,6},{8,9},{9,8},{10,11... | collective-permute-start | bytes 2359304 | tf_op jit(solution)/shard_map/ppermute | solution.py:1047
  130.1 22.7 %collective-permute-start.11 = (bf16[2,192,1024]{2,1,0:T(8,128)(2,1)}, bf16[2,192,1024]{2,1,0:T(8,128)(2,1)}, u32[]{:S(2)}, u32[]{:S(2)}) collective-permute-start(bf16[2,192,1024]{2,1,0:T(8,128)(2,1)} %collective-permute-done.6.rest_1_), channel_id=1, source_target_pairs={{0,1},{1,0},{2,3},{3,2},{4,5},{5,4},{6,7},{7,6},{8,9},{9,8},{10,11... | collective-permute-start | bytes 2359304 | tf_op jit(solution)/shard_map/ppermute | solution.py:1047
  147.9 23.6 %all-to-all-start.3 = ((bf16[4,4,192,128]{3,2,1,0:T(8,128)(2,1)}), bf16[4,4,192,128]{3,2,1,0:T(8,128)(2,1)S(1)}, u32[]{:S(2)}, u32[]{:S(2)}) async-start(bf16[4,4,192,128]{3,2,1,0:T(8,128)(2,1)} %get-tuple-element.69), calls=%async_computation.3 | async-start | bytes 1572864 | tf_op jit(solution)/shard_map/all_to_all | solution.py:1042
  202.3 13.8 %all-to-all-start.4 = ((bf16[4,4,192,128]{3,2,1,0:T(8,128)(2,1)}), bf16[4,4,192,128]{3,2,1,0:T(8,128)(2,1)S(1)}, u32[]{:S(2)}, u32[]{:S(2)}) async-start(bf16[4,4,192,128]{3,2,1,0:T(8,128)(2,1)} %get-tuple-element.73), calls=%async_computation.4 | async-start | bytes 1572864 | tf_op jit(solution)/shard_map/all_to_all | solution.py:1042
  205.8 186.4 %reduce-scatter.3.cloned.1.call-start = ((), (), s32[]{:S(2)}) async-start(), calls=%async_computation.12 | async-start | bytes 11943936 | tf_op jit(solution)/shard_map/reduce_scatter | solution.py:1260
  321.7 27.4 %collective-permute-start.17 = (bf16[2,192,1024]{2,1,0:T(8,128)(2,1)S(1)}, bf16[2,192,1024]{2,1,0:T(8,128)(2,1)S(1)}, u32[]{:S(2)}, u32[]{:S(2)}) collective-permute-start(bf16[2,192,1024]{2,1,0:T(8,128)(2,1)S(1)} %get-tuple-element.133), channel_id=1, source_target_pairs={{0,6},{1,7},{2,0},{3,1},{4,2},{5,3},{6,4},{7,5},{8,14},{9,15},{10,... | collective-permute-start | bytes 2359304 | tf_op jit(solution)/shard_map/ppermute | solution.py:1047
  323.1 26.0 %collective-permute-start.16 = (bf16[2,192,1024]{2,1,0:T(8,128)(2,1)S(1)}, bf16[2,192,1024]{2,1,0:T(8,128)(2,1)}, u32[]{:S(2)}, u32[]{:S(2)}) collective-permute-start(bf16[2,192,1024]{2,1,0:T(8,128)(2,1)S(1)} %get-tuple-element.134), channel_id=1, source_target_pairs={{0,4},{1,5},{2,6},{3,7},{4,0},{5,1},{6,2},{7,3},{8,12},{9,13},{10,... | collective-permute-start | bytes 2359304 | tf_op jit(solution)/shard_map/ppermute | solution.py:1047
  324.4 42.3 %collective-permute-start.15 = (bf16[2,192,1024]{2,1,0:T(8,128)(2,1)S(1)}, bf16[2,192,1024]{2,1,0:T(8,128)(2,1)}, u32[]{:S(2)}, u32[]{:S(2)}) collective-permute-start(bf16[2,192,1024]{2,1,0:T(8,128)(2,1)S(1)} %get-tuple-element.135), channel_id=1, source_target_pairs={{0,2},{1,3},{2,4},{3,5},{4,6},{5,7},{6,0},{7,1},{8,10},{9,11},{10,... | collective-permute-start | bytes 2359304 | tf_op jit(solution)/shard_map/ppermute | solution.py:1047
  366.7 14.6 %all-to-all-start.6 = ((bf16[4,4,192,128]{3,2,1,0:T(8,128)(2,1)}), bf16[4,4,192,128]{3,2,1,0:T(8,128)(2,1)S(1)}, u32[]{:S(2)}, u32[]{:S(2)}) async-start(bf16[4,4,192,128]{3,2,1,0:T(8,128)(2,1)} %get-tuple-element.83), calls=%async_computation.6 | async-start | bytes 1572864 | tf_op jit(solution)/shard_map/all_to_all | solution.py:1042
  370.2 80.5 %reduce-scatter.5.cloned.1.call-start = ((), (), s32[]{:S(2)}) async-start(), calls=%async_computation.13 | async-start | bytes 5529600 | tf_op jit(solution)/shard_map/reduce_scatter | solution.py:1260
  393.4 12.6 %collective-permute-start.18 = (bf16[24,6912]{1,0:T(8,128)(2,1)S(1)}, bf16[24,6912]{1,0:T(8,128)(2,1)S(1)}, u32[]{:S(2)}, u32[]{:S(2)}) collective-permute-start(bf16[24,6912]{1,0:T(8,128)(2,1)S(1)} %get-tuple-element.146), channel_id=1, source_target_pairs={{0,8},{8,16},{16,24},{24,0},{1,9},{9,17},{17,25},{25,1},{2,10},{10... | collective-permute-start | bytes 995336 | tf_op jit(solution)/shard_map/ppermute | solution.py:1067
  394.9 15.6 %collective-permute-start.20 = (bf16[24,6912]{1,0:T(8,128)(2,1)S(1)}, bf16[24,6912]{1,0:T(8,128)(2,1)S(1)}, u32[]{:S(2)}, u32[]{:S(2)}) collective-permute-start(bf16[24,6912]{1,0:T(8,128)(2,1)S(1)} %get-tuple-element.147), channel_id=1, source_target_pairs={{0,24},{8,0},{16,8},{24,16},{1,25},{9,1},{17,9},{25,17},{2,26},{10... | collective-permute-start | bytes 995336 | tf_op jit(solution)/shard_map/ppermute | solution.py:1067
  397.3 28.1 %collective-permute-start.19 = (bf16[24,6912]{1,0:T(8,128)(2,1)S(1)}, bf16[24,6912]{1,0:T(8,128)(2,1)S(1)}, u32[]{:S(2)}, u32[]{:S(2)}) collective-permute-start(bf16[24,6912]{1,0:T(8,128)(2,1)S(1)} %get-tuple-element.148), channel_id=1, source_target_pairs={{0,16},{8,24},{16,0},{24,8},{1,17},{9,25},{17,1},{25,9},{2,18},{10... | collective-permute-start | bytes 995336 | tf_op jit(solution)/shard_map/ppermute | solution.py:1067
  397.9 29.3 %all-to-all-start.7 = ((bf16[8,2,192,128]{3,2,1,0:T(8,128)(2,1)}), bf16[8,2,192,128]{3,2,1,0:T(8,128)(2,1)S(1)}, u32[]{:S(2)}, u32[]{:S(2)}) async-start(bf16[8,2,192,128]{3,2,1,0:T(8,128)(2,1)} %get-tuple-element.97), calls=%async_computation.7 | async-start | bytes 1572864 | tf_op jit(solution)/shard_map/all_to_all | solution.py:1311
  401.5 131.9 %all-gather.7.cloned.1.call-start = ((), (), s32[]{:S(2)}) async-start(), calls=%async_computation.14 | async-start | bytes 5419008 | tf_op jit(solution)/shard_map/all_gather | solution.py:1345
  452.0 15.2 %collective-permute-start.24 = (bf16[24,5632]{1,0:T(8,128)(2,1)S(1)}, bf16[24,5632]{1,0:T(8,128)(2,1)S(1)}, u32[]{:S(2)}, u32[]{:S(2)}) collective-permute-start(bf16[24,5632]{1,0:T(8,128)(2,1)S(1)} %get-tuple-element.150), channel_id=1, source_target_pairs={{0,24},{8,0},{16,8},{24,16},{1,25},{9,1},{17,9},{25,17},{2,26},{10... | collective-permute-start | bytes 811016 | tf_op jit(solution)/shard_map/ppermute | solution.py:1067
  455.9 22.1 %collective-permute-start.23 = (bf16[24,5632]{1,0:T(8,128)(2,1)S(1)}, bf16[24,5632]{1,0:T(8,128)(2,1)S(1)}, u32[]{:S(2)}, u32[]{:S(2)}) collective-permute-start(bf16[24,5632]{1,0:T(8,128)(2,1)S(1)} %get-tuple-element.151), channel_id=1, source_target_pairs={{0,16},{8,24},{16,0},{24,8},{1,17},{9,25},{17,1},{25,9},{2,18},{10... | collective-permute-start | bytes 811016 | tf_op jit(solution)/shard_map/ppermute | solution.py:1067
  479.0 41.2 %all-to-all-start.8 = ((bf16[8,2,576,128]{3,2,1,0:T(8,128)(2,1)}), bf16[8,2,576,128]{3,2,1,0:T(8,128)(2,1)S(1)}, u32[]{:S(2)}, u32[]{:S(2)}) async-start(bf16[8,2,576,128]{3,2,1,0:T(8,128)(2,1)} %get-tuple-element.103), calls=%async_computation.10 | async-start | bytes 4718592 | tf_op jit(solution)/shard_map/all_to_all | solution.py:1324
  (33 other events, 302.0 us)
Sparse Core Ops, SparseCore 0:
  10.2 44.4 all-gather.8
  58.1 137.2 all-gather.4
  248.6 92.4 reduce-scatter.2
  392.2 54.8 reduce-scatter.4
  479.1 54.2 all-gather.6
